TPU v7x, 32 devices: a whole 2x2x4 slice. The times are simulated.
32 devices in a mesh: ctx: 8 (over z, x), inner: 4 (over y, core).
Axes of the slice: x: 2, y: 2, z: 4, core: 2. Of those that a mesh axis runs over, the one named last changes fastest.
Arguments:
- lin_query: bfloat16 [4096, 4096], P(('ctx', 'inner')), may hold values from -6 to 6
- lin_key: bfloat16 [4096, 4096], P(('ctx', 'inner')), may hold values from -6 to 6
- lin_value: bfloat16 [4096, 4096], P(('ctx', 'inner')), may hold values from -6 to 6
- sparse_query: bfloat16 [4096, 4096], P(('ctx', 'inner')), may hold values from -48 to 48
- sparse_key: bfloat16 [4096, 4096], P(('ctx', 'inner')), may hold values from -48 to 48
- decay: float32 [32, 4096], P('inner', 'ctx'), may hold values from 0.5 to 1
- norm_gain: float32 [32, 128], P('inner'), may hold values from 0.1 to 1.9
- block_pattern: int32 [64, 8], P('ctx'), may hold values from -1 to 63, as said below
Outputs:
- layer_out: bfloat16 [4096, 4096], P(('ctx', 'inner'))
Inputs may be any that keep to these rules, and one draw needn't show every extreme that they name: `block_pattern`: row i lists distinct blocks: the first entry is i, the others lie in i - 16 to i - 1, and -1 stands where that range falls before block 0; in a row whose index is a multiple of 8 the last entry is i - 16.
All inputs are finite; a program needn't handle non-finite values.
Results may differ from a plain program's by a relative error of at most 0.0049.
Values may be sent and summed in bfloat16 or wider, within the bound.
No kernel may reach another device: no remote copies, remote signals or barrier semaphores. Data moves between devices by JAX's collectives and lax.ppermute only.
A program may use at most 128 MiB of HBM per device.

v0:
```python
import math

import jax
import jax.numpy as jnp
from jax import lax
from jax.sharding import PartitionSpec as P

LBLK = 128
BLK = 64
NSEL = 8


precise_mode = lax.Precision.HIGHEST


def carried_in(part, axis, combine, identity):
    place = lax.axis_index(axis)
    gathered = jax.tree.map(lambda a: lax.all_gather(a, axis), part)
    state = jax.tree.map(lambda a, e: jnp.zeros_like(a) + jnp.asarray(e, a.dtype), part, identity)

    def one(lap, state):
        return combine(
            state, jax.tree.map(lambda a: lax.dynamic_index_in_dim(a, lap, 0, False), gathered)
        )

    return lax.fori_loop(0, place, one, state)


def from_behind(value, axis, steps):
    count = lax.axis_size(axis)
    leading, last = (max(0, -steps), min(count, count - steps))
    return lax.ppermute(value, axis, [(source, source + steps) for source in range(leading, last)])


def block_math(queries_blk, keys_blk, values_blk, cumul, carried):
    query_f = queries_blk.astype(jnp.float32)
    key_f = keys_blk.astype(jnp.float32)
    value_f = values_blk.astype(jnp.float32)
    scores = jnp.einsum("ihd,jhd->hij", query_f, key_f, precision=precise_mode)
    length = cumul.shape[1]
    causal = (jnp.arange(length)[:, None] >= jnp.arange(length)[None, :])[None]
    log_gap = cumul[:, :, None] - cumul[:, None, :]
    weights = jnp.where(causal, jnp.exp(jnp.where(causal, log_gap, 0.0)), 0.0) * scores
    inside = jnp.einsum("hij,jhd->ihd", weights, value_f, precision=precise_mode)
    lifted = query_f * jnp.exp(cumul).T[:, :, None]
    outside = jnp.einsum("ihd,hde->ihe", lifted, carried, precision=precise_mode)
    final_log = cumul[:, -1]
    tail_scale = jnp.exp(final_log[:, None] - cumul).T[:, :, None]
    new_state = jnp.exp(final_log)[:, None, None] * carried + jnp.einsum(
        "jhd,jhe->hde", key_f * tail_scale, value_f, precision=precise_mode
    )
    return (inside + outside, new_state)


def normalize(raw_out, norm_gain):
    scale_rows = lax.rsqrt(jnp.mean(raw_out * raw_out, axis=-1, keepdims=True) + 1e-06)
    return (raw_out * scale_rows * norm_gain).astype(jnp.bfloat16)


def local(lin_query, lin_key, lin_value, sparse_query, sparse_key, decay, norm_gain, block_pattern):
    heads_here = norm_gain.shape[0]
    head_dim = norm_gain.shape[1]
    width_here = heads_here * head_dim
    query_heads, key_heads, value_heads, sparse_queries, sparse_keys = (
        lax.all_to_all(lin_query, "inner", split_axis=1, concat_axis=0, tiled=True),
        lax.all_to_all(lin_key, "inner", split_axis=1, concat_axis=0, tiled=True),
        lax.all_to_all(lin_value, "inner", split_axis=1, concat_axis=0, tiled=True),
        lax.all_to_all(sparse_query, "inner", split_axis=1, concat_axis=0, tiled=True),
        lax.all_to_all(sparse_key, "inner", split_axis=1, concat_axis=0, tiled=True),
    )
    shard_len = query_heads.shape[0]
    num_blocks = shard_len // LBLK
    log_decay = jnp.log(decay)
    block_logs = log_decay.reshape(heads_here, num_blocks, LBLK).transpose(1, 0, 2)

    def blocked(array):
        return array.reshape(num_blocks, LBLK, heads_here, head_dim)

    def advance(carried, inputs):
        queries_blk, keys_blk, values_blk, logs_blk = inputs
        produced, carried = block_math(
            queries_blk, keys_blk, values_blk, jnp.cumsum(logs_blk, axis=1), carried
        )
        return (carried, produced)

    shard_state, results = lax.scan(
        advance,
        jnp.zeros((heads_here, head_dim, head_dim), jnp.float32),
        (blocked(query_heads), blocked(key_heads), blocked(value_heads), block_logs),
    )
    shard_log = jnp.sum(log_decay, axis=1)

    def combine(earlier, later):
        return (earlier[0] + later[0], jnp.exp(later[0])[:, None, None] * earlier[1] + later[1])

    identity = (jnp.zeros_like(shard_log), jnp.zeros_like(shard_state))
    _, entering = carried_in((shard_log, shard_state), "ctx", combine, identity)
    cum_all = jnp.cumsum(log_decay, axis=1)
    lifted = (
        query_heads.reshape(shard_len, heads_here, head_dim).astype(jnp.float32)
        * jnp.exp(cum_all).T[:, :, None]
    )
    raw_out = results.reshape(shard_len, heads_here, head_dim) + jnp.einsum(
        "ihd,hde->ihe", lifted, entering, precision=precise_mode
    )
    first_out = normalize(raw_out, norm_gain)
    value_rows = first_out.reshape(shard_len, width_here)
    shifted = [from_behind((sparse_keys, value_rows), "ctx", distance) for distance in (2, 1)]
    key_window = jnp.concatenate([shifted[0][0], shifted[1][0], sparse_keys], axis=0)
    value_window = jnp.concatenate([shifted[0][1], shifted[1][1], value_rows], axis=0)
    shard_blocks = shard_len // BLK
    group_size = min(shard_blocks, max(1, 512 // BLK))
    num_groups = shard_blocks // group_size
    base_block = lax.axis_index("ctx") * shard_blocks
    window_start = base_block - 2 * shard_blocks
    key_blocks = key_window.reshape(3 * shard_blocks, BLK, width_here)
    value_blocks = value_window.reshape(3 * shard_blocks, BLK, width_here)
    offsets = jnp.arange(BLK, dtype=jnp.int32)
    scale = 1.0 / math.sqrt(head_dim)

    def attend(group_id):
        chosen = lax.dynamic_slice_in_dim(block_pattern, group_id * group_size, group_size, 0)
        in_window = jnp.clip(chosen - window_start, 0, 3 * shard_blocks - 1)
        keys_here = key_blocks[in_window].reshape(group_size, NSEL * BLK, heads_here, head_dim)
        values_here = value_blocks[in_window].reshape(group_size, NSEL * BLK, heads_here, head_dim)
        queries_here = lax.dynamic_slice_in_dim(
            sparse_queries, group_id * group_size * BLK, group_size * BLK, 0
        ).reshape(group_size, BLK, heads_here, head_dim)
        scores = (
            jnp.einsum(
                "gihd,gjhd->ghij", queries_here, keys_here, preferred_element_type=jnp.float32
            )
            * scale
        )
        key_pos = (chosen[:, :, None] * BLK + offsets[None, None, :]).reshape(
            group_size, NSEL * BLK
        )
        is_live = jnp.repeat(chosen >= 0, BLK, axis=1)
        query_pos = (base_block + group_id * group_size + jnp.arange(group_size, dtype=jnp.int32))[
            :, None
        ] * BLK + offsets[None, :]
        allowed = (is_live[:, None, :] & (key_pos[:, None, :] <= query_pos[:, :, None]))[:, None]
        scores = jnp.where(allowed, scores, -1e30)
        row_max = jnp.max(scores, axis=-1, keepdims=True)
        probs = jnp.where(allowed, jnp.exp(scores - row_max), 0.0)
        weights = (probs / jnp.sum(probs, axis=-1, keepdims=True)).astype(jnp.bfloat16)
        combined = jnp.einsum(
            "ghij,gjhd->gihd", weights, values_here, preferred_element_type=jnp.float32
        )
        return combined.reshape(group_size * BLK, width_here)

    second_out = lax.map(attend, jnp.arange(num_groups, dtype=jnp.int32)).reshape(
        shard_len, width_here
    )
    layer_rows = (value_rows.astype(jnp.float32) + second_out).astype(jnp.bfloat16)
    return lax.all_to_all(layer_rows, "inner", split_axis=0, concat_axis=1, tiled=True)


def solution(mesh):
    placed = (
        P(("ctx", "inner"), None),
        P(("ctx", "inner"), None),
        P(("ctx", "inner"), None),
        P(("ctx", "inner"), None),
        P(("ctx", "inner"), None),
        P("inner", "ctx"),
        P("inner", None),
        P("ctx", None),
    )
    return jax.shard_map(
        local, mesh=mesh, in_specs=placed, out_specs=P(("ctx", "inner"), None), check_vma=False
    )
```

profile of v0, /device:TPU:17, one launch (start us, length us, event | category | flops | bytes accessed | tf_op | source)
XLA Modules:
  0.0 392.4 jit_solution(5964652396613439505)
XLA Ops:
  6.5 2.4 copy.92
  8.9 4.9 %all-to-all-start.2 = ((bf16[128,4,1024]{0,2,1:T(8,128)(2,1)}), bf16[128,4,1024]{0,2,1:T(8,128)(2,1)}, u32[]{:S(2)}, u32[]{:S(2)}) async-start(bf16[128,4,1024]{0,2,1:T(8,128)(2,1)} %bitcast.10), calls=%async_computation.2 | async-start | bytes 2097152 | tf_op jit(solution)/shard_map/all_to_all | solution.py:65
  13.8 1.3 copy.90
  15.1 12.4 %all-to-all-done.2 = bf16[128,4,1024]{0,2,1:T(8,128)(2,1)} async-done(((bf16[128,4,1024]{0,2,1:T(8,128)(2,1)}), bf16[128,4,1024]{0,2,1:T(8,128)(2,1)}, u32[]{:S(2)}, u32[]{:S(2)}) %all-to-all-start.2) | async-done | bytes 1048608 | tf_op jit(solution)/shard_map/all_to_all | solution.py:65
  27.5 5.1 %all-to-all-start = ((bf16[128,4,1024]{0,2,1:T(8,128)(2,1)}), bf16[128,4,1024]{0,2,1:T(8,128)(2,1)}, u32[]{:S(2)}, u32[]{:S(2)}) async-start(bf16[128,4,1024]{0,2,1:T(8,128)(2,1)} %bitcast.4), calls=%async_computation | async-start | bytes 2097152 | tf_op jit(solution)/shard_map/all_to_all | solution.py:66
  32.6 1.3 copy.91
  33.9 12.4 %all-to-all-done = bf16[128,4,1024]{0,2,1:T(8,128)(2,1)} async-done(((bf16[128,4,1024]{0,2,1:T(8,128)(2,1)}), bf16[128,4,1024]{0,2,1:T(8,128)(2,1)}, u32[]{:S(2)}, u32[]{:S(2)}) %all-to-all-start) | async-done | bytes 1048608 | tf_op jit(solution)/shard_map/all_to_all | solution.py:66
  46.3 4.4 %all-to-all-start.1 = ((bf16[128,4,1024]{0,2,1:T(8,128)(2,1)}), bf16[128,4,1024]{0,2,1:T(8,128)(2,1)S(1)}, u32[]{:S(2)}, u32[]{:S(2)}) async-start(bf16[128,4,1024]{0,2,1:T(8,128)(2,1)} %bitcast.7), calls=%async_computation.1 | async-start | bytes 2097152 | tf_op jit(solution)/shard_map/all_to_all | solution.py:67
  50.8 13.5 %all-to-all-done.1 = bf16[128,4,1024]{0,2,1:T(8,128)(2,1)S(1)} async-done(((bf16[128,4,1024]{0,2,1:T(8,128)(2,1)}), bf16[128,4,1024]{0,2,1:T(8,128)(2,1)S(1)}, u32[]{:S(2)}, u32[]{:S(2)}) %all-to-all-start.1) | async-done | bytes 1048608 | tf_op jit(solution)/shard_map/all_to_all | solution.py:67
  64.2 79.4 %while.30 = (s32[]{:T(128)}, f32[8,128,128]{2,1,0:T(8,128)S(1)}, f32[4,128,8,128]{1,0,3,2:T(4,128)}, f32[4,8,128]{2,1,0:T(8,128)S(1)}, bf16[4,128,8,128]{1,3,2,0...) while((s32[]{:T(128)}, f32[8,128,128]{2,1,0:T(8,128)S(1)}, ...), condition=%wide.region_2.3_spmd.clone, body=%wide.region_0.2_spmd.clone.sunk | while | flops 639385600 | bytes 8987432 | solution.py:86
  67.1 1.2 fusion.61
  68.3 14.7 %dynamic_update_slice.9 = f32[4,128,8,128]{1,0,3,2:T(4,128)} dynamic-update-slice(f32[4,128,8,128]{1,0,3,2:T(4,128)} %get-tuple-element.301, f32[1,128,8,128]{1,0,3,2:T(1,128)S(1)} %bitcast.146, s32[]{:T(128)} %get-tuple-element.299, s32[]{:T(128)} %constant.84.clone.1..sunk.1, s32[]{:T(128)} %constant.84.clone.1..sunk.1, s32[]{:T(128)} %constant.84.clone.1..sunk.1) | dynamic-update-slice | bytes 1048580 | tf_op jit(solution)/shard_map/while/body/jit(dynamic_update_index_in_dim)/dynamic_update_slice | solution.py:86
  84.1 1.1 constant_dynamic-slice_fusion.3
  87.0 1.2 fusion.61
  88.2 14.7 %dynamic_update_slice.9 = f32[4,128,8,128]{1,0,3,2:T(4,128)} dynamic-update-slice(f32[4,128,8,128]{1,0,3,2:T(4,128)} %get-tuple-element.301, f32[1,128,8,128]{1,0,3,2:T(1,128)S(1)} %bitcast.146, s32[]{:T(128)} %get-tuple-element.299, s32[]{:T(128)} %constant.84.clone.1..sunk.1, s32[]{:T(128)} %constant.84.clone.1..sunk.1, s32[]{:T(128)} %constant.84.clone.1..sunk.1) | dynamic-update-slice | bytes 1048580 | tf_op jit(solution)/shard_map/while/body/jit(dynamic_update_index_in_dim)/dynamic_update_slice | solution.py:86
  104.0 1.1 constant_dynamic-slice_fusion.3
  106.8 1.2 fusion.61
  108.0 14.7 %dynamic_update_slice.9 = f32[4,128,8,128]{1,0,3,2:T(4,128)} dynamic-update-slice(f32[4,128,8,128]{1,0,3,2:T(4,128)} %get-tuple-element.301, f32[1,128,8,128]{1,0,3,2:T(1,128)S(1)} %bitcast.146, s32[]{:T(128)} %get-tuple-element.299, s32[]{:T(128)} %constant.84.clone.1..sunk.1, s32[]{:T(128)} %constant.84.clone.1..sunk.1, s32[]{:T(128)} %constant.84.clone.1..sunk.1) | dynamic-update-slice | bytes 1048580 | tf_op jit(solution)/shard_map/while/body/jit(dynamic_update_index_in_dim)/dynamic_update_slice | solution.py:86
  123.8 1.1 constant_dynamic-slice_fusion.3
  126.7 1.2 fusion.61
  127.9 14.7 %dynamic_update_slice.9 = f32[4,128,8,128]{1,0,3,2:T(4,128)} dynamic-update-slice(f32[4,128,8,128]{1,0,3,2:T(4,128)} %get-tuple-element.301, f32[1,128,8,128]{1,0,3,2:T(1,128)S(1)} %bitcast.146, s32[]{:T(128)} %get-tuple-element.299, s32[]{:T(128)} %constant.84.clone.1..sunk.1, s32[]{:T(128)} %constant.84.clone.1..sunk.1, s32[]{:T(128)} %constant.84.clone.1..sunk.1) | dynamic-update-slice | bytes 1048580 | tf_op jit(solution)/shard_map/while/body/jit(dynamic_update_index_in_dim)/dynamic_update_slice | solution.py:86
  144.5 2.3 copy.104
  146.8 4.4 %all-to-all-start.3 = ((bf16[128,4,1024]{0,2,1:T(8,128)(2,1)}), bf16[128,4,1024]{0,2,1:T(8,128)(2,1)S(1)}, u32[]{:S(2)}, u32[]{:S(2)}) async-start(bf16[128,4,1024]{0,2,1:T(8,128)(2,1)} %bitcast.20), calls=%async_computation.3 | async-start | bytes 2097152 | tf_op jit(solution)/shard_map/all_to_all | solution.py:69
  151.1 1.1 reduce-window.6
  152.5 1.1 copy.148
  154.0 10.9 %all-to-all-done.3 = bf16[128,4,1024]{0,2,1:T(8,128)(2,1)S(1)} async-done(((bf16[128,4,1024]{0,2,1:T(8,128)(2,1)}), bf16[128,4,1024]{0,2,1:T(8,128)(2,1)S(1)}, u32[]{:S(2)}, u32[]{:S(2)}) %all-to-all-start.3) | async-done | bytes 1048608 | tf_op jit(solution)/shard_map/all_to_all | solution.py:69
  164.8 4.3 %all-to-all-start.4 = ((bf16[128,4,1024]{2,0,1:T(8,128)(2,1)}), bf16[128,4,1024]{2,0,1:T(8,128)(2,1)S(1)}, u32[]{:S(2)}, u32[]{:S(2)}) async-start(bf16[128,4,1024]{2,0,1:T(8,128)(2,1)} %bitcast.117), calls=%async_computation.4 | async-start | bytes 2097152 | tf_op jit(solution)/shard_map/all_to_all | solution.py:68
  170.6 13.1 %all-reduce = f32[64]{0:T(128)S(1)} all-reduce(f32[64]{0:T(128)S(1)} %dynamic-update-slice), channel_id=2, replica_groups=mesh['ctx'=8,'inner'=4] {'ctx'}, use_global_device_ids=true, to_apply=%add | all-reduce | flops 64 | bytes 512
  184.0 1.3 copy.105
  185.4 4.0 %collective-permute-start.2 = (bf16[512,1024]{1,0:T(8,128)(2,1)}, bf16[512,1024]{1,0:T(8,128)(2,1)}, u32[]{:S(2)}, u32[]{:S(2)}) collective-permute-start(bf16[512,1024]{1,0:T(8,128)(2,1)} %bitcast.22), channel_id=1, source_target_pairs={{0,8},{4,12},{8,16},{12,20},{16,24},{20,28},{1,9},{5,13},{9,17},{1... | collective-permute-start | bytes 3145736 | tf_op jit(solution)/shard_map/ppermute | solution.py:32
  189.3 3.1 collective-permute-start.3
  193.5 1.4 bitcast_convert_fusion
  194.8 1.8 copy.97
  196.7 2.1 copy.129
  198.7 3.1 reshape.174
  201.8 1.3 copy.131
  203.2 2.0 bitcast_multiply_fusion
  205.1 30.6 %collective-permute-done.2 = bf16[512,1024]{1,0:T(8,128)(2,1)} collective-permute-done((bf16[512,1024]{1,0:T(8,128)(2,1)}, bf16[512,1024]{1,0:T(8,128)(2,1)}, u32[]{:S(2)}, u32[]{:S(2)}) %collective-permute-start.2) | collective-permute-done | bytes 1048608 | tf_op jit(solution)/shard_map/ppermute | solution.py:32
  235.7 23.4 %collective-permute-done.3 = bf16[512,1024]{1,0:T(8,128)(2,1)} collective-permute-done((bf16[512,1024]{1,0:T(8,128)(2,1)}, bf16[512,1024]{1,0:T(8,128)(2,1)}, u32[]{:S(2)}, u32[]{:S(2)}) %collective-permute-start.3) | collective-permute-done | bytes 1048608 | tf_op jit(solution)/shard_map/ppermute | solution.py:32
  259.1 2.1 pad_maximum_fusion
  261.2 5.5 %gather_fusion.1 = bf16[64,64,1024]{2,1,0:T(8,128)(2,1)} fusion(bf16[24,64,1024]{2,1,0:T(8,128)(2,1)S(1)} %bitcast.148, s32[1024]{0:T(1024)S(1)} %pad_clamp_fusion), kind=kCustom, calls=%fused_computation.1 | custom fusion | bytes 16777472 | tf_op jit(solution)/shard_map/while/body/eval_jaxpr/gather | solution.py:124
  266.7 8.8 %copy.130 = bf16[512,8,8,128]{3,2,1,0:T(8,128)(2,1)} copy(bf16[512,8,8,128]{3,1,2,0:T(8,128)(2,1)} %bitcast.150) | data formatting | bytes 16777216
  275.6 5.1 %while.29 = (s32[]{:T(128)}, f32[8,128,128]{2,1,0:T(8,128)S(1)}, s32[]{:T(128)}, f32[8,8]{1,0:T(8,128)S(1)}, f32[8,8,128,128]{3,2,1,0:T(8,128)}, /*index=5*/s32[]{:T(128)}, s32[]{:T(128)}, s32[]{:T(128)}) while((s32[]{:T(128)}, f32[8,128,128]{2,1,0:T(8,128)S(1)}, s32[]{:T(128)}, f32[8,8]{1,0:T(8,128)S(1)}, f32[8,8,128,128]{3,2,1,0:T(8,128)}, ...), condition=%wide.region_5.6_spmd, body=%wide.region_4.5_spmd.sunk | while | flops 262149 | bytes 1573087 | solution.py:26
  275.6 1.3 bitcast_add_fusion.3
  277.0 1.2 bitcast_add_fusion.3
  278.2 1.2 bitcast_add_fusion.3
  279.4 1.2 bitcast_add_fusion.3
  280.7 3.9 multiply_reduce_fusion
  284.9 1.3 copy.101
  286.2 5.6 %collective-permute-start = (bf16[512,1024]{1,0:T(8,128)(2,1)}, bf16[512,1024]{1,0:T(8,128)(2,1)}, u32[]{:S(2)}, u32[]{:S(2)}) collective-permute-start(bf16[512,1024]{1,0:T(8,128)(2,1)} %copy.101), channel_id=1, source_target_pairs={{0,8},{4,12},{8,16},{12,20},{16,24},{20,28},{1,9},{5,13},{9,17},{1... | collective-permute-start | bytes 3145736 | tf_op jit(solution)/shard_map/ppermute | solution.py:32
  291.8 2.1 collective-permute-start.1
  294.0 9.7 %fusion.24 = f32[8,8,512,64]{2,3,1,0:T(8,128)} fusion(bf16[8,512,8,128]{3,2,1,0:T(8,128)(2,1)} %bitcast.151, bf16[8,64,8,128]{3,2,1,0:T(8,128)(2,1)S(1)} %bitcast.156), kind=kOutput, calls=%fused_computation.40 | convolution fusion | flops 536870912 | bytes 17825792 | tf_op jit(solution)/shard_map/while/body/eval_jaxpr/gihd,gjhd->ghij/dot_general | solution.py:130
  303.6 12.8 %fusion.41 = (f32[8,8,64]{2,1,0:T(8,128)S(1)}, f32[8,8,64,512]{3,2,1,0:T(8,128)}) fusion(f32[8,8,512,64]{2,3,1,0:T(8,128)} %fusion.24, pred[8,64,512]{2,1,0:T(8,128)(4,1)S(1)} %copy-done.7), kind=kOutput, calls=%fused_computation.78 | output fusion | flops 14680575 | bytes 17055744 | tf_op jit(solution)/shard_map/while/body/eval_jaxpr/sub | solution.py:145
  317.2 1.9 copy.111
  319.1 15.5 %collective-permute-done.1 = bf16[512,1024]{1,0:T(8,128)(2,1)} collective-permute-done((bf16[512,1024]{1,0:T(8,128)(2,1)}, bf16[512,1024]{1,0:T(8,128)(2,1)}, u32[]{:S(2)}, u32[]{:S(2)}) %collective-permute-start.1) | collective-permute-done | bytes 1048608 | tf_op jit(solution)/shard_map/ppermute | solution.py:32
  334.6 2.1 pad_maximum_fusion.1
  336.7 5.5 %gather_fusion = bf16[64,64,1024]{2,1,0:T(8,128)(2,1)} fusion(bf16[24,64,1024]{2,1,0:T(8,128)(2,1)S(1)} %bitcast.147, s32[1024]{0:T(1024)S(1)} %pad_clamp_fusion), kind=kCustom, calls=%fused_computation | custom fusion | bytes 16777472 | tf_op jit(solution)/shard_map/while/body/eval_jaxpr/gather | solution.py:125
  342.2 8.8 %copy.132 = bf16[512,8,8,128]{3,2,1,0:T(8,128)(2,1)} copy(bf16[512,8,8,128]{3,1,2,0:T(8,128)(2,1)} %bitcast.149) | data formatting | bytes 16777216
  351.0 7.5 %fusion.33 = f32[8,64,8,128]{3,1,2,0:T(8,128)S(1)} fusion(bf16[8,512,8,128]{3,2,1,0:T(8,128)(2,1)} %bitcast.154, f32[8,8,64,512]{3,2,1,0:T(8,128)} %get-tuple-element.205, f32[8,8,64]{2,1,0:T(8,128)S(1)} %get-tuple-element.204), kind=kOutput, calls=%fused_computation.58 | convolution fusion | flops 541065216 | bytes 18890752 | tf_op jit(solution)/shard_map/while/body/eval_jaxpr/ghij,gjhd->gihd/dot_general | solution.py:147
  358.5 2.5 copy.110
  361.0 2.7 reshape.182
  363.7 1.9 add_convert_fusion
  365.6 18.0 %all_to_all.99 = bf16[4,128,1024]{2,1,0:T(8,128)(2,1)S(1)} all-to-all(bf16[4,128,1024]{2,1,0:T(8,128)(2,1)S(1)} %add_convert_fusion), channel_id=1, replica_groups=mesh['ctx'=8,'inner'=4] {'inner'}, dimensions={0} | all-to-all | bytes 2097152 | tf_op jit(solution)/shard_map/all_to_all | solution.py:156
  384.3 1.3 copy.113
  (109 shorter events, 17.6 us)
Async XLA Ops:
  6.5 7.3 %copy-start.4 = (bf16[128,4096]{1,0:T(8,128)(2,1)S(1)}, bf16[128,4096]{1,0:T(8,128)(2,1)}, u32[]{:S(2)}) copy-start(bf16[128,4096]{1,0:T(8,128)(2,1)} %param.13) | copy-start | bytes 3145732
  6.5 26.1 %copy-start.5 = (bf16[128,4096]{1,0:T(8,128)(2,1)S(1)}, bf16[128,4096]{1,0:T(8,128)(2,1)}, u32[]{:S(2)}) copy-start(bf16[128,4096]{1,0:T(8,128)(2,1)} %param.14) | copy-start | bytes 3145732
  8.9 18.6 %all-to-all-start.2 = ((bf16[128,4,1024]{0,2,1:T(8,128)(2,1)}), bf16[128,4,1024]{0,2,1:T(8,128)(2,1)}, u32[]{:S(2)}, u32[]{:S(2)}) async-start(bf16[128,4,1024]{0,2,1:T(8,128)(2,1)} %bitcast.10), calls=%async_computation.2 | async-start | bytes 2097152 | tf_op jit(solution)/shard_map/all_to_all | solution.py:65
  13.8 36.8 %copy-start.8 = (f32[8,512]{1,0:T(8,128)S(1)}, f32[8,512]{1,0:T(8,128)}, u32[]{:S(2)}) copy-start(f32[8,512]{1,0:T(8,128)} %param.17) | copy-start | bytes 49156
  27.5 18.8 %all-to-all-start = ((bf16[128,4,1024]{0,2,1:T(8,128)(2,1)}), bf16[128,4,1024]{0,2,1:T(8,128)(2,1)}, u32[]{:S(2)}, u32[]{:S(2)}) async-start(bf16[128,4,1024]{0,2,1:T(8,128)(2,1)} %bitcast.4), calls=%async_computation | async-start | bytes 2097152 | tf_op jit(solution)/shard_map/all_to_all | solution.py:66
  46.3 18.0 %all-to-all-start.1 = ((bf16[128,4,1024]{0,2,1:T(8,128)(2,1)}), bf16[128,4,1024]{0,2,1:T(8,128)(2,1)S(1)}, u32[]{:S(2)}, u32[]{:S(2)}) async-start(bf16[128,4,1024]{0,2,1:T(8,128)(2,1)} %bitcast.7), calls=%async_computation.1 | async-start | bytes 2097152 | tf_op jit(solution)/shard_map/all_to_all | solution.py:67
  50.6 224.9 %all-gather.4.cloned.1.call-start = ((), (), s32[]{:S(2)}) async-start(), calls=%async_computation.6 | async-start | bytes 4718592 | tf_op jit(solution)/shard_map/all_gather | solution.py:18
  143.7 0.8 copy-start
  143.7 8.8 %copy-start.9 = (s32[8,8]{1,0:T(8,128)S(1)}, s32[8,8]{1,0:T(8,128)}, u32[]{:S(2)}) copy-start(s32[8,8]{1,0:T(8,128)} %param.19) | copy-start | bytes 772
  143.7 8.8 %copy-start.6 = (bf16[128,4096]{1,0:T(8,128)(2,1)S(1)}, bf16[128,4096]{1,0:T(8,128)(2,1)}, u32[]{:S(2)}) copy-start(bf16[128,4096]{1,0:T(8,128)(2,1)} %param.15) | copy-start | bytes 3145732
  144.5 24.6 %copy-start.11 = (u32[32]{0:T(128)S(1)}, u32[32]{0:T(128)}, u32[]{:S(2)}) copy-start(u32[32]{0:T(128)} %constant.100) | copy-start | bytes 388
  146.8 18.1 %all-to-all-start.3 = ((bf16[128,4,1024]{0,2,1:T(8,128)(2,1)}), bf16[128,4,1024]{0,2,1:T(8,128)(2,1)S(1)}, u32[]{:S(2)}, u32[]{:S(2)}) async-start(bf16[128,4,1024]{0,2,1:T(8,128)(2,1)} %bitcast.20), calls=%async_computation.3 | async-start | bytes 2097152 | tf_op jit(solution)/shard_map/all_to_all | solution.py:69
  164.8 37.0 %all-to-all-start.4 = ((bf16[128,4,1024]{2,0,1:T(8,128)(2,1)}), bf16[128,4,1024]{2,0,1:T(8,128)(2,1)S(1)}, u32[]{:S(2)}, u32[]{:S(2)}) async-start(bf16[128,4,1024]{2,0,1:T(8,128)(2,1)} %bitcast.117), calls=%async_computation.4 | async-start | bytes 2097152 | tf_op jit(solution)/shard_map/all_to_all | solution.py:68
  185.4 50.4 %collective-permute-start.2 = (bf16[512,1024]{1,0:T(8,128)(2,1)}, bf16[512,1024]{1,0:T(8,128)(2,1)}, u32[]{:S(2)}, u32[]{:S(2)}) collective-permute-start(bf16[512,1024]{1,0:T(8,128)(2,1)} %bitcast.22), channel_id=1, source_target_pairs={{0,8},{4,12},{8,16},{12,20},{16,24},{20,28},{1,9},{5,13},{9,17},{1... | collective-permute-start | bytes 3145736 | tf_op jit(solution)/shard_map/ppermute | solution.py:32
  189.3 69.8 %collective-permute-start.3 = (bf16[512,1024]{1,0:T(8,128)(2,1)}, bf16[512,1024]{1,0:T(8,128)(2,1)}, u32[]{:S(2)}, u32[]{:S(2)}) collective-permute-start(bf16[512,1024]{1,0:T(8,128)(2,1)} %bitcast.22), channel_id=1, source_target_pairs={{0,4},{4,8},{8,12},{12,16},{16,20},{20,24},{24,28},{1,5},{5,9},{9,... | collective-permute-start | bytes 3145736 | tf_op jit(solution)/shard_map/ppermute | solution.py:32
  275.5 5.1 %copy-start.1 = (f32[512,8,128]{0,2,1:T(8,128)S(1)}, f32[512,8,128]{0,2,1:T(8,128)}, u32[]{:S(2)}) copy-start(f32[512,8,128]{0,2,1:T(8,128)} %reshape.174) | copy-start | bytes 6291460
  280.6 4.0 %copy-start.10 = (f32[8,128]{1,0:T(8,128)S(1)}, f32[8,128]{1,0:T(8,128)}, u32[]{:S(2)}) copy-start(f32[8,128]{1,0:T(8,128)} %param.18) | copy-start | bytes 12292
  284.6 9.4 %copy-start.3 = (bf16[64,8,8,128]{3,2,1,0:T(8,128)(2,1)S(1)}, bf16[64,8,8,128]{3,2,1,0:T(8,128)(2,1)}, u32[]{:S(2)}) copy-start(bf16[64,8,8,128]{3,2,1,0:T(8,128)(2,1)} %copy.131) | copy-start | bytes 3145732
  286.2 32.8 %collective-permute-start = (bf16[512,1024]{1,0:T(8,128)(2,1)}, bf16[512,1024]{1,0:T(8,128)(2,1)}, u32[]{:S(2)}, u32[]{:S(2)}) collective-permute-start(bf16[512,1024]{1,0:T(8,128)(2,1)} %copy.101), channel_id=1, source_target_pairs={{0,8},{4,12},{8,16},{12,20},{16,24},{20,28},{1,9},{5,13},{9,17},{1... | collective-permute-start | bytes 3145736 | tf_op jit(solution)/shard_map/ppermute | solution.py:32
  291.8 42.8 %collective-permute-start.1 = (bf16[512,1024]{1,0:T(8,128)(2,1)}, bf16[512,1024]{1,0:T(8,128)(2,1)}, u32[]{:S(2)}, u32[]{:S(2)}) collective-permute-start(bf16[512,1024]{1,0:T(8,128)(2,1)} %copy.101), channel_id=1, source_target_pairs={{0,4},{4,8},{8,12},{12,16},{16,20},{20,24},{24,28},{1,5},{5,9},{9,... | collective-permute-start | bytes 3145736 | tf_op jit(solution)/shard_map/ppermute | solution.py:32
  294.0 9.7 %copy-start.7 = (pred[8,64,512]{2,1,0:T(8,128)(4,1)S(1)}, pred[8,64,512]{2,1,0:T(8,128)(4,1)}, u32[]{:S(2)}) copy-start(pred[8,64,512]{2,1,0:T(8,128)(4,1)} %compare_and_fusion) | copy-start | bytes 786436
  358.5 5.3 %copy-start.2 = (f32[4,128,1024]{2,1,0:T(8,128)S(1)}, f32[4,128,1024]{2,1,0:T(8,128)}, u32[]{:S(2)}) copy-start(f32[4,128,1024]{2,1,0:T(8,128)} %copy.111) | copy-start | bytes 6291460
Sparse Core Ops, SparseCore 0:
  144.6 85.9 all-gather.3
where the time goes:
time: 395 us; the launch traced here: 392 us
  local copies, waits for them, and re-layouts  126 us (32%)
  waiting for transfers between devices  119 us (30%)
  starting transfers between devices  37.7 us (10%)
  matrix products  33.2 us (8%)
  other arithmetic  31.3 us (8%)
  blocking collectives  31.1 us (8%)
  between operations  14.3 us (4%)
    ppermute x4, waiting for transfers between devices, from_behind(): lax.ppermute(value, axis, [(source, source + steps) for source in range(l...  69.5 us
    dynamic_update_slice x4, local copies, waits for them, and re-layouts, local(): lax.scan(advance, jnp.zeros((heads_here, head_dim, head_dim), jnp.float32...  58.9 us
    unnamed x35, local copies, waits for them, and re-layouts  29.8 us
    all_to_all x1, blocking collectives, local(): lax.all_to_all(layer_rows, 'inner', split_axis=0, concat_axis=1, tiled=True)  18 us
    ppermute x4, starting transfers between devices, from_behind(): lax.ppermute(value, axis, [(source, source + steps) for source in range(l...  14.8 us
    all_to_all x1, waiting for transfers between devices, local(): lax.all_to_all(lin_value, 'inner', split_axis=1, concat_axis=0, tiled=True)  13.5 us
    unnamed x1, blocking collectives  13.1 us
    sub x1, other arithmetic, attend(): probs = jnp.where(allowed, jnp.exp(scores - row_max), 0.0)  12.8 us
  transfers between devices with their start and end apart: 10, of which 7 were waited for; matrix products, arithmetic and copies ran while one was open for 16% of the time, Pallas kernels for 0%

commit v1 on v0

v1 whole, which is shorter than its diff:
```python
import functools
import math

import jax
import jax.numpy as jnp
from jax import lax
from jax.experimental import pallas as pl
from jax.experimental.pallas import tpu as pltpu
from jax.sharding import Mesh
from jax.sharding import PartitionSpec as P

BLK = 64
F32 = jnp.float32
BF16 = jnp.bfloat16
HIGHEST = lax.Precision.HIGHEST
VMEM = pl.BlockSpec(memory_space=pltpu.VMEM)
SMEM = pl.BlockSpec(memory_space=pltpu.SMEM)


def halves(x):
    high = x.astype(BF16)
    return high, (x - high.astype(F32)).astype(BF16)


def dot(a, b, dims):
    return lax.dot_general(a, b, (dims, ((), ())), preferred_element_type=F32)


def summed_logs(decay_ref):
    logs = jnp.log(decay_ref[...])
    length = logs.shape[1]
    row = lax.broadcasted_iota(jnp.int32, (length, length), 0)
    col = lax.broadcasted_iota(jnp.int32, (length, length), 1)
    upper = (row <= col).astype(F32)
    lower = (row >= col).astype(F32)
    along = lax.dot_general(logs, upper, (((1,), (0,)), ((), ())), precision=HIGHEST, preferred_element_type=F32)
    down = lax.dot_general(lower, logs, (((1,), (1,)), ((), ())), precision=HIGHEST, preferred_element_type=F32)
    return along, down, row >= col


def state_kernel(kv_ref, decay_ref, sent_ref, entering_ref):
    heads, chunks, width, _ = entering_ref.shape
    length = kv_ref.shape[1] // 2
    along, down, _ = summed_logs(decay_ref)
    for h in range(heads):
        columns = slice(h * width, (h + 1) * width)
        state = jnp.zeros((width, width), F32)
        whole = jnp.zeros((1, 1), F32)
        for c in range(chunks):
            at = h * chunks + c
            entering_ref[h, c] = state
            total = along[at : at + 1, length - 1 : length]
            keys = kv_ref[c, :length, columns].astype(F32)
            values = kv_ref[c, length:, columns]
            high, low = halves(keys * jnp.exp(total - down[:, at : at + 1]))
            state = jnp.exp(total) * state + dot(
                jnp.concatenate([high, low], 0), jnp.concatenate([values, values], 0), ((0,), (0,))
            )
            whole = whole + total
        sent_ref[h, :width, :] = state.astype(BF16)
        factor = jnp.exp(whole)
        first = factor.astype(BF16).astype(F32)
        second = (factor - first).astype(BF16).astype(F32)
        third = factor - first - second
        place = lax.broadcasted_iota(jnp.int32, (16, width), 0)
        sent_ref[h, width:, :] = jnp.where(
            place == 0, first, jnp.where(place == 1, second, jnp.where(place == 2, third, 0.0))
        ).astype(BF16)


def first_kernel(q_ref, kv_ref, decay_ref, entering_ref, gain_ref, *refs):
    earlier, out_ref = refs[:-1], refs[-1]
    heads, chunks, width, _ = entering_ref.shape
    length = q_ref.shape[1]
    along, down, causal = summed_logs(decay_ref)
    for h in range(heads):
        columns = slice(h * width, (h + 1) * width)
        carried = jnp.zeros((width, width), F32)
        factor = jnp.ones((1, 1), F32)
        for ref in earlier:
            carried = carried + factor * ref[h, :width, :].astype(F32)
            parts = ref[h, width:, :].astype(F32)
            factor = factor * (parts[0:1, 0:1] + parts[1:2, 0:1] + parts[2:3, 0:1])
        gain = gain_ref[h : h + 1, :]
        before = jnp.zeros((1, 1), F32)
        for c in range(chunks):
            at = h * chunks + c
            queries = q_ref[c, :, columns]
            keys = kv_ref[c, :length, columns]
            values = kv_ref[c, length:, columns]
            high, low = halves(entering_ref[h, c] + jnp.exp(before) * carried)
            outside = dot(
                jnp.concatenate([queries, queries], 1), jnp.concatenate([high, low], 0), ((1,), (0,))
            )
            down_here = down[:, at : at + 1]
            gap = jnp.where(causal, down_here - along[at : at + 1, :], 0.0)
            weights = jnp.where(causal, jnp.exp(gap), 0.0) * dot(queries, keys, ((1,), (1,)))
            inside = dot(
                jnp.concatenate(halves(weights), 1), jnp.concatenate([values, values], 0), ((1,), (0,))
            )
            raw = inside + jnp.exp(down_here) * outside
            scale = lax.rsqrt(jnp.mean(raw * raw, axis=-1, keepdims=True) + 1e-06)
            out_ref[c, :, columns] = (raw * scale * gain).astype(BF16)
            before = before + along[at : at + 1, length - 1 : length]


def weights_kernel(window_ref, q_ref, own_ref, earlier_ref, bias_ref, out_ref, keys_ref, picked_ref):
    tokens, width = q_ref.shape
    blocks = tokens // BLK
    picks = picked_ref.shape[0] // BLK
    keys_ref[:tokens, :] = earlier_ref[...]
    keys_ref[tokens:, :] = own_ref[...]
    row = lax.broadcasted_iota(jnp.int32, (BLK, picks * BLK), 0)
    col = lax.broadcasted_iota(jnp.int32, (BLK, picks * BLK), 1)
    causal = jnp.where((col >= BLK) | (col <= row), 0.0, -1e30)
    scale = 1.0 / math.sqrt(width)

    def one(b, _):
        for j in range(picks):
            start = pl.multiple_of(window_ref[b, j] * BLK, BLK)
            picked_ref[j * BLK : (j + 1) * BLK, :] = keys_ref[pl.ds(start, BLK), :]
        rows = pl.ds(pl.multiple_of(b * BLK, BLK), BLK)
        scores = dot(q_ref[rows, :], picked_ref[...], ((1,), (1,))) * scale
        scores = scores + (causal + bias_ref[pl.ds(b, 1), :])
        probs = jnp.exp(scores - jnp.max(scores, axis=-1, keepdims=True))
        out_ref[0, rows, :] = (probs / jnp.sum(probs, axis=-1, keepdims=True)).astype(BF16)
        return 0

    lax.fori_loop(0, blocks, one, 0)


def sum_kernel(window_ref, weights_ref, own_ref, earlier_ref, out_ref, values_ref, picked_ref):
    tokens, width = own_ref.shape
    blocks = tokens // BLK
    picks = picked_ref.shape[0] // BLK
    values_ref[:tokens, :] = earlier_ref[...]
    values_ref[tokens:, :] = own_ref[...]

    def one(b, _):
        for j in range(picks):
            start = pl.multiple_of(window_ref[b, j] * BLK, BLK)
            picked_ref[j * BLK : (j + 1) * BLK, :] = values_ref[pl.ds(start, BLK), :]
        rows = pl.ds(pl.multiple_of(b * BLK, BLK), BLK)
        second = dot(weights_ref[0, rows, :], picked_ref[...], ((1,), (0,)))
        out_ref[rows, :] = (own_ref[rows, :].astype(F32) + second).astype(BF16)
        return 0

    lax.fori_loop(0, blocks, one, 0)


PARAMS = pltpu.CompilerParams(vmem_limit_bytes=48 * 2**20)


def local(lin_query, lin_key, lin_value, sparse_query, sparse_key, decay, norm_gain, block_pattern):
    groups, inner = lax.axis_size("group"), lax.axis_size("inner")
    place, side = lax.axis_index("group"), lax.axis_index("side")
    ways = 2 * inner
    length, model = lin_query.shape
    width = norm_gain.shape[1]
    heads = norm_gain.shape[0] // 2
    here = heads * width
    tokens = ways * length
    blocks = tokens // BLK
    picks = block_pattern.shape[1]

    def pieces(x):
        return x.reshape(length, inner, 2, here).transpose(2, 1, 0, 3).reshape(ways, length, here)

    def exchange(x):
        return lax.all_to_all(x, ("side", "inner"), split_axis=0, concat_axis=0, tiled=True)

    def onward(x, steps=1):
        return lax.ppermute(x, "group", [(i, i + steps) for i in range(groups - steps)])

    span = decay.shape[1]
    flat = block_pattern.reshape(1, -1).astype(F32)
    flat = jnp.pad(flat, ((0, 0), (0, span - flat.shape[1])))
    mine = lax.dynamic_slice_in_dim(decay, side * heads, heads, 0)
    theirs = lax.dynamic_slice_in_dim(decay, (1 - side) * heads, heads, 0)
    other = lax.ppermute(jnp.concatenate([theirs, flat], 0), "side", [(0, 1), (1, 0)])
    own = jnp.concatenate([mine, flat], 0)
    both = jnp.where(side == 0, jnp.stack([own, other], 1), jnp.stack([other, own], 1))
    decays = both[:heads].reshape(heads * ways, length)
    pattern = both[heads, :, : block_pattern.size].reshape(blocks, picks).astype(jnp.int32)
    window = jnp.maximum(pattern - (place - 1) * blocks, 0)
    window = jnp.where(pattern >= 0, window, 0)
    bias = jnp.repeat(jnp.where(pattern >= 0, 0.0, -1e30).astype(F32), BLK, axis=1)
    gain = lax.dynamic_slice_in_dim(norm_gain, side * heads, heads, 0)

    sparse_keys = exchange(pieces(sparse_key))
    earlier_keys = onward(sparse_keys)
    keys_values = exchange(jnp.concatenate([pieces(lin_key), pieces(lin_value)], 1))
    queries = exchange(pieces(lin_query))
    sparse_queries = exchange(pieces(sparse_query))

    sent, entering = pl.pallas_call(
        state_kernel,
        out_shape=(
            jax.ShapeDtypeStruct((heads, width + 16, width), BF16),
            jax.ShapeDtypeStruct((heads, ways, width, width), F32),
        ),
        in_specs=[VMEM] * 2,
        out_specs=(VMEM, VMEM),
        compiler_params=PARAMS,
        name="state",
    )(keys_values, decays)
    states = [onward(sent, steps) for steps in range(1, groups)]
    first = pl.pallas_call(
        first_kernel,
        out_shape=jax.ShapeDtypeStruct((ways, length, here), BF16),
        in_specs=[VMEM] * (5 + len(states)),
        out_specs=VMEM,
        compiler_params=PARAMS,
        name="first",
    )(queries, keys_values, decays, entering, gain, *states)
    earlier_first = onward(first)

    column = pl.BlockSpec((tokens, width), lambda h: (0, h))
    table = pl.BlockSpec((1, tokens, picks * BLK), lambda h: (h, 0, 0))
    weights = pl.pallas_call(
        weights_kernel,
        out_shape=jax.ShapeDtypeStruct((heads, tokens, picks * BLK), BF16),
        grid=(heads,),
        in_specs=[SMEM, column, column, column, pl.BlockSpec((blocks, picks * BLK), lambda h: (0, 0))],
        out_specs=table,
        scratch_shapes=[pltpu.VMEM((2 * tokens, width), BF16), pltpu.VMEM((picks * BLK, width), BF16)],
        compiler_params=PARAMS,
        name="weights",
    )(
        window,
        sparse_queries.reshape(tokens, here),
        sparse_keys.reshape(tokens, here),
        earlier_keys.reshape(tokens, here),
        bias,
    )
    layer = pl.pallas_call(
        sum_kernel,
        out_shape=jax.ShapeDtypeStruct((tokens, here), BF16),
        grid=(heads,),
        in_specs=[SMEM, table, column, column],
        out_specs=column,
        scratch_shapes=[pltpu.VMEM((2 * tokens, width), BF16), pltpu.VMEM((picks * BLK, width), BF16)],
        compiler_params=PARAMS,
        name="sum",
    )(window, weights, first.reshape(tokens, here), earlier_first.reshape(tokens, here))
    back = exchange(layer.reshape(ways, length, here))
    return back.reshape(2, inner, length, here).transpose(2, 1, 0, 3).reshape(length, model)


def solution(mesh):
    spans, inner = mesh.devices.shape
    finer = Mesh(mesh.devices.reshape(spans // 2, 2, inner), ("group", "side", "inner"))
    rows = P(("group", "side", "inner"), None)
    placed = (rows,) * 5 + (P("inner", ("group", "side")), P("inner", None), P(("group", "side"), None))
    return jax.shard_map(local, mesh=finer, in_specs=placed, out_specs=rows, check_vma=False)
```

time: 395 us -> 187 us (0.47)
  local copies, waits for them, and re-layouts: 126 us -> 16.2 us
  waiting for transfers between devices: 119 us -> 59.7 us
  Pallas kernels: 0 us -> 52.8 us
  matrix products: 33.2 us -> 0 us
  other arithmetic: 31.3 us -> 1.55 us
  between operations: 14.3 us -> 0.19 us
  blocking collectives: 31.1 us -> 17.3 us
    dynamic_update_slice x4 -> x0, local copies, waits for them, and re-layouts: 58.9 us -> none  [local(): lax.scan(advance, jnp.zeros((heads_here, head_dim, head_dim), jnp.float32...]
    ppermute x4 -> x6, waiting for transfers between devices: 69.5 us -> 14.9 us  [the longest x1 12.4 us: local(): lax.ppermute(jnp.concatenate([theirs, flat], 0), 'side', [(0, 1), (1, 0)])]
    pallas_call x0 -> x4, Pallas kernels: none -> 52.8 us  [the longest x1 25.7 us: local(): pl.pallas_call(weights_kernel, out_shape=jax.ShapeDtypeStruct((heads, tok...]
    dot_general x19 -> x0, matrix products: 33.2 us -> none  [the longest x1 9.68 us: attend(): jnp.einsum('gihd,gjhd->ghij', queries_here, keys_here, preferred_element_...]
    unnamed x35 -> x12, local copies, waits for them, and re-layouts: 29.8 us -> 1.47 us
    unnamed x1 -> x0, blocking collectives: 13.1 us -> none
    sub x1 -> x0, other arithmetic: 12.8 us -> none  [attend(): probs = jnp.where(allowed, jnp.exp(scores - row_max), 0.0)]
    gather x2 -> x0, local copies, waits for them, and re-layouts: 11.1 us -> none  [the longest x1 5.54 us: attend(): value_blocks[in_window]]
  transfers between devices with their start and end apart: 10 -> 10, of which waited for: 7 -> 5; matrix products, arithmetic and copies ran while one was open for 16% -> 6% of each run, Pallas kernels for 0% -> 21%
where the time goes in v1:
time: 187 us; the launch traced here: 186 us
  waiting for transfers between devices  59.7 us (32%)
  Pallas kernels  52.8 us (28%)
  starting transfers between devices  38.1 us (20%)
  blocking collectives  17.3 us (9%)
  local copies, waits for them, and re-layouts  16.2 us (9%)
    all_to_all x4, waiting for transfers between devices, exchange(): lax.all_to_all(x, ('side', 'inner'), split_axis=0, concat_axis=0, tiled=T...  44.8 us
    pallas_call x1, Pallas kernels, local(): pl.pallas_call(weights_kernel, out_shape=jax.ShapeDtypeStruct((heads, tok...  25.7 us
    all_to_all x4, starting transfers between devices, exchange(): lax.all_to_all(x, ('side', 'inner'), split_axis=0, concat_axis=0, tiled=T...  19.6 us
    all_to_all x1, blocking collectives, exchange(): lax.all_to_all(x, ('side', 'inner'), split_axis=0, concat_axis=0, tiled=T...  17.3 us
    ppermute x5, starting transfers between devices, onward(): lax.ppermute(x, 'group', [(i, i + steps) for i in range(groups - steps)])  17 us
    pallas_call x1, Pallas kernels, local(): pl.pallas_call(sum_kernel, out_shape=jax.ShapeDtypeStruct((tokens, here),...  13 us
    ppermute x1, waiting for transfers between devices, local(): lax.ppermute(jnp.concatenate([theirs, flat], 0), 'side', [(0, 1), (1, 0)])  12.4 us
    reshape x8, local copies, waits for them, and re-layouts, pieces(): x.reshape(length, inner, 2, here).transpose(2, 1, 0, 3)  9.01 us
  transfers between devices with their start and end apart: 10, of which 5 were waited for; matrix products, arithmetic and copies ran while one was open for 6% of the time, Pallas kernels for 21%

profile of v1, /device:TPU:17, one launch (start us, length us, event | category | flops | bytes accessed | tf_op | source)
XLA Modules:
  0.0 185.8 jit_solution(15112838555910996963)
XLA Ops:
  0.0 0.0 copy-start
  0.0 1.8 reshape.89
  1.9 0.0 copy-start.2
  1.9 1.3 copy.17
  3.2 4.8 %all-to-all-start.1 = ((bf16[8,128,512]{2,1,0:T(8,128)(2,1)}), bf16[8,128,512]{2,1,0:T(8,128)(2,1)}, u32[]{:S(2)}, u32[]{:S(2)}) async-start(bf16[8,128,512]{2,1,0:T(8,128)(2,1)} %bitcast.6), calls=%async_computation.1 | async-start | bytes 2097152 | tf_op jit(solution)/shard_map/all_to_all | solution.py:170
  7.9 0.0 copy-done.2
  7.9 0.0 copy-start.3
  8.0 0.8 reshape.96
  8.8 0.3 copy.19
  9.1 0.1 copy-done.3
  9.2 0.8 reshape.98
  10.0 0.3 copy.20
  10.3 1.5 pad_maximum_fusion
  11.8 9.9 %all-to-all-done.1 = bf16[8,128,512]{2,1,0:T(8,128)(2,1)} async-done(((bf16[8,128,512]{2,1,0:T(8,128)(2,1)}), bf16[8,128,512]{2,1,0:T(8,128)(2,1)}, u32[]{:S(2)}, u32[]{:S(2)}) %all-to-all-start.1) | async-done | bytes 1048608 | tf_op jit(solution)/shard_map/all_to_all | solution.py:170
  21.7 4.4 %all-to-all-start.3 = ((bf16[8,256,512]{2,1,0:T(8,128)(2,1)}), bf16[8,256,512]{2,1,0:T(8,128)(2,1)S(1)}, u32[]{:S(2)}, u32[]{:S(2)}) async-start(bf16[8,256,512]{2,1,0:T(8,128)(2,1)} %pad_maximum_fusion), calls=%async_computation.3 | async-start | bytes 4194304 | tf_op jit(solution)/shard_map/all_to_all | solution.py:170
  26.0 1.8 reshape.94
  27.9 0.0 copy-start.5
  27.9 0.0 copy-start.4
  27.9 1.3 copy.18
  29.2 21.7 %all-to-all-done.3.kv_ref = bf16[8,256,512]{2,1,0:T(8,128)(2,1)S(1)} async-done(((bf16[8,256,512]{2,1,0:T(8,128)(2,1)}), bf16[8,256,512]{2,1,0:T(8,128)(2,1)S(1)}, u32[]{:S(2)}, u32[]{:S(2)}) %all-to-all-start.3) | async-done | bytes 2097184 | tf_op jit(solution)/shard_map/all_to_all | solution.py:170
  50.9 4.3 %all-to-all-start.2 = ((bf16[8,128,512]{2,1,0:T(8,128)(2,1)}), bf16[8,128,512]{2,1,0:T(8,128)(2,1)S(1)}, u32[]{:S(2)}, u32[]{:S(2)}) async-start(bf16[8,128,512]{2,1,0:T(8,128)(2,1)} %bitcast.29), calls=%async_computation.2 | async-start | bytes 2097152 | tf_op jit(solution)/shard_map/all_to_all | solution.py:170
  55.2 0.0 copy-done.5
  55.2 0.1 convert_element_type.21
  55.3 0.0 copy-done.4
  55.3 1.5 collective-permute-start
  56.8 12.4 %collective-permute-done = f32[5,512]{1,0:T(8,128)S(1)} collective-permute-done((f32[5,512]{1,0:T(8,128)S(1)}, f32[5,512]{1,0:T(8,128)S(1)}, u32[]{:S(2)}, u32[]{:S(2)}) %collective-permute-start) | collective-permute-done | bytes 10272 | tf_op jit(solution)/shard_map/ppermute | solution.py:180
  69.2 5.9 %state.1 = (bf16[4,144,128]{2,1,0:T(8,128)(2,1)}, f32[4,8,128,128]{3,2,1,0:T(8,128)S(1)}) custom-call(bf16[8,256,512]{2,1,0:T(8,128)(2,1)S(1)} %all-to-all-done.3.kv_ref, f32[32,128]{1,0:T(8,128)S(1)} %reshape.100.decay_ref), custom_call_target="tpu_custom_call" | custom-call | tf_op jit(solution)/shard_map/state/pallas_call | solution.py:196
  75.1 0.0 copy-start.1
  75.1 1.3 copy-done.1
  76.5 3.2 %collective-permute-start.2 = (bf16[4,144,128]{2,1,0:T(8,128)(2,1)}, bf16[4,144,128]{2,1,0:T(8,128)(2,1)S(1)}, u32[]{:S(2)}, u32[]{:S(2)}) collective-permute-start(bf16[4,144,128]{2,1,0:T(8,128)(2,1)} %get-tuple-element.8), channel_id=1, source_target_pairs={{0,8},{8,16},{16,24},{1,9},{9,17},{17,25},{2,10},{10,18},{18,26},{... | collective-permute-start | bytes 442376 | tf_op jit(solution)/shard_map/ppermute | solution.py:173
  79.7 1.3 collective-permute-start.3
  81.0 1.3 collective-permute-start.4
  82.3 0.0 copy-done
  82.3 1.9 %collective-permute-start.1 = (bf16[8,128,512]{2,1,0:T(8,128)(2,1)}, bf16[8,128,512]{2,1,0:T(8,128)(2,1)}, u32[]{:S(2)}, u32[]{:S(2)}) collective-permute-start(bf16[8,128,512]{2,1,0:T(8,128)(2,1)} %all-to-all-done.1), channel_id=1, source_target_pairs={{0,8},{8,16},{16,24},{1,9},{9,17},{17,25},{2,10},{10,18},{18,26},{... | collective-permute-start | bytes 3145736 | tf_op jit(solution)/shard_map/ppermute | solution.py:173
  84.2 0.0 all-to-all-done.2.q_ref
  84.2 0.0 collective-permute-done.2.refs_0_
  84.3 2.5 %collective-permute-done.3.refs_1_ = bf16[4,144,128]{2,1,0:T(8,128)(2,1)S(1)} collective-permute-done((bf16[4,144,128]{2,1,0:T(8,128)(2,1)}, bf16[4,144,128]{2,1,0:T(8,128)(2,1)S(1)}, u32[]{:S(2)}, u32[]{:S(2)}) %collective-permute-start.3) | collective-permute-done | bytes 147488 | tf_op jit(solution)/shard_map/ppermute | solution.py:173
  86.8 0.0 collective-permute-done.4.refs_2_
  86.8 8.2 %first.1 = bf16[8,128,512]{2,1,0:T(8,128)(2,1)} custom-call(bf16[8,128,512]{2,1,0:T(8,128)(2,1)S(1)} %all-to-all-done.2.q_ref, bf16[8,256,512]{2,1,0:T(8,128)(2,1)S(1)} %all-to-all-done.3.kv_ref, f32[32,128]{1,0:T(8,128)S(1)} %reshape.100.decay_ref, f32[4,8,128,128]{3,2,1,0:T(8,128)} %copy-done.1, f32[4,128]{1,0:T(4,128)S(1)} %constant_dynamic-slice_fusion.gain_ref, ...), custom_call_target="tpu_custom_call" | custom-call | tf_op jit(solution)/shard_map/first/pallas_call | solution.py:208
  95.0 9.3 %collective-permute-start.5 = (bf16[8,128,512]{2,1,0:T(8,128)(2,1)}, bf16[8,128,512]{2,1,0:T(8,128)(2,1)S(1)}, u32[]{:S(2)}, u32[]{:S(2)}) collective-permute-start(bf16[8,128,512]{2,1,0:T(8,128)(2,1)} %first.1), channel_id=1, source_target_pairs={{0,8},{8,16},{16,24},{1,9},{9,17},{17,25},{2,10},{10,18},{18,26},{... | collective-permute-start | bytes 3145736 | tf_op jit(solution)/shard_map/ppermute | solution.py:173
  104.3 1.8 reshape.86
  106.1 1.3 copy.16
  107.4 6.1 %all-to-all-start = ((bf16[8,128,512]{2,1,0:T(8,128)(2,1)}), bf16[8,128,512]{2,1,0:T(8,128)(2,1)S(1)}, u32[]{:S(2)}, u32[]{:S(2)}) async-start(bf16[8,128,512]{2,1,0:T(8,128)(2,1)} %bitcast.3), calls=%async_computation | async-start | bytes 2097152 | tf_op jit(solution)/shard_map/all_to_all | solution.py:170
  113.5 0.1 select_n.35
  113.6 0.1 broadcast_in_dim.15
  113.7 0.1 reshape.93.bias_ref
  113.8 0.1 select_n.33.window_ref
  113.9 13.2 %all-to-all-done = bf16[8,128,512]{2,1,0:T(8,128)(2,1)S(1)} async-done(((bf16[8,128,512]{2,1,0:T(8,128)(2,1)}), bf16[8,128,512]{2,1,0:T(8,128)(2,1)S(1)}, u32[]{:S(2)}, u32[]{:S(2)}) %all-to-all-start) | async-done | bytes 1048608 | tf_op jit(solution)/shard_map/all_to_all | solution.py:170
  127.1 0.0 collective-permute-done.1
  127.1 25.7 %weights.1.weights_ref = bf16[4,1024,512]{2,1,0:T(8,128)(2,1)} custom-call(s32[16,8]{1,0:T(8,128)S(1)} %select_n.33.window_ref, bf16[1024,512]{1,0:T(8,128)(2,1)S(1)} %bitcast.26, bf16[1024,512]{1,0:T(8,128)(2,1)} %bitcast.7.own_ref, bf16[1024,512]{1,0:T(8,128)(2,1)} %bitcast.8.earlier_ref, f32[16,512]{1,0:T(8,128)S(1)} %reshape.93.bias_ref), custom_call_target="tpu_custom_call" | custom-call | tf_op jit(solution)/shard_map/weights/pallas_call | solution.py:220
  152.8 0.0 collective-permute-done.5
  152.8 13.0 %sum.1 = bf16[1024,512]{1,0:T(8,128)(2,1)S(1)} custom-call(s32[16,8]{1,0:T(8,128)S(1)} %select_n.33.window_ref, bf16[4,1024,512]{2,1,0:T(8,128)(2,1)} %weights.1.weights_ref, bf16[1024,512]{1,0:T(8,128)(2,1)} %bitcast.15.own_ref, bf16[1024,512]{1,0:T(8,128)(2,1)S(1)} %bitcast.28), custom_call_target="tpu_custom_call" | custom-call | tf_op jit(solution)/shard_map/sum/pallas_call | solution.py:236
  165.8 17.3 %all_to_all.25 = bf16[8,128,512]{2,1,0:T(8,128)(2,1)S(1)} all-to-all(bf16[8,128,512]{2,1,0:T(8,128)(2,1)S(1)} %bitcast.27), channel_id=1, replica_groups=mesh['group'=4,'side'=2,'inner'=4] {'side','inner'}, dimensions={0} | all-to-all | bytes 2097152 | tf_op jit(solution)/shard_map/all_to_all | solution.py:170
  183.1 1.1 copy.24
  184.2 1.6 reshape.105
  (10 shorter events, 0.1 us)
Async XLA Ops:
  0.0 82.3 %copy-start = (f32[8,128]{1,0:T(8,128)S(1)}, f32[8,128]{1,0:T(8,128)}, u32[]{:S(2)}) copy-start(f32[8,128]{1,0:T(8,128)} %param.14) | copy-start | bytes 12292
  1.9 6.1 %copy-start.2 = (bf16[128,4096]{1,0:T(8,128)(2,1)S(1)}, bf16[128,4096]{1,0:T(8,128)(2,1)}, u32[]{:S(2)}) copy-start(bf16[128,4096]{1,0:T(8,128)(2,1)} %param.9) | copy-start | bytes 3145732
  3.2 18.5 %all-to-all-start.1 = ((bf16[8,128,512]{2,1,0:T(8,128)(2,1)}), bf16[8,128,512]{2,1,0:T(8,128)(2,1)}, u32[]{:S(2)}, u32[]{:S(2)}) async-start(bf16[8,128,512]{2,1,0:T(8,128)(2,1)} %bitcast.6), calls=%async_computation.1 | async-start | bytes 2097152 | tf_op jit(solution)/shard_map/all_to_all | solution.py:170
  7.9 1.2 copy-start.3
  21.7 29.2 %all-to-all-start.3 = ((bf16[8,256,512]{2,1,0:T(8,128)(2,1)}), bf16[8,256,512]{2,1,0:T(8,128)(2,1)S(1)}, u32[]{:S(2)}, u32[]{:S(2)}) async-start(bf16[8,256,512]{2,1,0:T(8,128)(2,1)} %pad_maximum_fusion), calls=%async_computation.3 | async-start | bytes 4194304 | tf_op jit(solution)/shard_map/all_to_all | solution.py:170
  27.9 27.3 %copy-start.5 = (s32[8,8]{1,0:T(8,128)S(1)}, s32[8,8]{1,0:T(8,128)}, u32[]{:S(2)}) copy-start(s32[8,8]{1,0:T(8,128)} %param.15) | copy-start | bytes 772
  27.9 27.4 %copy-start.4 = (f32[8,512]{1,0:T(8,128)S(1)}, f32[8,512]{1,0:T(8,128)}, u32[]{:S(2)}) copy-start(f32[8,512]{1,0:T(8,128)} %param.13) | copy-start | bytes 49156
  50.9 33.4 %all-to-all-start.2 = ((bf16[8,128,512]{2,1,0:T(8,128)(2,1)}), bf16[8,128,512]{2,1,0:T(8,128)(2,1)S(1)}, u32[]{:S(2)}, u32[]{:S(2)}) async-start(bf16[8,128,512]{2,1,0:T(8,128)(2,1)} %bitcast.29), calls=%async_computation.2 | async-start | bytes 2097152 | tf_op jit(solution)/shard_map/all_to_all | solution.py:170
  55.3 13.8 %collective-permute-start = (f32[5,512]{1,0:T(8,128)S(1)}, f32[5,512]{1,0:T(8,128)S(1)}, u32[]{:S(2)}, u32[]{:S(2)}) collective-permute-start(f32[5,512]{1,0:T(8,128)S(1)} %get-tuple-element.12), channel_id=1, source_target_pairs={{0,4},{4,0},{1,5},{5,1},{2,6},{6,2},{3,7},{7,3},{8,12},{12,8},{9,1... | collective-permute-start | bytes 30728 | tf_op jit(solution)/shard_map/ppermute | solution.py:180
  75.1 1.3 copy-start.1
  76.5 7.8 %collective-permute-start.2 = (bf16[4,144,128]{2,1,0:T(8,128)(2,1)}, bf16[4,144,128]{2,1,0:T(8,128)(2,1)S(1)}, u32[]{:S(2)}, u32[]{:S(2)}) collective-permute-start(bf16[4,144,128]{2,1,0:T(8,128)(2,1)} %get-tuple-element.8), channel_id=1, source_target_pairs={{0,8},{8,16},{16,24},{1,9},{9,17},{17,25},{2,10},{10,18},{18,26},{... | collective-permute-start | bytes 442376 | tf_op jit(solution)/shard_map/ppermute | solution.py:173
  79.7 7.1 %collective-permute-start.3 = (bf16[4,144,128]{2,1,0:T(8,128)(2,1)}, bf16[4,144,128]{2,1,0:T(8,128)(2,1)S(1)}, u32[]{:S(2)}, u32[]{:S(2)}) collective-permute-start(bf16[4,144,128]{2,1,0:T(8,128)(2,1)} %get-tuple-element.8), channel_id=1, source_target_pairs={{0,16},{8,24},{1,17},{9,25},{2,18},{10,26},{3,19},{11,27},{4,20},{... | collective-permute-start | bytes 442376 | tf_op jit(solution)/shard_map/ppermute | solution.py:173
  81.0 5.8 %collective-permute-start.4 = (bf16[4,144,128]{2,1,0:T(8,128)(2,1)}, bf16[4,144,128]{2,1,0:T(8,128)(2,1)}, u32[]{:S(2)}, u32[]{:S(2)}) collective-permute-start(bf16[4,144,128]{2,1,0:T(8,128)(2,1)} %get-tuple-element.8), channel_id=1, source_target_pairs={{0,24},{1,25},{2,26},{3,27},{4,28},{5,29},{6,30},{7,31}} | collective-permute-start | bytes 442376 | tf_op jit(solution)/shard_map/ppermute | solution.py:173
  82.3 44.8 %collective-permute-start.1 = (bf16[8,128,512]{2,1,0:T(8,128)(2,1)}, bf16[8,128,512]{2,1,0:T(8,128)(2,1)}, u32[]{:S(2)}, u32[]{:S(2)}) collective-permute-start(bf16[8,128,512]{2,1,0:T(8,128)(2,1)} %all-to-all-done.1), channel_id=1, source_target_pairs={{0,8},{8,16},{16,24},{1,9},{9,17},{17,25},{2,10},{10,18},{18,26},{... | collective-permute-start | bytes 3145736 | tf_op jit(solution)/shard_map/ppermute | solution.py:173
  95.0 57.8 %collective-permute-start.5 = (bf16[8,128,512]{2,1,0:T(8,128)(2,1)}, bf16[8,128,512]{2,1,0:T(8,128)(2,1)S(1)}, u32[]{:S(2)}, u32[]{:S(2)}) collective-permute-start(bf16[8,128,512]{2,1,0:T(8,128)(2,1)} %first.1), channel_id=1, source_target_pairs={{0,8},{8,16},{16,24},{1,9},{9,17},{17,25},{2,10},{10,18},{18,26},{... | collective-permute-start | bytes 3145736 | tf_op jit(solution)/shard_map/ppermute | solution.py:173
  107.4 19.7 %all-to-all-start = ((bf16[8,128,512]{2,1,0:T(8,128)(2,1)}), bf16[8,128,512]{2,1,0:T(8,128)(2,1)S(1)}, u32[]{:S(2)}, u32[]{:S(2)}) async-start(bf16[8,128,512]{2,1,0:T(8,128)(2,1)} %bitcast.3), calls=%async_computation | async-start | bytes 2097152 | tf_op jit(solution)/shard_map/all_to_all | solution.py:170

commit v2 on v1

v2 whole, which is shorter than its diff:
```python
import math

import jax
import jax.numpy as jnp
from jax import lax
from jax.experimental import pallas as pl
from jax.experimental.pallas import tpu as pltpu
from jax.sharding import Mesh
from jax.sharding import PartitionSpec as P

BLK = 64
STEP = 2
F32 = jnp.float32
BF16 = jnp.bfloat16
HIGHEST = lax.Precision.HIGHEST
VMEM = pl.BlockSpec(memory_space=pltpu.VMEM)
SMEM = pl.BlockSpec(memory_space=pltpu.SMEM)
ANY = pl.BlockSpec(memory_space=pl.ANY)
HBM = pl.BlockSpec(memory_space=pltpu.HBM)
PARAMS = pltpu.CompilerParams(vmem_limit_bytes=16 * 2**20)


def halves(x):
    high = x.astype(BF16)
    return high, (x - high.astype(F32)).astype(BF16)


def dot(a, b, dims):
    return lax.dot_general(a, b, (dims, ((), ())), preferred_element_type=F32)


def exact(a, b, dims):
    return lax.dot_general(a, b, (dims, ((), ())), precision=HIGHEST, preferred_element_type=F32)


def grid_of(shape):
    return lax.broadcasted_iota(jnp.int32, shape, 0), lax.broadcasted_iota(jnp.int32, shape, 1)


def summed_down(logs):
    length = logs.shape[1]
    row, col = grid_of((length, length))
    return exact((row >= col).astype(F32), logs, ((1,), (1,)))


def other_chunks(totals, chunks, later):
    count = totals.shape[1]
    row, col = grid_of((count, count))
    same = row // chunks == col // chunks
    taken = same & ((row > col) if later else (row < col))
    return exact(totals, taken.astype(F32), ((1,), (0,)))


def run_all(copies):
    for copy in copies:
        copy.start()
    for copy in copies:
        copy.wait()


def pieces_kernel(in_ref, *refs):
    out_ref, sem = refs[-2:]
    ways, _, here = out_ref.shape
    run_all([
        pltpu.make_async_copy(
            in_ref.at[:, pl.ds((d % (ways // 2) * 2 + d // (ways // 2)) * here, here)], out_ref.at[d], sem.at[d]
        )
        for d in range(ways)
    ])


def outward_kernel(columns_ref, *refs):
    ins, out_ref, sem = refs[:-2], refs[-2], refs[-1]
    length, here = ins[0].shape[0], out_ref.shape[2]
    run_all([
        pltpu.make_async_copy(
            ref.at[:, pl.ds(pl.multiple_of(columns_ref[k, 1], 128), here)],
            out_ref.at[k, pl.ds(n * length, length), :],
            sem.at[k, n],
        )
        for k in range(out_ref.shape[0])
        for n, ref in enumerate(ins)
    ])


def thirds(x):
    first = x.astype(BF16).astype(F32)
    second = (x - first).astype(BF16).astype(F32)
    return first, second, x - first - second


def parcel_kernel(count, extra, columns_ref, place_ref, *refs):
    ins, got_ref, table_ref = refs[:count], refs[count], refs[count + 1]
    scratch = 2 if extra else 1
    chips = got_ref.shape[0]
    outs, sem = refs[-scratch - chips : -scratch], refs[-1]
    length, here = ins[0].shape[0], got_ref.shape[2]
    core = place_ref[1]
    copies = []
    for k, out_ref in enumerate(outs):
        start = pl.multiple_of(columns_ref[k, 0], 128)
        for n, ref in enumerate(ins):
            copies.append(
                pltpu.make_async_copy(
                    ref.at[:, pl.ds(start, here)], out_ref.at[core, pl.ds(n * length, length), :], sem.at[k, n]
                )
            )
        copies.append(
            pltpu.make_async_copy(
                got_ref.at[k], out_ref.at[1 - core, pl.ds(0, count * length), :], sem.at[k, count]
            )
        )
    if extra:
        rows_ref = refs[-2]
        parts = jnp.concatenate(thirds(table_ref[...]), 0)
        if extra > parts.shape[0]:
            parts = jnp.concatenate([parts, jnp.zeros((extra - parts.shape[0], here), F32)], 0)
        for n in range(2):
            rows_ref[n] = parts.astype(BF16)
        copies.append(
            pltpu.make_async_copy(
                rows_ref, outs[chips // 2].at[:, pl.ds(count * length, extra), :], sem.at[0, count + 1]
            )
        )
    run_all(copies)


def gather_chunks(place_ref, refs, out_ref):
    for k, ref in enumerate(refs):
        chip = jnp.bitwise_xor(place_ref[0], k)
        out_ref[pl.ds(pl.multiple_of(2 * chip, 2), 2)] = ref[:, : out_ref.shape[1], :]


def state_kernel(place_ref, table_ref, *refs):
    parts, (sent_ref, start_ref, decay_ref, other_ref, kv_ref) = refs[:-5], refs[-5:]
    heads, width = sent_ref.shape[0], sent_ref.shape[2]
    chunks = kv_ref.shape[0]
    length = kv_ref.shape[1] // 2
    gather_chunks(place_ref, parts, kv_ref)
    size, here = table_ref.shape
    got = parts[len(parts) // 2][0, 2 * length :, :].astype(F32)
    mine, theirs = table_ref[...], got[:size] + got[size : 2 * size] + got[2 * size : 3 * size]
    leads = place_ref[2] == 0
    spans = (jnp.where(leads, mine, theirs), jnp.where(leads, theirs, mine))
    span = size * here // (heads + 1)
    for n, table in enumerate(spans):
        for h in range(heads):
            for t in range(chunks // 2):
                row, lane = divmod(h * span + t * length, here)
                at = h * chunks + n * (chunks // 2) + t
                decay_ref[at : at + 1, :] = table[row : row + 1, lane : lane + length]
        other_ref[n] = table[size - span // here :, :]
    down = summed_down(jnp.log(decay_ref[...]))
    totals = down[length - 1 : length, :]
    left = jnp.exp(totals - down)
    kept = jnp.exp(totals)
    factors = jnp.exp(totals + other_chunks(totals, chunks, True))
    place = lax.broadcasted_iota(jnp.int32, (16, width), 0)
    for h in range(heads):
        columns = slice(h * width, (h + 1) * width)
        state = jnp.zeros((width, width), F32)
        for c in range(chunks):
            at = h * chunks + c
            if c:
                high, low = halves(state)
                start_ref[h, c, :width, :] = high
                start_ref[h, c, width:, :] = low
            keys = kv_ref[c, :length, columns].astype(F32)
            values = kv_ref[c, length:, columns]
            high, low = halves(keys * left[:, at : at + 1])
            state = kept[:, at : at + 1] * state + dot(
                jnp.concatenate([high, low], 0), jnp.concatenate([values, values], 0), ((0,), (0,))
            )
        sent_ref[h, :width, :] = state.astype(BF16)
        factor = factors[:, h * chunks : h * chunks + 1]
        first, second, third = thirds(factor)
        sent_ref[h, width:, :] = jnp.where(
            place == 0, first, jnp.where(place == 1, second, jnp.where(place == 2, third, 0.0))
        ).astype(BF16)


def inside_kernel(count, place_ref, decay_ref, start_ref, *refs):
    q_parts, kv_parts, (raw_ref, q_ref, kv_ref) = refs[:count], refs[count : 2 * count], refs[2 * count :]
    chunks, length, here = q_ref.shape
    heads = decay_ref.shape[0] // chunks
    width = here // heads
    gather_chunks(place_ref, q_parts, q_ref)
    gather_chunks(place_ref, kv_parts, kv_ref)
    logs = jnp.log(decay_ref[...])
    row, col = grid_of((length, length))
    along = exact(logs, (row <= col).astype(F32), ((1,), (0,)))
    down = summed_down(logs)
    lifts = jnp.exp(down)
    causal = row >= col
    for h in range(heads):
        columns = slice(h * width, (h + 1) * width)
        for c in range(chunks):
            at = h * chunks + c
            queries = q_ref[c, :, columns]
            keys = kv_ref[c, :length, columns]
            values = kv_ref[c, length:, columns]
            gap = jnp.where(causal, down[:, at : at + 1] - along[at : at + 1, :], 0.0)
            weights = jnp.where(causal, jnp.exp(gap), 0.0) * dot(queries, keys, ((1,), (1,)))
            raw = dot(jnp.concatenate(halves(weights), 1), jnp.concatenate([values, values], 0), ((1,), (0,)))
            if c:
                raw = raw + lifts[:, at : at + 1] * dot(
                    jnp.concatenate([queries, queries], 1), start_ref[h, c], ((1,), (0,))
                )
            raw_ref[c, :, columns] = raw


def first_kernel(raw_ref, q_ref, decay_ref, gain_ref, *refs):
    earlier, out_ref = refs[:-2], refs[-1]
    chunks, length, here = q_ref.shape
    heads, width = gain_ref.shape
    down = summed_down(jnp.log(decay_ref[...]))
    lifts = jnp.exp(down + other_chunks(down[length - 1 : length, :], chunks, False))
    for h in range(heads):
        columns = slice(h * width, (h + 1) * width)
        carried = jnp.zeros((width, width), F32)
        factor = jnp.ones((1, 1), F32)
        for ref in earlier:
            carried = carried + factor * ref[h, :width, :].astype(F32)
            parts = ref[h, width:, :].astype(F32)
            factor = factor * (parts[0:1, 0:1] + parts[1:2, 0:1] + parts[2:3, 0:1])
        both = jnp.concatenate(halves(carried), 0)
        gain = gain_ref[h : h + 1, :]
        for c in range(chunks):
            at = h * chunks + c
            queries = q_ref[c, :, columns]
            outside = dot(jnp.concatenate([queries, queries], 1), both, ((1,), (0,)))
            raw = raw_ref[c, :, columns] + lifts[:, at : at + 1] * outside
            scale = lax.rsqrt(jnp.mean(raw * raw, axis=-1, keepdims=True) + 1e-06)
            out_ref[c, :, columns] = (raw * scale * gain).astype(BF16)


def pick(window_ref, b, source_ref, picked_ref):
    for j in range(picked_ref.shape[0] // BLK):
        start = pl.multiple_of(window_ref[b, j] * BLK, BLK)
        picked_ref[j * BLK : (j + 1) * BLK, :] = source_ref[pl.ds(start, BLK), :]


def weights_kernel(window_ref, own_ref, earlier_ref, bias_ref, q_ref, out_ref, keys_ref, picked_ref):
    tokens, here = own_ref.shape
    heads = out_ref.shape[0]
    width = here // heads
    picks = picked_ref.shape[1] // BLK
    group = pl.program_id(0)

    @pl.when(group == 0)
    def _():
        keys_ref[:tokens, :] = earlier_ref[...]
        keys_ref[tokens:, :] = own_ref[...]

    row, col = grid_of((BLK, picks * BLK))
    causal = jnp.where((col >= BLK) | (col <= row), 0.0, -1e30)
    scale = 1.0 / math.sqrt(width)
    for t in range(STEP):
        b = group * STEP + t
        pick(window_ref, b, keys_ref, picked_ref.at[t])
        bias = causal + bias_ref[pl.ds(b, 1), :]
        for h in range(heads):
            columns = slice(h * width, (h + 1) * width)
            scores = dot(q_ref[t * BLK : (t + 1) * BLK, columns], picked_ref[t, :, columns], ((1,), (1,))) * scale
            scores = scores + bias
            probs = jnp.exp(scores - jnp.max(scores, axis=-1, keepdims=True))
            share = 1.0 / jnp.sum(probs, axis=-1, keepdims=True)
            out_ref[h, t * BLK : (t + 1) * BLK, :] = (probs * share).astype(BF16)


def sum_kernel(window_ref, weights_ref, own_ref, earlier_ref, out_ref, values_ref, picked_ref):
    tokens, here = own_ref.shape
    heads = weights_ref.shape[0]
    width = here // heads
    group = pl.program_id(0)

    @pl.when(group == 0)
    def _():
        values_ref[:tokens, :] = earlier_ref[...]
        values_ref[tokens:, :] = own_ref[...]

    for t in range(STEP):
        b = group * STEP + t
        pick(window_ref, b, values_ref, picked_ref.at[t])
        rows = pl.ds(pl.multiple_of(b * BLK, BLK), BLK)
        for h in range(heads):
            columns = slice(h * width, (h + 1) * width)
            second = dot(weights_ref[h, t * BLK : (t + 1) * BLK, :], picked_ref[t, :, columns], ((1,), (0,)))
            out_ref[t * BLK : (t + 1) * BLK, columns] = (own_ref[rows, columns].astype(F32) + second).astype(BF16)


def local(lin_query, lin_key, lin_value, sparse_query, sparse_key, decay, norm_gain, block_pattern):
    groups, inner = lax.axis_size("group"), lax.axis_size("inner")
    level, side, index = lax.axis_index("group"), lax.axis_index("side"), lax.axis_index("inner")
    ways = 2 * inner
    chips = ways // 2
    length, model = lin_query.shape
    width = norm_gain.shape[1]
    heads = norm_gain.shape[0] // 2
    here = heads * width
    tokens = ways * length
    blocks = tokens // BLK
    picks = block_pattern.shape[1]

    chip, core = side * (inner // 2) + index // 2, index % 2
    place = jnp.stack([chip, core, side]).astype(jnp.int32)
    peers = jnp.bitwise_xor(chip, jnp.arange(chips, dtype=jnp.int32))
    cores = jnp.stack([core, 1 - core])
    indices = (peers % (inner // 2))[:, None] * 2 + cores[None, :]
    columns = ((indices * 2 + (peers // (inner // 2))[:, None]) * here).astype(jnp.int32)

    def swap(x):
        return lax.ppermute(x, ("side", "inner"), [(i, i ^ 1) for i in range(ways)])

    def spread(*arrays, table=None, after=()):
        rows = len(arrays) * length
        extra = 0 if table is None else -(-3 * table.shape[0] // 16) * 16
        after = after if table is None else (table, *after)
        out = pl.pallas_call(
            outward_kernel,
            out_shape=pltpu.HBM((chips, rows, here), BF16),
            in_specs=[SMEM] + [VMEM] * len(arrays),
            out_specs=HBM,
            scratch_shapes=[pltpu.SemaphoreType.DMA((chips, len(arrays)))],
            compiler_params=PARAMS,
            name="outward",
        )(columns, *arrays)
        parcels = pl.pallas_call(
            lambda *refs: parcel_kernel(len(arrays), extra, *refs),
            out_shape=[
                pltpu.HBM((2, rows + (extra if k == chips // 2 else 0), here), BF16) for k in range(chips)
            ],
            in_specs=[SMEM, SMEM] + [VMEM] * (len(arrays) + 1) + [VMEM] * bool(extra) + [ANY] * (len(after) - bool(extra)),
            out_specs=[HBM] * chips,
            scratch_shapes=[pltpu.VMEM((2, extra, here), BF16)] * bool(extra)
            + [pltpu.SemaphoreType.DMA((chips, len(arrays) + 2))],
            compiler_params=PARAMS,
            name="parcels",
        )(columns, place, *arrays, swap(out), *after)
        return parcels, [parcels[0]] + [
            lax.ppermute(x, ("side", "inner"), [(i, i ^ (2 * k)) for i in range(ways)])
            for k, x in enumerate(parcels)
            if k
        ]

    def exchange(x, after=()):
        pieces = pl.pallas_call(
            pieces_kernel,
            out_shape=pltpu.HBM((ways, length, here), BF16),
            in_specs=[VMEM] + [ANY] * len(after),
            out_specs=HBM,
            scratch_shapes=[pltpu.SemaphoreType.DMA((ways,))],
            compiler_params=PARAMS,
            name="pieces",
        )(x, *after)
        return lax.all_to_all(pieces, ("side", "inner"), split_axis=0, concat_axis=0, tiled=True)

    def onward(x, steps=1):
        return lax.ppermute(x, "group", [(i, i + steps) for i in range(groups - steps)])

    span = decay.shape[1]
    flat = block_pattern.reshape(1, -1).astype(F32)
    flat = jnp.pad(flat, ((0, 0), (0, span - flat.shape[1])))

    def table(first_head):
        return jnp.concatenate([lax.dynamic_slice_in_dim(decay, first_head, heads, 0), flat], 0).reshape(-1, here)

    mine = table(side * heads)
    gain = lax.dynamic_slice_in_dim(norm_gain, side * heads, heads, 0)

    sparse_keys = exchange(sparse_key)
    parcels, kv_parts = spread(lin_key, lin_value, table=table((1 - side) * heads))
    _, q_parts = spread(lin_query, after=kv_parts[1:3])
    earlier_keys = onward(sparse_keys)

    sent, starts, decays, others = pl.pallas_call(
        state_kernel,
        out_shape=(
            jax.ShapeDtypeStruct((heads, width + 16, width), BF16),
            jax.ShapeDtypeStruct((heads, ways, 2 * width, width), BF16),
            jax.ShapeDtypeStruct((heads * ways, length), F32),
            jax.ShapeDtypeStruct((2, span // here, here), F32),
        ),
        in_specs=[SMEM, VMEM] + [VMEM] * chips,
        out_specs=(VMEM,) * 4,
        scratch_shapes=[pltpu.VMEM((ways, 2 * length, here), BF16)],
        compiler_params=PARAMS,
        name="state",
    )(place, mine, *kv_parts)
    pattern = others.reshape(2, span)[:, : block_pattern.size].reshape(blocks, picks).astype(jnp.int32)
    window = jnp.where(pattern >= 0, pattern - (level - 1) * blocks, 0)
    bias = jnp.repeat(jnp.where(pattern >= 0, 0.0, -1e30).astype(F32), BLK, axis=1)
    states = [onward(sent, steps) for steps in range(1, groups)]
    raw, queries = pl.pallas_call(
        lambda *refs: inside_kernel(chips, *refs),
        out_shape=(
            jax.ShapeDtypeStruct((ways, length, here), F32),
            jax.ShapeDtypeStruct((ways, length, here), BF16),
        ),
        in_specs=[SMEM, VMEM, VMEM] + [VMEM] * (2 * chips),
        out_specs=(VMEM, VMEM),
        scratch_shapes=[pltpu.VMEM((ways, 2 * length, here), BF16)],
        compiler_params=PARAMS,
        cost_estimate=pl.CostEstimate(flops=2**31, bytes_accessed=6 * 2**20, transcendentals=2**19),
        name="inside",
    )(place, decays, starts, *q_parts, *kv_parts)
    sparse_queries = exchange(sparse_query, after=(raw,))
    first = pl.pallas_call(
        first_kernel,
        out_shape=jax.ShapeDtypeStruct((ways, length, here), BF16),
        in_specs=[VMEM] * (4 + len(states)) + [ANY],
        out_specs=VMEM,
        compiler_params=PARAMS,
        name="first",
    )(raw, queries, decays, gain, *states, earlier_keys)
    earlier_first = onward(first)

    steps = blocks // STEP
    rows = STEP * BLK
    whole = pl.BlockSpec((tokens, here), lambda g: (0, 0))
    part = pl.BlockSpec((rows, here), lambda g: (g, 0))
    table = pl.BlockSpec((heads, rows, picks * BLK), lambda g: (0, g, 0))
    weights = pl.pallas_call(
        weights_kernel,
        out_shape=jax.ShapeDtypeStruct((heads, tokens, picks * BLK), BF16),
        grid=(steps,),
        in_specs=[SMEM, whole, whole, pl.BlockSpec((blocks, picks * BLK), lambda g: (0, 0)), part],
        out_specs=table,
        scratch_shapes=[
            pltpu.VMEM((2 * tokens, here), BF16),
            pltpu.VMEM((STEP, picks * BLK, here), BF16),
        ],
        compiler_params=PARAMS,
        cost_estimate=pl.CostEstimate(flops=2**31, bytes_accessed=8 * 2**20, transcendentals=2**21),
        name="weights",
    )(
        window,
        sparse_keys.reshape(tokens, here),
        earlier_keys.reshape(tokens, here),
        bias,
        sparse_queries.reshape(tokens, here),
    )
    layer = pl.pallas_call(
        sum_kernel,
        out_shape=jax.ShapeDtypeStruct((tokens, here), BF16),
        grid=(steps,),
        in_specs=[SMEM, table, whole, whole],
        out_specs=part,
        scratch_shapes=[
            pltpu.VMEM((2 * tokens, here), BF16),
            pltpu.VMEM((STEP, picks * BLK, here), BF16),
        ],
        compiler_params=PARAMS,
        name="sum",
    )(window, weights, first.reshape(tokens, here), earlier_first.reshape(tokens, here))
    back = lax.all_to_all(
        layer.reshape(ways, length, here), ("side", "inner"), split_axis=0, concat_axis=0, tiled=True
    )
    return back.reshape(2, inner, length, here).transpose(2, 1, 0, 3).reshape(length, model)


def solution(mesh):
    spans, inner = mesh.devices.shape
    finer = Mesh(mesh.devices.reshape(spans // 2, 2, inner), ("group", "side", "inner"))
    rows = P(("group", "side", "inner"), None)
    placed = (rows,) * 5 + (P("inner", ("group", "side")), P("inner", None), P(("group", "side"), None))
    return jax.shard_map(local, mesh=finer, in_specs=placed, out_specs=rows, check_vma=False)
```

time: 187 us -> 132 us (0.71)
  waiting for transfers between devices: 59.7 us -> 36.9 us
  Pallas kernels: 52.8 us -> 33.7 us
  starting transfers between devices: 38.1 us -> 29.4 us
  local copies, waits for them, and re-layouts: 16.2 us -> 11.5 us
    all_to_all x4 -> x2, waiting for transfers between devices: 44.8 us -> 9.91 us  [exchange(): lax.all_to_all(pieces, ('side', 'inner'), split_axis=0, concat_axis=0, ti...]
    pallas_call x1, Pallas kernels: 25.7 us -> 8.25 us  [local(): pl.pallas_call(weights_kernel, out_shape=jax.ShapeDtypeStruct((heads, tok...]
    pallas_call x0 -> x7, Pallas kernels: none -> 14.3 us  [the longest x2 5.11 us: spread(): pl.pallas_call(lambda *refs: parcel_kernel(len(arrays), extra, *refs), ou...]
    all_to_all x4 -> x2, starting transfers between devices: 19.6 us -> 9.2 us  [exchange(): lax.all_to_all(pieces, ('side', 'inner'), split_axis=0, concat_axis=0, ti...]
    reshape x9 -> x0, local copies, waits for them, and re-layouts: 9.02 us -> none  [the longest x8 9.01 us: pieces(): x.reshape(length, inner, 2, here).transpose(2, 1, 0, 3)]
    pallas_call x1, Pallas kernels: 13 us -> 4.35 us  [local(): pl.pallas_call(sum_kernel, out_shape=jax.ShapeDtypeStruct((tokens, here),...]
    ppermute x5, waiting for transfers between devices: 2.54 us -> 10.6 us  [onward(): lax.ppermute(x, 'group', [(i, i + steps) for i in range(groups - steps)])]
    unnamed x12 -> x43, local copies, waits for them, and re-layouts: 1.47 us -> 8.38 us
  transfers between devices with their start and end apart: 10 -> 15, of which waited for: 5 -> 8; matrix products, arithmetic and copies ran while one was open for 6% -> 0% of each run, Pallas kernels for 21% -> 21%
where the time goes in v2:
time: 132 us; the launch traced here: 131 us
  waiting for transfers between devices  36.9 us (28%)
  Pallas kernels  33.7 us (26%)
  starting transfers between devices  29.4 us (22%)
  blocking collectives  18.5 us (14%)
  local copies, waits for them, and re-layouts  11.5 us (9%)
    all_to_all x1, blocking collectives, local(): lax.all_to_all(layer.reshape(ways, length, here), ('side', 'inner'), spli...  18.5 us
    ppermute x6, waiting for transfers between devices, spread(): lax.ppermute(x, ('side', 'inner'), [(i, i ^ 2 * k) for i in range(ways)])  16.4 us
    ppermute x5, starting transfers between devices, onward(): lax.ppermute(x, 'group', [(i, i + steps) for i in range(groups - steps)])  12.2 us
    ppermute x5, waiting for transfers between devices, onward(): lax.ppermute(x, 'group', [(i, i + steps) for i in range(groups - steps)])  10.6 us
    all_to_all x2, waiting for transfers between devices, exchange(): lax.all_to_all(pieces, ('side', 'inner'), split_axis=0, concat_axis=0, ti...  9.91 us
    all_to_all x2, starting transfers between devices, exchange(): lax.all_to_all(pieces, ('side', 'inner'), split_axis=0, concat_axis=0, ti...  9.2 us
    unnamed x43, local copies, waits for them, and re-layouts  8.38 us
    pallas_call x1, Pallas kernels, local(): pl.pallas_call(weights_kernel, out_shape=jax.ShapeDtypeStruct((heads, tok...  8.25 us
  transfers between devices with their start and end apart: 15, of which 8 were waited for; matrix products, arithmetic and copies ran while one was open for 0% of the time, Pallas kernels for 21%

profile of v2, /device:TPU:17, one launch (start us, length us, event | category | flops | bytes accessed | tf_op | source)
XLA Modules:
  0.0 130.6 jit_solution(9646522244216832867)
XLA Ops:
  0.0 0.1 pad_add_fusion.1
  0.1 0.1 add_multiply_fusion.columns_ref.refs_0_
  0.2 1.2 copy-done.1
  1.4 1.2 copy-done.3
  2.6 1.6 %outward.2 = bf16[4,256,512]{2,1,0:T(8,128)(2,1)} custom-call(s32[4,2]{1,0:T(4,128)S(1)} %add_multiply_fusion.columns_ref.refs_0_, bf16[128,4096]{1,0:T(8,128)(2,1)S(1)} %copy-done.1, bf16[128,4096]{1,0:T(8,128)(2,1)S(1)} %copy-done.3), custom_call_target="tpu_custom_call" | custom-call | tf_op jit(solution)/shard_map/outward/pallas_call | solution.py:319
  4.2 0.0 copy-start.20
  4.2 0.0 copy-start.19
  4.2 0.0 copy-start.2
  4.3 0.0 copy-start.4
  4.3 0.7 collective-permute-start
  5.0 1.1 pieces.2
  6.1 4.2 %all-to-all-start = ((bf16[8,128,512]{2,1,0:T(8,128)(2,1)}), bf16[8,128,512]{2,1,0:T(8,128)(2,1)}, u32[]{:S(2)}, u32[]{:S(2)}) async-start(bf16[8,128,512]{2,1,0:T(8,128)(2,1)} %pieces.2), calls=%async_computation | async-start | bytes 2097152 | tf_op jit(solution)/shard_map/all_to_all | solution.py:356
  10.3 0.0 copy-start.5
  10.3 0.1 convert_element_type.21
  10.4 0.1 pad_add_fusion.refs_1_.place_ref.refs_0_
  10.5 0.0 collective-permute-done.refs_4_
  10.6 2.7 %parcels.2 = (bf16[2,256,512]{2,1,0:T(8,128)(2,1)}, bf16[2,256,512]{2,1,0:T(8,128)(2,1)}, bf16[2,272,512]{2,1,0:T(8,128)(2,1)}, bf16[2,256,512]{2,1,0:T(8,128)(2,1)}) custom-call(s32[4,2]{1,0:T(4,128)S(1)} %add_multiply_fusion.columns_ref.refs_0_, s32[3]{0:T(128)S(1)} %pad_add_fusion.refs_1_.place_ref.refs_0_, bf16[128,4096]{1,0:T(8,128)(2,1)S(1)} %copy-done.2, ...), custom_call_target="tpu_custom_call" | custom-call | tf_op jit(solution)/shard_map/parcels/pallas_call | solution.py:328
  13.3 1.4 %collective-permute-start.2 = (bf16[2,272,512]{2,1,0:T(8,128)(2,1)}, bf16[2,272,512]{2,1,0:T(8,128)(2,1)S(1)}, u32[]{:S(2)}, u32[]{:S(2)}) collective-permute-start(bf16[2,272,512]{2,1,0:T(8,128)(2,1)} %get-tuple-element.21), channel_id=1, source_target_pairs={{0,4},{1,5},{2,6},{3,7},{4,0},{5,1},{6,2},{7,3},{8,12},{9,13},{10,... | collective-permute-start | bytes 1671176 | tf_op jit(solution)/shard_map/ppermute | solution.py:341
  14.7 1.4 %outward.3 = bf16[4,128,512]{2,1,0:T(8,128)(2,1)} custom-call(s32[4,2]{1,0:T(4,128)S(1)} %add_multiply_fusion.columns_ref.refs_0_, bf16[128,4096]{1,0:T(8,128)(2,1)S(1)} %copy-done.5), custom_call_target="tpu_custom_call" | custom-call | tf_op jit(solution)/shard_map/outward/pallas_call | solution.py:319
  16.1 0.7 collective-permute-start.5
  16.9 1.2 collective-permute-start.1
  18.1 5.9 %all-to-all-done = bf16[8,128,512]{2,1,0:T(8,128)(2,1)} async-done(((bf16[8,128,512]{2,1,0:T(8,128)(2,1)}), bf16[8,128,512]{2,1,0:T(8,128)(2,1)}, u32[]{:S(2)}, u32[]{:S(2)}) %all-to-all-start) | async-done | bytes 1048608 | tf_op jit(solution)/shard_map/all_to_all | solution.py:356
  24.0 3.2 %collective-permute-start.4 = (bf16[8,128,512]{2,1,0:T(8,128)(2,1)}, bf16[8,128,512]{2,1,0:T(8,128)(2,1)}, u32[]{:S(2)}, u32[]{:S(2)}) collective-permute-start(bf16[8,128,512]{2,1,0:T(8,128)(2,1)} %all-to-all-done), channel_id=1, source_target_pairs={{0,8},{8,16},{16,24},{1,9},{9,17},{17,25},{2,10},{10,18},{18,26},{... | collective-permute-start | bytes 3145736 | tf_op jit(solution)/shard_map/ppermute | solution.py:359
  27.2 1.2 collective-permute-start.3
  28.4 0.0 collective-permute-done.5.refs_3_
  28.4 6.8 %collective-permute-done.1.refs_1_.refs_4_.refs_8_ = bf16[2,256,512]{2,1,0:T(8,128)(2,1)S(1)} collective-permute-done((bf16[2,256,512]{2,1,0:T(8,128)(2,1)}, bf16[2,256,512]{2,1,0:T(8,128)(2,1)S(1)}, u32[]{:S(2)}, u32[]{:S(2)}) %collective-permute-start.1) | collective-permute-done | bytes 524320 | tf_op jit(solution)/shard_map/ppermute | solution.py:341
  35.2 0.7 collective-permute-done.2.refs_2_.refs_5_.refs_9_
  35.9 2.4 %parcels.3 = (bf16[2,128,512]{2,1,0:T(8,128)(2,1)}, bf16[2,128,512]{2,1,0:T(8,128)(2,1)}, bf16[2,128,512]{2,1,0:T(8,128)(2,1)}, bf16[2,128,512]{2,1,0:T(8,128)(2,1)}) custom-call(s32[4,2]{1,0:T(4,128)S(1)} %add_multiply_fusion.columns_ref.refs_0_, s32[3]{0:T(128)S(1)} %pad_add_fusion.refs_1_.place_ref.refs_0_, bf16[128,4096]{1,0:T(8,128)(2,1)S(1)} %copy-done.5, ...), custom_call_target="tpu_custom_call" | custom-call | tf_op jit(solution)/shard_map/parcels/pallas_call | solution.py:328
  38.3 1.3 collective-permute-start.6
  39.5 0.3 collective-permute-start.7
  39.8 1.2 collective-permute-start.8
  41.0 7.0 %collective-permute-done.3.refs_3_.refs_10_ = bf16[2,256,512]{2,1,0:T(8,128)(2,1)S(1)} collective-permute-done((bf16[2,256,512]{2,1,0:T(8,128)(2,1)}, bf16[2,256,512]{2,1,0:T(8,128)(2,1)S(1)}, u32[]{:S(2)}, u32[]{:S(2)}) %collective-permute-start.3) | collective-permute-done | bytes 524320 | tf_op jit(solution)/shard_map/ppermute | solution.py:341
  48.0 3.5 %state.1 = (bf16[4,144,128]{2,1,0:T(8,128)(2,1)S(1)}, bf16[4,8,256,128]{3,2,1,0:T(8,128)(2,1)S(1)}, f32[32,128]{1,0:T(8,128)S(1)}, f32[2,1,512]{2,1,0:T(1,128)S(1)}) custom-call(s32[3]{0:T(128)S(1)} %pad_add_fusion.refs_1_.place_ref.refs_0_, f32[5,512]{1,0:T(8,128)S(1)} %get-tuple-element.36.table_ref, bf16[2,256,512]{2,1,0:T(8,128)(2,1)S(1)} %copy-done.14, ...), custom_call_target="tpu_custom_call" | custom-call | tf_op jit(solution)/shard_map/state/pallas_call | solution.py:376
  51.5 1.3 collective-permute-start.10
  52.8 1.5 %collective-permute-done.6.refs_4_ = bf16[2,128,512]{2,1,0:T(8,128)(2,1)S(1)} collective-permute-done((bf16[2,128,512]{2,1,0:T(8,128)(2,1)}, bf16[2,128,512]{2,1,0:T(8,128)(2,1)S(1)}, u32[]{:S(2)}, u32[]{:S(2)}) %collective-permute-start.6) | collective-permute-done | bytes 262176 | tf_op jit(solution)/shard_map/ppermute | solution.py:341
  54.3 0.7 collective-permute-start.11
  54.9 0.0 collective-permute-done.7.refs_5_
  54.9 3.8 %collective-permute-start.9 = (bf16[4,144,128]{2,1,0:T(8,128)(2,1)S(1)}, bf16[4,144,128]{2,1,0:T(8,128)(2,1)S(1)}, u32[]{:S(2)}, u32[]{:S(2)}) collective-permute-start(bf16[4,144,128]{2,1,0:T(8,128)(2,1)S(1)} %get-tuple-element.32), channel_id=1, source_target_pairs={{0,8},{8,16},{16,24},{1,9},{9,17},{17,25},{2,10},{10,18},{18,26},{... | collective-permute-start | bytes 442376 | tf_op jit(solution)/shard_map/ppermute | solution.py:359
  58.8 0.4 collective-permute-done.8.refs_6_
  59.2 1.1 copy-done.7
  60.3 1.0 copy-done.9
  61.3 4.1 %inside.1 = (f32[8,128,512]{2,1,0:T(8,128)S(1)}, bf16[8,128,512]{2,1,0:T(8,128)(2,1)S(1)}) custom-call(s32[3]{0:T(128)S(1)} %pad_add_fusion.refs_1_.place_ref.refs_0_, f32[32,128]{1,0:T(8,128)S(1)} %get-tuple-element.24.refs_1_.decay_ref, bf16[4,8,256,128]{3,2,1,0:T(8,128)(2,1)S(1)} %get-tuple-element.25.refs_2_, bf16[2,128,512]{2,1,0:T(8,128)(2,1)S(1)} %copy-done.18, ...), custom_call_target="tpu_custom_call" | custom-call | flops 2147483648 | bytes 6291456 | tf_op jit(solution)/shard_map/inside/pallas_call | solution.py:394
  65.4 1.0 copy-done.12
  66.4 1.0 pieces.3
  67.4 5.0 %all-to-all-start.1 = ((bf16[8,128,512]{2,1,0:T(8,128)(2,1)}), bf16[8,128,512]{2,1,0:T(8,128)(2,1)}, u32[]{:S(2)}, u32[]{:S(2)}) async-start(bf16[8,128,512]{2,1,0:T(8,128)(2,1)} %pieces.3), calls=%async_computation.1 | async-start | bytes 2097152 | tf_op jit(solution)/shard_map/all_to_all | solution.py:356
  72.4 0.0 collective-permute-done.10.refs_1_
  72.5 0.0 collective-permute-done.9.refs_0_
  72.5 0.7 copy-done.16
  73.1 0.0 collective-permute-done.4.refs_3_
  73.2 1.2 copy-done.13
  74.4 0.9 copy-done.17
  75.3 3.3 %first.1 = bf16[8,128,512]{2,1,0:T(8,128)(2,1)S(1)} custom-call(f32[8,128,512]{2,1,0:T(8,128)S(1)} %get-tuple-element.30.refs_0_.raw_ref, bf16[8,128,512]{2,1,0:T(8,128)(2,1)S(1)} %copy-done.13, f32[32,128]{1,0:T(8,128)S(1)} %get-tuple-element.24.refs_1_.decay_ref, f32[4,128]{1,0:T(4,128)S(1)} %constant_dynamic-slice_fusion.gain_ref, ...), custom_call_target="tpu_custom_call" | custom-call | tf_op jit(solution)/shard_map/first/pallas_call | solution.py:408
  78.6 3.2 %collective-permute-start.12 = (bf16[8,128,512]{2,1,0:T(8,128)(2,1)S(1)}, bf16[8,128,512]{2,1,0:T(8,128)(2,1)S(1)}, u32[]{:S(2)}, u32[]{:S(2)}) collective-permute-start(bf16[8,128,512]{2,1,0:T(8,128)(2,1)S(1)} %first.1), channel_id=1, source_target_pairs={{0,8},{8,16},{16,24},{1,9},{9,17},{17,25},{2,10},{10,18},{18,26},{... | collective-permute-start | bytes 3145736 | tf_op jit(solution)/shard_map/ppermute | solution.py:359
  81.8 0.1 select_n.59
  81.9 0.1 broadcast_in_dim.18
  82.0 0.1 reshape.93.bias_ref
  82.0 0.1 select_n.57.window_ref
  82.1 4.0 %all-to-all-done.1 = bf16[8,128,512]{2,1,0:T(8,128)(2,1)} async-done(((bf16[8,128,512]{2,1,0:T(8,128)(2,1)}), bf16[8,128,512]{2,1,0:T(8,128)(2,1)}, u32[]{:S(2)}, u32[]{:S(2)}) %all-to-all-start.1) | async-done | bytes 1048608 | tf_op jit(solution)/shard_map/all_to_all | solution.py:356
  86.2 8.3 %weights.1.weights_ref = bf16[4,1024,512]{2,1,0:T(8,128)(2,1)S(1)} custom-call(s32[16,8]{1,0:T(8,128)S(1)} %select_n.57.window_ref, bf16[1024,512]{1,0:T(8,128)(2,1)} %bitcast.4.own_ref, bf16[1024,512]{1,0:T(8,128)(2,1)} %bitcast.5.earlier_ref, f32[16,512]{1,0:T(8,128)S(1)} %reshape.93.bias_ref, bf16[1024,512]{1,0:T(8,128)(2,1)} %bitcast.6.q_ref), custom_call_target="tpu_custom_call" | custom-call | flops 2147483648 | bytes 8388608 | tf_op jit(solution)/shard_map/weights/pallas_call | solution.py:423
  94.4 10.6 %collective-permute-done.12 = bf16[8,128,512]{2,1,0:T(8,128)(2,1)S(1)} collective-permute-done((bf16[8,128,512]{2,1,0:T(8,128)(2,1)S(1)}, bf16[8,128,512]{2,1,0:T(8,128)(2,1)S(1)}, u32[]{:S(2)}, u32[]{:S(2)}) %collective-permute-start.12) | collective-permute-done | bytes 1048608 | tf_op jit(solution)/shard_map/ppermute | solution.py:359
  105.1 4.4 %sum.1 = bf16[1024,512]{1,0:T(8,128)(2,1)S(1)} custom-call(s32[16,8]{1,0:T(8,128)S(1)} %select_n.57.window_ref, bf16[4,1024,512]{2,1,0:T(8,128)(2,1)S(1)} %weights.1.weights_ref, bf16[1024,512]{1,0:T(8,128)(2,1)S(1)} %bitcast.18, bf16[1024,512]{1,0:T(8,128)(2,1)S(1)} %bitcast.19), custom_call_target="tpu_custom_call" | custom-call | tf_op jit(solution)/shard_map/sum/pallas_call | solution.py:443
  109.4 18.5 %all_to_all.15 = bf16[8,128,512]{2,1,0:T(8,128)(2,1)S(1)} all-to-all(bf16[8,128,512]{2,1,0:T(8,128)(2,1)S(1)} %bitcast.17), channel_id=1, replica_groups=mesh['group'=4,'side'=2,'inner'=4] {'side','inner'}, dimensions={0} | all-to-all | bytes 2097152 | tf_op jit(solution)/shard_map/all_to_all | solution.py:456
  127.9 1.1 copy.14
  129.0 1.6 %reshape.99 = bf16[128,4096]{1,0:T(8,128)(2,1)} reshape(bf16[128,4,2,512]{3,2,1,0:T(2,128)(2,1)S(1)} %bitcast.21) | data formatting | bytes 2097152 | tf_op jit(solution)/shard_map/reshape | solution.py:459
  (38 shorter events, 0.1 us)
Async XLA Ops:
  0.0 72.4 %copy-start = (f32[8,128]{1,0:T(8,128)S(1)}, f32[8,128]{1,0:T(8,128)}, u32[]{:S(2)}) copy-start(f32[8,128]{1,0:T(8,128)} %param.14) | copy-start | bytes 12292
  0.2 1.2 copy-start.1
  1.4 1.2 copy-start.3
  2.6 2.4 %copy-start.10 = (bf16[128,4096]{1,0:T(8,128)(2,1)S(1)}, bf16[128,4096]{1,0:T(8,128)(2,1)}, u32[]{:S(2)}) copy-start(bf16[128,4096]{1,0:T(8,128)(2,1)} %in_ref.2) | copy-start | bytes 3145732
  4.2 6.1 %copy-start.20 = (s32[8,8]{1,0:T(8,128)S(1)}, s32[8,8]{1,0:T(8,128)}, u32[]{:S(2)}) copy-start(s32[8,8]{1,0:T(8,128)} %param.15) | copy-start | bytes 772
  4.2 6.3 %copy-start.19 = (f32[8,512]{1,0:T(8,128)S(1)}, f32[8,512]{1,0:T(8,128)}, u32[]{:S(2)}) copy-start(f32[8,512]{1,0:T(8,128)} %param.13) | copy-start | bytes 49156
  4.2 6.3 %copy-start.2 = (bf16[128,4096]{1,0:T(8,128)(2,1)S(1)}, bf16[128,4096]{1,0:T(8,128)(2,1)}, u32[]{:S(2)}) copy-start(bf16[128,4096]{1,0:T(8,128)(2,1)} %refs_2_.2) | copy-start | bytes 3145732
  4.3 6.3 %copy-start.4 = (bf16[128,4096]{1,0:T(8,128)(2,1)S(1)}, bf16[128,4096]{1,0:T(8,128)(2,1)}, u32[]{:S(2)}) copy-start(bf16[128,4096]{1,0:T(8,128)(2,1)} %refs_3_.1) | copy-start | bytes 3145732
  4.3 6.3 %collective-permute-start = (bf16[4,256,512]{2,1,0:T(8,128)(2,1)}, bf16[4,256,512]{2,1,0:T(8,128)(2,1)}, u32[]{:S(2)}, u32[]{:S(2)}) collective-permute-start(bf16[4,256,512]{2,1,0:T(8,128)(2,1)} %outward.2), channel_id=1, source_target_pairs={{0,1},{1,0},{2,3},{3,2},{4,5},{5,4},{6,7},{7,6},{8,9},{9,8},{10,11... | collective-permute-start | bytes 3145736 | tf_op jit(solution)/shard_map/ppermute | solution.py:313
  6.1 17.9 %all-to-all-start = ((bf16[8,128,512]{2,1,0:T(8,128)(2,1)}), bf16[8,128,512]{2,1,0:T(8,128)(2,1)}, u32[]{:S(2)}, u32[]{:S(2)}) async-start(bf16[8,128,512]{2,1,0:T(8,128)(2,1)} %pieces.2), calls=%async_computation | async-start | bytes 2097152 | tf_op jit(solution)/shard_map/all_to_all | solution.py:356
  10.3 4.4 %copy-start.5 = (bf16[128,4096]{1,0:T(8,128)(2,1)S(1)}, bf16[128,4096]{1,0:T(8,128)(2,1)}, u32[]{:S(2)}) copy-start(bf16[128,4096]{1,0:T(8,128)(2,1)} %refs_2_.3) | copy-start | bytes 3145732
  13.3 34.7 %copy-start.14 = (bf16[2,256,512]{2,1,0:T(8,128)(2,1)S(1)}, bf16[2,256,512]{2,1,0:T(8,128)(2,1)}, u32[]{:S(2)}) copy-start(bf16[2,256,512]{2,1,0:T(8,128)(2,1)} %get-tuple-element.19.refs_0_.refs_7_) | copy-start | bytes 1572868
  13.3 22.6 %collective-permute-start.2 = (bf16[2,272,512]{2,1,0:T(8,128)(2,1)}, bf16[2,272,512]{2,1,0:T(8,128)(2,1)S(1)}, u32[]{:S(2)}, u32[]{:S(2)}) collective-permute-start(bf16[2,272,512]{2,1,0:T(8,128)(2,1)} %get-tuple-element.21), channel_id=1, source_target_pairs={{0,4},{1,5},{2,6},{3,7},{4,0},{5,1},{6,2},{7,3},{8,12},{9,13},{10,... | collective-permute-start | bytes 1671176 | tf_op jit(solution)/shard_map/ppermute | solution.py:341
  16.1 12.3 %collective-permute-start.5 = (bf16[4,128,512]{2,1,0:T(8,128)(2,1)}, bf16[4,128,512]{2,1,0:T(8,128)(2,1)}, u32[]{:S(2)}, u32[]{:S(2)}) collective-permute-start(bf16[4,128,512]{2,1,0:T(8,128)(2,1)} %outward.3), channel_id=1, source_target_pairs={{0,1},{1,0},{2,3},{3,2},{4,5},{5,4},{6,7},{7,6},{8,9},{9,8},{10,11... | collective-permute-start | bytes 1572872 | tf_op jit(solution)/shard_map/ppermute | solution.py:313
  16.9 18.3 %collective-permute-start.1 = (bf16[2,256,512]{2,1,0:T(8,128)(2,1)}, bf16[2,256,512]{2,1,0:T(8,128)(2,1)S(1)}, u32[]{:S(2)}, u32[]{:S(2)}) collective-permute-start(bf16[2,256,512]{2,1,0:T(8,128)(2,1)} %get-tuple-element.20), channel_id=1, source_target_pairs={{0,2},{1,3},{2,0},{3,1},{4,6},{5,7},{6,4},{7,5},{8,10},{9,11},{10,... | collective-permute-start | bytes 1572872 | tf_op jit(solution)/shard_map/ppermute | solution.py:341
  24.0 49.2 %collective-permute-start.4 = (bf16[8,128,512]{2,1,0:T(8,128)(2,1)}, bf16[8,128,512]{2,1,0:T(8,128)(2,1)}, u32[]{:S(2)}, u32[]{:S(2)}) collective-permute-start(bf16[8,128,512]{2,1,0:T(8,128)(2,1)} %all-to-all-done), channel_id=1, source_target_pairs={{0,8},{8,16},{16,24},{1,9},{9,17},{17,25},{2,10},{10,18},{18,26},{... | collective-permute-start | bytes 3145736 | tf_op jit(solution)/shard_map/ppermute | solution.py:359
  27.2 32.1 %copy-start.15 = (bf16[2,256,512]{2,1,0:T(8,128)(2,1)S(1)}, bf16[2,256,512]{2,1,0:T(8,128)(2,1)}, u32[]{:S(2)}) copy-start(bf16[2,256,512]{2,1,0:T(8,128)(2,1)} %get-tuple-element.19.refs_0_.refs_7_) | copy-start | bytes 1572868
  27.2 20.8 %collective-permute-start.3 = (bf16[2,256,512]{2,1,0:T(8,128)(2,1)}, bf16[2,256,512]{2,1,0:T(8,128)(2,1)S(1)}, u32[]{:S(2)}, u32[]{:S(2)}) collective-permute-start(bf16[2,256,512]{2,1,0:T(8,128)(2,1)} %get-tuple-element.22), channel_id=1, source_target_pairs={{0,6},{1,7},{2,4},{3,5},{4,2},{5,3},{6,0},{7,1},{8,14},{9,15},{10,... | collective-permute-start | bytes 1572872 | tf_op jit(solution)/shard_map/ppermute | solution.py:341
  35.2 16.3 %copy-start.8 = (bf16[2,256,512]{2,1,0:T(8,128)(2,1)}, bf16[2,256,512]{2,1,0:T(8,128)(2,1)S(1)}, u32[]{:S(2)}) copy-start(bf16[2,256,512]{2,1,0:T(8,128)(2,1)S(1)} %collective-permute-done.1.refs_1_.refs_4_.refs_8_) | copy-start | bytes 1572868
  35.9 15.6 %copy-start.6 = (bf16[2,272,512]{2,1,0:T(8,128)(2,1)}, bf16[2,272,512]{2,1,0:T(8,128)(2,1)S(1)}, u32[]{:S(2)}) copy-start(bf16[2,272,512]{2,1,0:T(8,128)(2,1)S(1)} %collective-permute-done.2.refs_2_.refs_5_.refs_9_) | copy-start | bytes 1671172
  38.3 20.9 %copy-start.18 = (bf16[2,128,512]{2,1,0:T(8,128)(2,1)S(1)}, bf16[2,128,512]{2,1,0:T(8,128)(2,1)}, u32[]{:S(2)}) copy-start(bf16[2,128,512]{2,1,0:T(8,128)(2,1)} %get-tuple-element.26.refs_3_) | copy-start | bytes 786436
  38.3 16.0 %collective-permute-start.6 = (bf16[2,128,512]{2,1,0:T(8,128)(2,1)}, bf16[2,128,512]{2,1,0:T(8,128)(2,1)S(1)}, u32[]{:S(2)}, u32[]{:S(2)}) collective-permute-start(bf16[2,128,512]{2,1,0:T(8,128)(2,1)} %get-tuple-element.27), channel_id=1, source_target_pairs={{0,2},{1,3},{2,0},{3,1},{4,6},{5,7},{6,4},{7,5},{8,10},{9,11},{10,... | collective-permute-start | bytes 786440 | tf_op jit(solution)/shard_map/ppermute | solution.py:341
  39.5 15.4 %collective-permute-start.7 = (bf16[2,128,512]{2,1,0:T(8,128)(2,1)}, bf16[2,128,512]{2,1,0:T(8,128)(2,1)S(1)}, u32[]{:S(2)}, u32[]{:S(2)}) collective-permute-start(bf16[2,128,512]{2,1,0:T(8,128)(2,1)} %get-tuple-element.28), channel_id=1, source_target_pairs={{0,4},{1,5},{2,6},{3,7},{4,0},{5,1},{6,2},{7,3},{8,12},{9,13},{10,... | collective-permute-start | bytes 786440 | tf_op jit(solution)/shard_map/ppermute | solution.py:341
  39.8 19.4 %collective-permute-start.8 = (bf16[2,128,512]{2,1,0:T(8,128)(2,1)}, bf16[2,128,512]{2,1,0:T(8,128)(2,1)S(1)}, u32[]{:S(2)}, u32[]{:S(2)}) collective-permute-start(bf16[2,128,512]{2,1,0:T(8,128)(2,1)} %get-tuple-element.29), channel_id=1, source_target_pairs={{0,6},{1,7},{2,4},{3,5},{4,2},{5,3},{6,0},{7,1},{8,14},{9,15},{10,... | collective-permute-start | bytes 786440 | tf_op jit(solution)/shard_map/ppermute | solution.py:341
  51.5 21.0 %collective-permute-start.10 = (bf16[4,144,128]{2,1,0:T(8,128)(2,1)S(1)}, bf16[4,144,128]{2,1,0:T(8,128)(2,1)S(1)}, u32[]{:S(2)}, u32[]{:S(2)}) collective-permute-start(bf16[4,144,128]{2,1,0:T(8,128)(2,1)S(1)} %get-tuple-element.32), channel_id=1, source_target_pairs={{0,16},{8,24},{1,17},{9,25},{2,18},{10,26},{3,19},{11,27},{4,20},{... | collective-permute-start | bytes 442376 | tf_op jit(solution)/shard_map/ppermute | solution.py:359
  54.3 18.2 %collective-permute-start.11 = (bf16[4,144,128]{2,1,0:T(8,128)(2,1)S(1)}, bf16[4,144,128]{2,1,0:T(8,128)(2,1)S(1)}, u32[]{:S(2)}, u32[]{:S(2)}) collective-permute-start(bf16[4,144,128]{2,1,0:T(8,128)(2,1)S(1)} %get-tuple-element.32), channel_id=1, source_target_pairs={{0,24},{1,25},{2,26},{3,27},{4,28},{5,29},{6,30},{7,31}} | collective-permute-start | bytes 442376 | tf_op jit(solution)/shard_map/ppermute | solution.py:359
  54.9 17.5 %collective-permute-start.9 = (bf16[4,144,128]{2,1,0:T(8,128)(2,1)S(1)}, bf16[4,144,128]{2,1,0:T(8,128)(2,1)S(1)}, u32[]{:S(2)}, u32[]{:S(2)}) collective-permute-start(bf16[4,144,128]{2,1,0:T(8,128)(2,1)S(1)} %get-tuple-element.32), channel_id=1, source_target_pairs={{0,8},{8,16},{16,24},{1,9},{9,17},{17,25},{2,10},{10,18},{18,26},{... | collective-permute-start | bytes 442376 | tf_op jit(solution)/shard_map/ppermute | solution.py:359
  59.2 1.1 copy-start.7
  60.3 1.0 copy-start.9
  61.3 5.1 %copy-start.11 = (bf16[128,4096]{1,0:T(8,128)(2,1)S(1)}, bf16[128,4096]{1,0:T(8,128)(2,1)}, u32[]{:S(2)}) copy-start(bf16[128,4096]{1,0:T(8,128)(2,1)} %in_ref.3) | copy-start | bytes 3145732
  65.4 1.0 copy-start.12
  67.4 18.7 %all-to-all-start.1 = ((bf16[8,128,512]{2,1,0:T(8,128)(2,1)}), bf16[8,128,512]{2,1,0:T(8,128)(2,1)}, u32[]{:S(2)}, u32[]{:S(2)}) async-start(bf16[8,128,512]{2,1,0:T(8,128)(2,1)} %pieces.3), calls=%async_computation.1 | async-start | bytes 2097152 | tf_op jit(solution)/shard_map/all_to_all | solution.py:356
  72.5 0.7 copy-start.16
  73.1 1.2 copy-start.13
  74.4 0.9 copy-start.17
  78.6 26.5 %collective-permute-start.12 = (bf16[8,128,512]{2,1,0:T(8,128)(2,1)S(1)}, bf16[8,128,512]{2,1,0:T(8,128)(2,1)S(1)}, u32[]{:S(2)}, u32[]{:S(2)}) collective-permute-start(bf16[8,128,512]{2,1,0:T(8,128)(2,1)S(1)} %first.1), channel_id=1, source_target_pairs={{0,8},{8,16},{16,24},{1,9},{9,17},{17,25},{2,10},{10,18},{18,26},{... | collective-permute-start | bytes 3145736 | tf_op jit(solution)/shard_map/ppermute | solution.py:359

commit v3 on v2

--- a/solution.py
+++ b/solution.py
@@ -210,7 +210,7 @@
 
 
 def first_kernel(raw_ref, q_ref, decay_ref, gain_ref, *refs):
-    earlier, out_ref = refs[:-2], refs[-1]
+    earlier, outs = refs[:-3], refs[-2:]
     chunks, length, here = q_ref.shape
     heads, width = gain_ref.shape
     down = summed_down(jnp.log(decay_ref[...]))
@@ -225,13 +225,14 @@
             factor = factor * (parts[0:1, 0:1] + parts[1:2, 0:1] + parts[2:3, 0:1])
         both = jnp.concatenate(halves(carried), 0)
         gain = gain_ref[h : h + 1, :]
+        place = h % (heads // 2)
         for c in range(chunks):
             at = h * chunks + c
             queries = q_ref[c, :, columns]
             outside = dot(jnp.concatenate([queries, queries], 1), both, ((1,), (0,)))
             raw = raw_ref[c, :, columns] + lifts[:, at : at + 1] * outside
             scale = lax.rsqrt(jnp.mean(raw * raw, axis=-1, keepdims=True) + 1e-06)
-            out_ref[c, :, columns] = (raw * scale * gain).astype(BF16)
+            outs[h // (heads // 2)][c, :, place * width : (place + 1) * width] = (raw * scale * gain).astype(BF16)
 
 
 def pick(window_ref, b, source_ref, picked_ref):
@@ -268,25 +269,43 @@
             out_ref[h, t * BLK : (t + 1) * BLK, :] = (probs * share).astype(BF16)
 
 
-def sum_kernel(window_ref, weights_ref, own_ref, earlier_ref, out_ref, values_ref, picked_ref):
+def sum_kernel(order_ref, window_ref, weights_ref, own_ref, earlier_ref, *refs):
+    outs, values_ref, picked_ref = refs[:-2], refs[-2], refs[-1]
     tokens, here = own_ref.shape
-    heads = weights_ref.shape[0]
+    heads, length, _ = weights_ref.shape
     width = here // heads
-    group = pl.program_id(0)
-
-    @pl.when(group == 0)
+    step = pl.program_id(0)
+
+    @pl.when(step == 0)
     def _():
         values_ref[:tokens, :] = earlier_ref[...]
         values_ref[tokens:, :] = own_ref[...]
 
-    for t in range(STEP):
-        b = group * STEP + t
+    results = []
+    for t in range(length // BLK):
+        b = order_ref[step] * (length // BLK) + t
         pick(window_ref, b, values_ref, picked_ref.at[t])
         rows = pl.ds(pl.multiple_of(b * BLK, BLK), BLK)
         for h in range(heads):
             columns = slice(h * width, (h + 1) * width)
             second = dot(weights_ref[h, t * BLK : (t + 1) * BLK, :], picked_ref[t, :, columns], ((1,), (0,)))
-            out_ref[t * BLK : (t + 1) * BLK, columns] = (own_ref[rows, columns].astype(F32) + second).astype(BF16)
+            results.append((t, columns, (own_ref[rows, columns].astype(F32) + second).astype(BF16)))
+    for k, out_ref in enumerate(outs):
+
+        @pl.when(step // 2 == k)
+        def _(out_ref=out_ref):
+            for t, columns, result in results:
+                out_ref[0, t * BLK : (t + 1) * BLK, columns] = result
+
+
+def join_kernel(columns_ref, *refs):
+    parts, out_ref = refs[:-1], refs[-1]
+    here = parts[0].shape[2]
+    chips = columns_ref.shape[0]
+    for n, ref in enumerate(parts):
+        half, k, core = n // (2 * chips), n // 2 % chips, n % 2
+        start = pl.multiple_of(columns_ref[k, core] + half * here, 128)
+        out_ref[:, pl.ds(start, here)] = ref[0]
 
 
 def local(lin_query, lin_key, lin_value, sparse_query, sparse_key, decay, norm_gain, block_pattern):
@@ -404,16 +423,16 @@
         cost_estimate=pl.CostEstimate(flops=2**31, bytes_accessed=6 * 2**20, transcendentals=2**19),
         name="inside",
     )(place, decays, starts, *q_parts, *kv_parts)
-    sparse_queries = exchange(sparse_query, after=(raw,))
-    first = pl.pallas_call(
+    sparse_queries = exchange(sparse_query, after=(raw, *states))
+    firsts = pl.pallas_call(
         first_kernel,
-        out_shape=jax.ShapeDtypeStruct((ways, length, here), BF16),
+        out_shape=[jax.ShapeDtypeStruct((ways, length, here // 2), BF16)] * 2,
         in_specs=[VMEM] * (4 + len(states)) + [ANY],
-        out_specs=VMEM,
+        out_specs=[VMEM] * 2,
         compiler_params=PARAMS,
         name="first",
     )(raw, queries, decays, gain, *states, earlier_keys)
-    earlier_first = onward(first)
+    earlier_firsts = [onward(x) for x in firsts]
 
     steps = blocks // STEP
     rows = STEP * BLK
@@ -440,23 +459,48 @@
         bias,
         sparse_queries.reshape(tokens, here),
     )
-    layer = pl.pallas_call(
-        sum_kernel,
-        out_shape=jax.ShapeDtypeStruct((tokens, here), BF16),
-        grid=(steps,),
-        in_specs=[SMEM, table, whole, whole],
-        out_specs=part,
-        scratch_shapes=[
-            pltpu.VMEM((2 * tokens, here), BF16),
-            pltpu.VMEM((STEP, picks * BLK, here), BF16),
-        ],
+    order = (peers[:, None] * 2 + cores[None, :]).reshape(-1).astype(jnp.int32)
+    some = here // 2
+    whole = pl.BlockSpec((tokens, some), lambda g, *_: (0, 0))
+    sums = []
+    for half, (own, earlier) in enumerate(zip(firsts, earlier_firsts)):
+        outs = pl.pallas_call(
+            sum_kernel,
+            out_shape=[jax.ShapeDtypeStruct((2, length, some), BF16)] * chips,
+            grid_spec=pltpu.PrefetchScalarGridSpec(
+                num_scalar_prefetch=2,
+                grid=(ways,),
+                in_specs=[
+                    pl.BlockSpec((heads // 2, length, picks * BLK), lambda g, order, _, half=half: (half, order[g], 0)),
+                    whole,
+                    whole,
+                ],
+                out_specs=[
+                    pl.BlockSpec((1, length, some), lambda g, *_, k=k: (jnp.clip(g - 2 * k, 0, 1), 0, 0))
+                    for k in range(chips)
+                ],
+                scratch_shapes=[
+                    pltpu.VMEM((2 * tokens, some), BF16),
+                    pltpu.VMEM((length // BLK, picks * BLK, some), BF16),
+                ],
+            ),
+            compiler_params=PARAMS,
+            name="sum",
+        )(order, window, weights, own.reshape(tokens, some), earlier.reshape(tokens, some))
+        for k, out in enumerate(outs):
+            if k:
+                out = lax.ppermute(out, ("side", "inner"), [(i, i ^ (2 * k)) for i in range(ways)])
+            sums += [out, swap(out)]
+    return pl.pallas_call(
+        join_kernel,
+        out_shape=jax.ShapeDtypeStruct((length, model), BF16),
+        grid=(1,),
+        in_specs=[SMEM]
+        + [pl.BlockSpec((1, length, some), lambda g, core=n % 2: (core, 0, 0)) for n in range(len(sums))],
+        out_specs=pl.BlockSpec((length, model), lambda g: (0, 0)),
         compiler_params=PARAMS,
-        name="sum",
-    )(window, weights, first.reshape(tokens, here), earlier_first.reshape(tokens, here))
-    back = lax.all_to_all(
-        layer.reshape(ways, length, here), ("side", "inner"), split_axis=0, concat_axis=0, tiled=True
-    )
-    return back.reshape(2, inner, length, here).transpose(2, 1, 0, 3).reshape(length, model)
+        name="join",
+    )(columns, *sums)
 
 
 def solution(mesh):

time: 132 us -> 127 us (0.962)
  blocking collectives: 18.5 us -> 0 us
  starting transfers between devices: 29.4 us -> 43.9 us
  Pallas kernels: 33.7 us -> 40 us
  waiting for transfers between devices: 36.9 us -> 31.3 us
  local copies, waits for them, and re-layouts: 11.5 us -> 10 us
    all_to_all x1 -> x0, blocking collectives: 18.5 us -> none  [local(): lax.all_to_all(layer.reshape(ways, length, here), ('side', 'inner'), spli...]
    ppermute x2 -> x10, starting transfers between devices: 1.45 us -> 11.5 us  [swap(): return lax.ppermute(x, ('side', 'inner'), [(i, i ^ 1) for i in range(ways)])]
    pallas_call x2 -> x4, Pallas kernels: 7.62 us -> 13.4 us  [the longest x2 7.69 us: local(): pl.pallas_call(sum_kernel, out_shape=[jax.ShapeDtypeStruct((2, length, so...]
    ppermute x0 -> x6, starting transfers between devices: none -> 5.43 us  [local(): lax.ppermute(out, ('side', 'inner'), [(i, i ^ 2 * k) for i in range(ways)])]
    ppermute x5 -> x6, waiting for transfers between devices: 10.6 us -> 5.38 us  [onward(): lax.ppermute(x, 'group', [(i, i + steps) for i in range(groups - steps)])]
    reshape x2 -> x0, local copies, waits for them, and re-layouts: 2.69 us -> none  [local(): back.reshape(2, inner, length, here).transpose(2, 1, 0, 3)]
    all_to_all x2, waiting for transfers between devices: 9.91 us -> 7.65 us  [exchange(): lax.all_to_all(pieces, ('side', 'inner'), split_axis=0, concat_axis=0, ti...]
    ppermute x5 -> x6, starting transfers between devices: 12.2 us -> 13.4 us  [onward(): lax.ppermute(x, 'group', [(i, i + steps) for i in range(groups - steps)])]
  transfers between devices with their start and end apart: 15 -> 30, of which waited for: 8 -> 14; matrix products, arithmetic and copies ran while one was open for 0% -> 0% of each run, Pallas kernels for 21% -> 29%
where the time goes in v3:
time: 127 us; the launch traced here: 126 us
  starting transfers between devices  43.9 us (35%)
  Pallas kernels  40 us (31%)
  waiting for transfers between devices  31.3 us (25%)
  local copies, waits for them, and re-layouts  10 us (8%)
    ppermute x6, waiting for transfers between devices, spread(): lax.ppermute(x, ('side', 'inner'), [(i, i ^ 2 * k) for i in range(ways)])  17.1 us
    ppermute x6, starting transfers between devices, onward(): lax.ppermute(x, 'group', [(i, i + steps) for i in range(groups - steps)])  13.4 us
    ppermute x10, starting transfers between devices, swap(): return lax.ppermute(x, ('side', 'inner'), [(i, i ^ 1) for i in range(ways)])  11.5 us
    unnamed x47, local copies, waits for them, and re-layouts  9.55 us
    all_to_all x2, starting transfers between devices, exchange(): lax.all_to_all(pieces, ('side', 'inner'), split_axis=0, concat_axis=0, ti...  8.31 us
    pallas_call x2, Pallas kernels, local(): pl.pallas_call(sum_kernel, out_shape=[jax.ShapeDtypeStruct((2, length, so...  7.69 us
    pallas_call x1, Pallas kernels, local(): pl.pallas_call(weights_kernel, out_shape=jax.ShapeDtypeStruct((heads, tok...  7.68 us
    all_to_all x2, waiting for transfers between devices, exchange(): lax.all_to_all(pieces, ('side', 'inner'), split_axis=0, concat_axis=0, ti...  7.65 us
  transfers between devices with their start and end apart: 30, of which 14 were waited for; matrix products, arithmetic and copies ran while one was open for 0% of the time, Pallas kernels for 29%

profile of v3, /device:TPU:17, one launch (start us, length us, event | category | flops | bytes accessed | tf_op | source)
XLA Modules:
  0.0 125.9 jit_solution(14118574198434901106)
XLA Ops:
  0.2 1.2 copy-done.1
  1.4 1.2 copy-done.3
  2.6 1.6 %outward.2 = bf16[4,256,512]{2,1,0:T(8,128)(2,1)} custom-call(s32[4,2]{1,0:T(4,128)S(1)} %get-tuple-element.58.columns_ref.refs_0_, bf16[128,4096]{1,0:T(8,128)(2,1)S(1)} %copy-done.1, bf16[128,4096]{1,0:T(8,128)(2,1)S(1)} %copy-done.3), custom_call_target="tpu_custom_call" | custom-call | tf_op jit(solution)/shard_map/outward/pallas_call | solution.py:338
  4.3 0.7 collective-permute-start
  5.0 1.1 pieces.2
  6.1 4.2 %all-to-all-start = ((bf16[8,128,512]{2,1,0:T(8,128)(2,1)}), bf16[8,128,512]{2,1,0:T(8,128)(2,1)}, u32[]{:S(2)}, u32[]{:S(2)}) async-start(bf16[8,128,512]{2,1,0:T(8,128)(2,1)} %pieces.2), calls=%async_computation | async-start | bytes 2097152 | tf_op jit(solution)/shard_map/all_to_all | solution.py:375
  10.6 2.7 %parcels.2 = (bf16[2,256,512]{2,1,0:T(8,128)(2,1)}, bf16[2,256,512]{2,1,0:T(8,128)(2,1)}, bf16[2,272,512]{2,1,0:T(8,128)(2,1)}, bf16[2,256,512]{2,1,0:T(8,128)(2,1)}) custom-call(s32[4,2]{1,0:T(4,128)S(1)} %get-tuple-element.58.columns_ref.refs_0_, s32[3]{0:T(128)S(1)} %pad_add_fusion.1.refs_1_.place_ref.refs_0_, bf16[128,4096]{1,0:T(8,128)(2,1)S(1)} %copy-done.2, ...), custom_call_target="tpu_custom_call" | custom-call | tf_op jit(solution)/shard_map/parcels/pallas_call | solution.py:347
  13.3 1.4 %collective-permute-start.2 = (bf16[2,272,512]{2,1,0:T(8,128)(2,1)}, bf16[2,272,512]{2,1,0:T(8,128)(2,1)S(1)}, u32[]{:S(2)}, u32[]{:S(2)}) collective-permute-start(bf16[2,272,512]{2,1,0:T(8,128)(2,1)} %get-tuple-element.31), channel_id=1, source_target_pairs={{0,4},{1,5},{2,6},{3,7},{4,0},{5,1},{6,2},{7,3},{8,12},{9,13},{10,... | collective-permute-start | bytes 1671176 | tf_op jit(solution)/shard_map/ppermute | solution.py:360
  14.7 1.4 %outward.3 = bf16[4,128,512]{2,1,0:T(8,128)(2,1)} custom-call(s32[4,2]{1,0:T(4,128)S(1)} %get-tuple-element.58.columns_ref.refs_0_, bf16[128,4096]{1,0:T(8,128)(2,1)S(1)} %copy-done.5), custom_call_target="tpu_custom_call" | custom-call | tf_op jit(solution)/shard_map/outward/pallas_call | solution.py:338
  16.1 0.7 collective-permute-start.5
  16.9 1.2 collective-permute-start.1
  18.1 5.9 %all-to-all-done = bf16[8,128,512]{2,1,0:T(8,128)(2,1)} async-done(((bf16[8,128,512]{2,1,0:T(8,128)(2,1)}), bf16[8,128,512]{2,1,0:T(8,128)(2,1)}, u32[]{:S(2)}, u32[]{:S(2)}) %all-to-all-start) | async-done | bytes 1048608 | tf_op jit(solution)/shard_map/all_to_all | solution.py:375
  24.0 3.2 %collective-permute-start.4 = (bf16[8,128,512]{2,1,0:T(8,128)(2,1)}, bf16[8,128,512]{2,1,0:T(8,128)(2,1)}, u32[]{:S(2)}, u32[]{:S(2)}) collective-permute-start(bf16[8,128,512]{2,1,0:T(8,128)(2,1)} %all-to-all-done), channel_id=1, source_target_pairs={{0,8},{8,16},{16,24},{1,9},{9,17},{17,25},{2,10},{10,18},{18,26},{... | collective-permute-start | bytes 3145736 | tf_op jit(solution)/shard_map/ppermute | solution.py:378
  27.2 8.0 %collective-permute-done.1.refs_1_.refs_4_.refs_8_ = bf16[2,256,512]{2,1,0:T(8,128)(2,1)S(1)} collective-permute-done((bf16[2,256,512]{2,1,0:T(8,128)(2,1)}, bf16[2,256,512]{2,1,0:T(8,128)(2,1)S(1)}, u32[]{:S(2)}, u32[]{:S(2)}) %collective-permute-start.1) | collective-permute-done | bytes 524320 | tf_op jit(solution)/shard_map/ppermute | solution.py:360
  35.2 0.7 collective-permute-done.2.refs_2_.refs_5_.refs_9_
  35.9 2.4 %parcels.3 = (bf16[2,128,512]{2,1,0:T(8,128)(2,1)}, bf16[2,128,512]{2,1,0:T(8,128)(2,1)}, bf16[2,128,512]{2,1,0:T(8,128)(2,1)}, bf16[2,128,512]{2,1,0:T(8,128)(2,1)}) custom-call(s32[4,2]{1,0:T(4,128)S(1)} %get-tuple-element.58.columns_ref.refs_0_, s32[3]{0:T(128)S(1)} %pad_add_fusion.1.refs_1_.place_ref.refs_0_, bf16[128,4096]{1,0:T(8,128)(2,1)S(1)} %copy-done.5, ...), custom_call_target="tpu_custom_call" | custom-call | tf_op jit(solution)/shard_map/parcels/pallas_call | solution.py:347
  38.3 1.3 %collective-permute-start.6 = (bf16[2,128,512]{2,1,0:T(8,128)(2,1)}, bf16[2,128,512]{2,1,0:T(8,128)(2,1)S(1)}, u32[]{:S(2)}, u32[]{:S(2)}) collective-permute-start(bf16[2,128,512]{2,1,0:T(8,128)(2,1)} %get-tuple-element.37), channel_id=1, source_target_pairs={{0,2},{1,3},{2,0},{3,1},{4,6},{5,7},{6,4},{7,5},{8,10},{9,11},{10,... | collective-permute-start | bytes 786440 | tf_op jit(solution)/shard_map/ppermute | solution.py:360
  39.6 0.3 collective-permute-start.7
  39.8 1.2 collective-permute-start.8
  41.0 7.1 %collective-permute-done.3.refs_3_.refs_10_ = bf16[2,256,512]{2,1,0:T(8,128)(2,1)} collective-permute-done((bf16[2,256,512]{2,1,0:T(8,128)(2,1)}, bf16[2,256,512]{2,1,0:T(8,128)(2,1)}, u32[]{:S(2)}, u32[]{:S(2)}) %collective-permute-start.3) | collective-permute-done | bytes 524320 | tf_op jit(solution)/shard_map/ppermute | solution.py:360
  48.1 4.0 %state.1 = (bf16[4,144,128]{2,1,0:T(8,128)(2,1)S(1)}, bf16[4,8,256,128]{3,2,1,0:T(8,128)(2,1)S(1)}, f32[32,128]{1,0:T(8,128)S(1)}, f32[2,1,512]{2,1,0:T(1,128)S(1)}) custom-call(s32[3]{0:T(128)S(1)} %pad_add_fusion.1.refs_1_.place_ref.refs_0_, f32[5,512]{1,0:T(8,128)S(1)} %get-tuple-element.56.table_ref, bf16[2,256,512]{2,1,0:T(8,128)(2,1)S(1)} %copy-done.16, ...), custom_call_target="tpu_custom_call" | custom-call | tf_op jit(solution)/shard_map/state/pallas_call | solution.py:395
  52.1 1.3 %collective-permute-start.10 = (bf16[4,144,128]{2,1,0:T(8,128)(2,1)S(1)}, bf16[4,144,128]{2,1,0:T(8,128)(2,1)S(1)}, u32[]{:S(2)}, u32[]{:S(2)}) collective-permute-start(bf16[4,144,128]{2,1,0:T(8,128)(2,1)S(1)} %get-tuple-element.41), channel_id=1, source_target_pairs={{0,16},{8,24},{1,17},{9,25},{2,18},{10,26},{3,19},{11,27},{4,20},{... | collective-permute-start | bytes 442376 | tf_op jit(solution)/shard_map/ppermute | solution.py:378
  53.4 0.8 collective-permute-done.6.refs_4_
  54.3 0.7 collective-permute-start.11
  55.0 3.8 %collective-permute-start.9 = (bf16[4,144,128]{2,1,0:T(8,128)(2,1)S(1)}, bf16[4,144,128]{2,1,0:T(8,128)(2,1)S(1)}, u32[]{:S(2)}, u32[]{:S(2)}) collective-permute-start(bf16[4,144,128]{2,1,0:T(8,128)(2,1)S(1)} %get-tuple-element.41), channel_id=1, source_target_pairs={{0,8},{8,16},{16,24},{1,9},{9,17},{17,25},{2,10},{10,18},{18,26},{... | collective-permute-start | bytes 442376 | tf_op jit(solution)/shard_map/ppermute | solution.py:378
  58.8 0.4 collective-permute-done.8.refs_6_
  59.2 1.1 copy-done.7
  60.3 1.0 copy-done.9
  61.3 1.0 copy-done.17
  62.4 4.7 %inside.1 = (f32[8,128,512]{2,1,0:T(8,128)S(1)}, bf16[8,128,512]{2,1,0:T(8,128)(2,1)S(1)}) custom-call(s32[3]{0:T(128)S(1)} %pad_add_fusion.1.refs_1_.place_ref.refs_0_, f32[32,128]{1,0:T(8,128)S(1)} %get-tuple-element.34.refs_1_.decay_ref, bf16[4,8,256,128]{3,2,1,0:T(8,128)(2,1)S(1)} %get-tuple-element.35.refs_2_, bf16[2,128,512]{2,1,0:T(8,128)(2,1)S(1)} %copy-done.20, ...), custom_call_target="tpu_custom_call" | custom-call | flops 2147483648 | bytes 6291456 | tf_op jit(solution)/shard_map/inside/pallas_call | solution.py:413
  67.1 1.0 copy-done.12
  68.1 2.0 %collective-permute-done.9.refs_1_.refs_0_ = bf16[4,144,128]{2,1,0:T(8,128)(2,1)S(1)} collective-permute-done((bf16[4,144,128]{2,1,0:T(8,128)(2,1)S(1)}, bf16[4,144,128]{2,1,0:T(8,128)(2,1)S(1)}, u32[]{:S(2)}, u32[]{:S(2)}) %collective-permute-start.9) | collective-permute-done | bytes 147488 | tf_op jit(solution)/shard_map/ppermute | solution.py:378
  70.1 1.1 pieces.3
  71.2 4.1 %all-to-all-start.1 = ((bf16[8,128,512]{2,1,0:T(8,128)(2,1)}), bf16[8,128,512]{2,1,0:T(8,128)(2,1)S(1)}, u32[]{:S(2)}, u32[]{:S(2)}) async-start(bf16[8,128,512]{2,1,0:T(8,128)(2,1)} %pieces.3), calls=%async_computation.1 | async-start | bytes 2097152 | tf_op jit(solution)/shard_map/all_to_all | solution.py:375
  75.4 1.2 copy-done.13
  76.6 0.9 copy-done.15
  77.5 4.1 %first.1 = (bf16[8,128,256]{2,1,0:T(8,128)(2,1)S(1)}, bf16[8,128,256]{2,1,0:T(8,128)(2,1)}) custom-call(f32[8,128,512]{2,1,0:T(8,128)S(1)} %get-tuple-element.40.refs_0_.raw_ref, bf16[8,128,512]{2,1,0:T(8,128)(2,1)S(1)} %copy-done.13, f32[32,128]{1,0:T(8,128)S(1)} %get-tuple-element.34.refs_1_.decay_ref, f32[4,128]{1,0:T(4,128)S(1)} %constant_dynamic-slice_fusion.gain_ref, ...), custom_call_target="tpu_custom_call" | custom-call | tf_op jit(solution)/shard_map/first/pallas_call | solution.py:427
  81.6 0.8 copy-done.18
  82.4 2.3 %collective-permute-start.20 = (bf16[8,128,256]{2,1,0:T(8,128)(2,1)}, bf16[8,128,256]{2,1,0:T(8,128)(2,1)S(1)}, u32[]{:S(2)}, u32[]{:S(2)}) collective-permute-start(bf16[8,128,256]{2,1,0:T(8,128)(2,1)} %get-tuple-element.48), channel_id=1, source_target_pairs={{0,8},{8,16},{16,24},{1,9},{9,17},{17,25},{2,10},{10,18},{18,26},{... | collective-permute-start | bytes 1572872 | tf_op jit(solution)/shard_map/ppermute | solution.py:378
  84.9 0.1 reshape.98.bias_ref
  84.9 2.1 %collective-permute-start.12 = (bf16[8,128,256]{2,1,0:T(8,128)(2,1)}, bf16[8,128,256]{2,1,0:T(8,128)(2,1)S(1)}, u32[]{:S(2)}, u32[]{:S(2)}) collective-permute-start(bf16[8,128,256]{2,1,0:T(8,128)(2,1)} %copy-done.18), channel_id=1, source_target_pairs={{0,8},{8,16},{16,24},{1,9},{9,17},{17,25},{2,10},{10,18},{18,26},{... | collective-permute-start | bytes 1572872 | tf_op jit(solution)/shard_map/ppermute | solution.py:378
  87.1 1.8 %all-to-all-done.1 = bf16[8,128,512]{2,1,0:T(8,128)(2,1)S(1)} async-done(((bf16[8,128,512]{2,1,0:T(8,128)(2,1)}), bf16[8,128,512]{2,1,0:T(8,128)(2,1)S(1)}, u32[]{:S(2)}, u32[]{:S(2)}) %all-to-all-start.1) | async-done | bytes 1048608 | tf_op jit(solution)/shard_map/all_to_all | solution.py:375
  88.9 7.7 %weights.1.weights_ref = bf16[4,1024,512]{2,1,0:T(8,128)(2,1)S(1)} custom-call(s32[16,8]{1,0:T(8,128)S(1)} %select_n.57.window_ref, bf16[1024,512]{1,0:T(8,128)(2,1)} %bitcast.4.own_ref, bf16[1024,512]{1,0:T(8,128)(2,1)} %bitcast.5.earlier_ref, f32[16,512]{1,0:T(8,128)S(1)} %reshape.98.bias_ref, bf16[1024,512]{1,0:T(8,128)(2,1)S(1)} %bitcast.14), custom_call_target="tpu_custom_call" | custom-call | flops 2147483648 | bytes 8388608 | tf_op jit(solution)/shard_map/weights/pallas_call | solution.py:442
  96.6 1.4 %collective-permute-done.20 = bf16[8,128,256]{2,1,0:T(8,128)(2,1)S(1)} collective-permute-done((bf16[8,128,256]{2,1,0:T(8,128)(2,1)}, bf16[8,128,256]{2,1,0:T(8,128)(2,1)S(1)}, u32[]{:S(2)}, u32[]{:S(2)}) %collective-permute-start.20) | collective-permute-done | bytes 524320 | tf_op jit(solution)/shard_map/ppermute | solution.py:378
  98.0 4.4 %sum.3 = (bf16[2,128,256]{2,1,0:T(8,128)(2,1)S(1)}, bf16[2,128,256]{2,1,0:T(8,128)(2,1)S(1)}, bf16[2,128,256]{2,1,0:T(8,128)(2,1)S(1)}, bf16[2,128,256]{2,1,0:T(8,128)(2,1)S(1)}) custom-call(s32[8]{0:T(128)S(1)} %add.79.order_ref, s32[16,8]{1,0:T(8,128)S(1)} %select_n.57.window_ref, bf16[4,1024,512]{2,1,0:T(8,128)(2,1)S(1)} %weights.1.weights_ref, ...), custom_call_target="tpu_custom_call" | custom-call | tf_op jit(solution)/shard_map/sum/pallas_call | solution.py:467
  102.3 1.1 collective-permute-start.22
  103.4 1.2 collective-permute-start.24
  104.7 0.4 collective-permute-start.26
  105.1 2.2 %collective-permute-start.21 = (bf16[2,128,256]{2,1,0:T(8,128)(2,1)S(1)}, bf16[2,128,256]{2,1,0:T(8,128)(2,1)S(1)}, u32[]{:S(2)}, u32[]{:S(2)}) collective-permute-start(bf16[2,128,256]{2,1,0:T(8,128)(2,1)S(1)} %get-tuple-element.49.refs_8_), channel_id=1, source_target_pairs={{0,1},{1,0},{2,3},{3,2},{4,5},{5,4},{6,7},{7,6},{8,9},{9,8},{10,11... | collective-permute-start | bytes 393224 | tf_op jit(solution)/shard_map/ppermute | solution.py:332
  107.2 2.0 %collective-permute-done.12 = bf16[8,128,256]{2,1,0:T(8,128)(2,1)S(1)} collective-permute-done((bf16[8,128,256]{2,1,0:T(8,128)(2,1)}, bf16[8,128,256]{2,1,0:T(8,128)(2,1)S(1)}, u32[]{:S(2)}, u32[]{:S(2)}) %collective-permute-start.12) | collective-permute-done | bytes 524320 | tf_op jit(solution)/shard_map/ppermute | solution.py:378
  109.2 3.3 %sum.2 = (bf16[2,128,256]{2,1,0:T(8,128)(2,1)S(1)}, bf16[2,128,256]{2,1,0:T(8,128)(2,1)S(1)}, bf16[2,128,256]{2,1,0:T(8,128)(2,1)S(1)}, bf16[2,128,256]{2,1,0:T(8,128)(2,1)S(1)}) custom-call(s32[8]{0:T(128)S(1)} %add.79.order_ref, s32[16,8]{1,0:T(8,128)S(1)} %select_n.57.window_ref, bf16[4,1024,512]{2,1,0:T(8,128)(2,1)S(1)} %weights.1.weights_ref, ...), custom_call_target="tpu_custom_call" | custom-call | tf_op jit(solution)/shard_map/sum/pallas_call | solution.py:467
  112.5 1.1 collective-permute-start.14
  113.7 1.2 collective-permute-start.16
  114.9 0.4 collective-permute-start.18
  115.3 1.7 %collective-permute-start.13 = (bf16[2,128,256]{2,1,0:T(8,128)(2,1)S(1)}, bf16[2,128,256]{2,1,0:T(8,128)(2,1)S(1)}, u32[]{:S(2)}, u32[]{:S(2)}) collective-permute-start(bf16[2,128,256]{2,1,0:T(8,128)(2,1)S(1)} %get-tuple-element.44.refs_0_), channel_id=1, source_target_pairs={{0,1},{1,0},{2,3},{3,2},{4,5},{5,4},{6,7},{7,6},{8,9},{9,8},{10,11... | collective-permute-start | bytes 393224 | tf_op jit(solution)/shard_map/ppermute | solution.py:332
  117.1 1.5 %collective-permute-start.25 = (bf16[2,128,256]{2,1,0:T(8,128)(2,1)S(1)}, bf16[2,128,256]{2,1,0:T(8,128)(2,1)S(1)}, u32[]{:S(2)}, u32[]{:S(2)}) collective-permute-start(bf16[2,128,256]{2,1,0:T(8,128)(2,1)S(1)} %collective-permute-done.24.refs_12_), channel_id=1, source_target_pairs={{0,1},{1,0},{2,3},{3,2},{4,5},{5,4},{6,7},{7,6},{8,9},{9,8},{10,11... | collective-permute-start | bytes 393224 | tf_op jit(solution)/shard_map/ppermute | solution.py:332
  118.5 2.4 %collective-permute-start.27 = (bf16[2,128,256]{2,1,0:T(8,128)(2,1)S(1)}, bf16[2,128,256]{2,1,0:T(8,128)(2,1)S(1)}, u32[]{:S(2)}, u32[]{:S(2)}) collective-permute-start(bf16[2,128,256]{2,1,0:T(8,128)(2,1)S(1)} %collective-permute-done.26.refs_14_), channel_id=1, source_target_pairs={{0,1},{1,0},{2,3},{3,2},{4,5},{5,4},{6,7},{7,6},{8,9},{9,8},{10,11... | collective-permute-start | bytes 393224 | tf_op jit(solution)/shard_map/ppermute | solution.py:332
  121.0 0.1 collective-permute-done.18.refs_6_
  121.1 1.6 %collective-permute-start.15 = (bf16[2,128,256]{2,1,0:T(8,128)(2,1)S(1)}, bf16[2,128,256]{2,1,0:T(8,128)(2,1)S(1)}, u32[]{:S(2)}, u32[]{:S(2)}) collective-permute-start(bf16[2,128,256]{2,1,0:T(8,128)(2,1)S(1)} %collective-permute-done.14.refs_2_), channel_id=1, source_target_pairs={{0,1},{1,0},{2,3},{3,2},{4,5},{5,4},{6,7},{7,6},{8,9},{9,8},{10,11... | collective-permute-start | bytes 393224 | tf_op jit(solution)/shard_map/ppermute | solution.py:332
  122.7 0.5 collective-permute-start.19
  123.3 0.5 collective-permute-done.15.refs_3_
  123.7 0.4 collective-permute-done.17.refs_5_
  124.1 0.2 collective-permute-done.19.refs_7_
  124.3 1.7 %join.1 = bf16[128,4096]{1,0:T(8,128)(2,1)} custom-call(s32[4,2]{1,0:T(4,128)S(1)} %get-tuple-element.58.columns_ref.refs_0_, bf16[2,128,256]{2,1,0:T(8,128)(2,1)S(1)} %get-tuple-element.44.refs_0_, bf16[2,128,256]{2,1,0:T(8,128)(2,1)S(1)} %collective-permute-done.13.refs_1_, bf16[2,128,256]{2,1,0:T(8,128)(2,1)S(1)} %collective-permute-done.14.refs_2_, ...), custom_call_target="tpu_custom_call" | custom-call | tf_op jit(solution)/shard_map/join/pallas_call | solution.py:494
  (73 shorter events, 0.9 us)
Async XLA Ops:
  0.0 75.4 %copy-start = (f32[8,128]{1,0:T(8,128)S(1)}, f32[8,128]{1,0:T(8,128)}, u32[]{:S(2)}) copy-start(f32[8,128]{1,0:T(8,128)} %param.14) | copy-start | bytes 12292
  0.2 1.2 copy-start.1
  1.4 1.2 copy-start.3
  2.6 2.4 %copy-start.10 = (bf16[128,4096]{1,0:T(8,128)(2,1)S(1)}, bf16[128,4096]{1,0:T(8,128)(2,1)}, u32[]{:S(2)}) copy-start(bf16[128,4096]{1,0:T(8,128)(2,1)} %in_ref.2) | copy-start | bytes 3145732
  4.2 6.1 %copy-start.22 = (s32[8,8]{1,0:T(8,128)S(1)}, s32[8,8]{1,0:T(8,128)}, u32[]{:S(2)}) copy-start(s32[8,8]{1,0:T(8,128)} %param.15) | copy-start | bytes 772
  4.3 6.3 %copy-start.21 = (f32[8,512]{1,0:T(8,128)S(1)}, f32[8,512]{1,0:T(8,128)}, u32[]{:S(2)}) copy-start(f32[8,512]{1,0:T(8,128)} %param.13) | copy-start | bytes 49156
  4.3 6.3 %copy-start.2 = (bf16[128,4096]{1,0:T(8,128)(2,1)S(1)}, bf16[128,4096]{1,0:T(8,128)(2,1)}, u32[]{:S(2)}) copy-start(bf16[128,4096]{1,0:T(8,128)(2,1)} %refs_2_.2) | copy-start | bytes 3145732
  4.3 6.3 %copy-start.4 = (bf16[128,4096]{1,0:T(8,128)(2,1)S(1)}, bf16[128,4096]{1,0:T(8,128)(2,1)}, u32[]{:S(2)}) copy-start(bf16[128,4096]{1,0:T(8,128)(2,1)} %refs_3_.1) | copy-start | bytes 3145732
  4.3 6.3 %collective-permute-start = (bf16[4,256,512]{2,1,0:T(8,128)(2,1)}, bf16[4,256,512]{2,1,0:T(8,128)(2,1)}, u32[]{:S(2)}, u32[]{:S(2)}) collective-permute-start(bf16[4,256,512]{2,1,0:T(8,128)(2,1)} %outward.2), channel_id=1, source_target_pairs={{0,1},{1,0},{2,3},{3,2},{4,5},{5,4},{6,7},{7,6},{8,9},{9,8},{10,11... | collective-permute-start | bytes 3145736 | tf_op jit(solution)/shard_map/ppermute | solution.py:332
  6.1 17.9 %all-to-all-start = ((bf16[8,128,512]{2,1,0:T(8,128)(2,1)}), bf16[8,128,512]{2,1,0:T(8,128)(2,1)}, u32[]{:S(2)}, u32[]{:S(2)}) async-start(bf16[8,128,512]{2,1,0:T(8,128)(2,1)} %pieces.2), calls=%async_computation | async-start | bytes 2097152 | tf_op jit(solution)/shard_map/all_to_all | solution.py:375
  10.3 4.4 %copy-start.5 = (bf16[128,4096]{1,0:T(8,128)(2,1)S(1)}, bf16[128,4096]{1,0:T(8,128)(2,1)}, u32[]{:S(2)}) copy-start(bf16[128,4096]{1,0:T(8,128)(2,1)} %refs_2_.3) | copy-start | bytes 3145732
  13.3 34.8 %copy-start.16 = (bf16[2,256,512]{2,1,0:T(8,128)(2,1)S(1)}, bf16[2,256,512]{2,1,0:T(8,128)(2,1)}, u32[]{:S(2)}) copy-start(bf16[2,256,512]{2,1,0:T(8,128)(2,1)} %get-tuple-element.29.refs_0_.refs_7_) | copy-start | bytes 1572868
  13.3 22.6 %collective-permute-start.2 = (bf16[2,272,512]{2,1,0:T(8,128)(2,1)}, bf16[2,272,512]{2,1,0:T(8,128)(2,1)S(1)}, u32[]{:S(2)}, u32[]{:S(2)}) collective-permute-start(bf16[2,272,512]{2,1,0:T(8,128)(2,1)} %get-tuple-element.31), channel_id=1, source_target_pairs={{0,4},{1,5},{2,6},{3,7},{4,0},{5,1},{6,2},{7,3},{8,12},{9,13},{10,... | collective-permute-start | bytes 1671176 | tf_op jit(solution)/shard_map/ppermute | solution.py:360
  16.1 11.0 %collective-permute-start.5 = (bf16[4,128,512]{2,1,0:T(8,128)(2,1)}, bf16[4,128,512]{2,1,0:T(8,128)(2,1)}, u32[]{:S(2)}, u32[]{:S(2)}) collective-permute-start(bf16[4,128,512]{2,1,0:T(8,128)(2,1)} %outward.3), channel_id=1, source_target_pairs={{0,1},{1,0},{2,3},{3,2},{4,5},{5,4},{6,7},{7,6},{8,9},{9,8},{10,11... | collective-permute-start | bytes 1572872 | tf_op jit(solution)/shard_map/ppermute | solution.py:332
  16.9 18.3 %collective-permute-start.1 = (bf16[2,256,512]{2,1,0:T(8,128)(2,1)}, bf16[2,256,512]{2,1,0:T(8,128)(2,1)S(1)}, u32[]{:S(2)}, u32[]{:S(2)}) collective-permute-start(bf16[2,256,512]{2,1,0:T(8,128)(2,1)} %get-tuple-element.30), channel_id=1, source_target_pairs={{0,2},{1,3},{2,0},{3,1},{4,6},{5,7},{6,4},{7,5},{8,10},{9,11},{10,... | collective-permute-start | bytes 1572872 | tf_op jit(solution)/shard_map/ppermute | solution.py:360
  18.1 30.0 %collective-permute-start.3 = (bf16[2,256,512]{2,1,0:T(8,128)(2,1)}, bf16[2,256,512]{2,1,0:T(8,128)(2,1)}, u32[]{:S(2)}, u32[]{:S(2)}) collective-permute-start(bf16[2,256,512]{2,1,0:T(8,128)(2,1)} %get-tuple-element.32), channel_id=1, source_target_pairs={{0,6},{1,7},{2,4},{3,5},{4,2},{5,3},{6,0},{7,1},{8,14},{9,15},{10,... | collective-permute-start | bytes 1572872 | tf_op jit(solution)/shard_map/ppermute | solution.py:360
  24.0 51.4 %collective-permute-start.4 = (bf16[8,128,512]{2,1,0:T(8,128)(2,1)}, bf16[8,128,512]{2,1,0:T(8,128)(2,1)}, u32[]{:S(2)}, u32[]{:S(2)}) collective-permute-start(bf16[8,128,512]{2,1,0:T(8,128)(2,1)} %all-to-all-done), channel_id=1, source_target_pairs={{0,8},{8,16},{16,24},{1,9},{9,17},{17,25},{2,10},{10,18},{18,26},{... | collective-permute-start | bytes 3145736 | tf_op jit(solution)/shard_map/ppermute | solution.py:378
  35.2 16.9 %copy-start.8 = (bf16[2,256,512]{2,1,0:T(8,128)(2,1)}, bf16[2,256,512]{2,1,0:T(8,128)(2,1)S(1)}, u32[]{:S(2)}) copy-start(bf16[2,256,512]{2,1,0:T(8,128)(2,1)S(1)} %collective-permute-done.1.refs_1_.refs_4_.refs_8_) | copy-start | bytes 1572868
  35.9 16.2 %copy-start.6 = (bf16[2,272,512]{2,1,0:T(8,128)(2,1)}, bf16[2,272,512]{2,1,0:T(8,128)(2,1)S(1)}, u32[]{:S(2)}) copy-start(bf16[2,272,512]{2,1,0:T(8,128)(2,1)S(1)} %collective-permute-done.2.refs_2_.refs_5_.refs_9_) | copy-start | bytes 1671172
  38.3 20.9 %copy-start.20 = (bf16[2,128,512]{2,1,0:T(8,128)(2,1)S(1)}, bf16[2,128,512]{2,1,0:T(8,128)(2,1)}, u32[]{:S(2)}) copy-start(bf16[2,128,512]{2,1,0:T(8,128)(2,1)} %get-tuple-element.36.refs_3_) | copy-start | bytes 786436
  38.3 16.0 %collective-permute-start.6 = (bf16[2,128,512]{2,1,0:T(8,128)(2,1)}, bf16[2,128,512]{2,1,0:T(8,128)(2,1)S(1)}, u32[]{:S(2)}, u32[]{:S(2)}) collective-permute-start(bf16[2,128,512]{2,1,0:T(8,128)(2,1)} %get-tuple-element.37), channel_id=1, source_target_pairs={{0,2},{1,3},{2,0},{3,1},{4,6},{5,7},{6,4},{7,5},{8,10},{9,11},{10,... | collective-permute-start | bytes 786440 | tf_op jit(solution)/shard_map/ppermute | solution.py:360
  39.6 15.4 %collective-permute-start.7 = (bf16[2,128,512]{2,1,0:T(8,128)(2,1)}, bf16[2,128,512]{2,1,0:T(8,128)(2,1)S(1)}, u32[]{:S(2)}, u32[]{:S(2)}) collective-permute-start(bf16[2,128,512]{2,1,0:T(8,128)(2,1)} %get-tuple-element.38), channel_id=1, source_target_pairs={{0,4},{1,5},{2,6},{3,7},{4,0},{5,1},{6,2},{7,3},{8,12},{9,13},{10,... | collective-permute-start | bytes 786440 | tf_op jit(solution)/shard_map/ppermute | solution.py:360
  39.8 19.4 %collective-permute-start.8 = (bf16[2,128,512]{2,1,0:T(8,128)(2,1)}, bf16[2,128,512]{2,1,0:T(8,128)(2,1)S(1)}, u32[]{:S(2)}, u32[]{:S(2)}) collective-permute-start(bf16[2,128,512]{2,1,0:T(8,128)(2,1)} %get-tuple-element.39), channel_id=1, source_target_pairs={{0,6},{1,7},{2,4},{3,5},{4,2},{5,3},{6,0},{7,1},{8,14},{9,15},{10,... | collective-permute-start | bytes 786440 | tf_op jit(solution)/shard_map/ppermute | solution.py:360
  52.1 15.9 %collective-permute-start.10 = (bf16[4,144,128]{2,1,0:T(8,128)(2,1)S(1)}, bf16[4,144,128]{2,1,0:T(8,128)(2,1)S(1)}, u32[]{:S(2)}, u32[]{:S(2)}) collective-permute-start(bf16[4,144,128]{2,1,0:T(8,128)(2,1)S(1)} %get-tuple-element.41), channel_id=1, source_target_pairs={{0,16},{8,24},{1,17},{9,25},{2,18},{10,26},{3,19},{11,27},{4,20},{... | collective-permute-start | bytes 442376 | tf_op jit(solution)/shard_map/ppermute | solution.py:378
  54.3 13.8 %collective-permute-start.11 = (bf16[4,144,128]{2,1,0:T(8,128)(2,1)S(1)}, bf16[4,144,128]{2,1,0:T(8,128)(2,1)S(1)}, u32[]{:S(2)}, u32[]{:S(2)}) collective-permute-start(bf16[4,144,128]{2,1,0:T(8,128)(2,1)S(1)} %get-tuple-element.41), channel_id=1, source_target_pairs={{0,24},{1,25},{2,26},{3,27},{4,28},{5,29},{6,30},{7,31}} | collective-permute-start | bytes 442376 | tf_op jit(solution)/shard_map/ppermute | solution.py:378
  55.0 15.1 %collective-permute-start.9 = (bf16[4,144,128]{2,1,0:T(8,128)(2,1)S(1)}, bf16[4,144,128]{2,1,0:T(8,128)(2,1)S(1)}, u32[]{:S(2)}, u32[]{:S(2)}) collective-permute-start(bf16[4,144,128]{2,1,0:T(8,128)(2,1)S(1)} %get-tuple-element.41), channel_id=1, source_target_pairs={{0,8},{8,16},{16,24},{1,9},{9,17},{17,25},{2,10},{10,18},{18,26},{... | collective-permute-start | bytes 442376 | tf_op jit(solution)/shard_map/ppermute | solution.py:378
  59.2 1.1 copy-start.7
  60.3 1.0 copy-start.9
  61.3 1.0 copy-start.17
  62.4 7.7 %copy-start.11 = (bf16[128,4096]{1,0:T(8,128)(2,1)S(1)}, bf16[128,4096]{1,0:T(8,128)(2,1)}, u32[]{:S(2)}) copy-start(bf16[128,4096]{1,0:T(8,128)(2,1)} %in_ref.3) | copy-start | bytes 3145732
  67.1 1.0 copy-start.12
  70.1 1.1 copy-start.14
  71.2 17.7 %all-to-all-start.1 = ((bf16[8,128,512]{2,1,0:T(8,128)(2,1)}), bf16[8,128,512]{2,1,0:T(8,128)(2,1)S(1)}, u32[]{:S(2)}, u32[]{:S(2)}) async-start(bf16[8,128,512]{2,1,0:T(8,128)(2,1)} %pieces.3), calls=%async_computation.1 | async-start | bytes 2097152 | tf_op jit(solution)/shard_map/all_to_all | solution.py:375
  75.4 1.2 copy-start.13
  76.6 0.9 copy-start.15
  81.6 0.8 copy-start.18
  82.4 15.6 %collective-permute-start.20 = (bf16[8,128,256]{2,1,0:T(8,128)(2,1)}, bf16[8,128,256]{2,1,0:T(8,128)(2,1)S(1)}, u32[]{:S(2)}, u32[]{:S(2)}) collective-permute-start(bf16[8,128,256]{2,1,0:T(8,128)(2,1)} %get-tuple-element.48), channel_id=1, source_target_pairs={{0,8},{8,16},{16,24},{1,9},{9,17},{17,25},{2,10},{10,18},{18,26},{... | collective-permute-start | bytes 1572872 | tf_op jit(solution)/shard_map/ppermute | solution.py:378
  84.9 24.3 %collective-permute-start.12 = (bf16[8,128,256]{2,1,0:T(8,128)(2,1)}, bf16[8,128,256]{2,1,0:T(8,128)(2,1)S(1)}, u32[]{:S(2)}, u32[]{:S(2)}) collective-permute-start(bf16[8,128,256]{2,1,0:T(8,128)(2,1)} %copy-done.18), channel_id=1, source_target_pairs={{0,8},{8,16},{16,24},{1,9},{9,17},{17,25},{2,10},{10,18},{18,26},{... | collective-permute-start | bytes 1572872 | tf_op jit(solution)/shard_map/ppermute | solution.py:378
  98.0 11.2 %copy-start.19 = (bf16[8,128,256]{2,1,0:T(8,128)(2,1)S(1)}, bf16[8,128,256]{2,1,0:T(8,128)(2,1)}, u32[]{:S(2)}) copy-start(bf16[8,128,256]{2,1,0:T(8,128)(2,1)} %copy-done.18) | copy-start | bytes 1572868
  102.3 11.3 %collective-permute-start.22 = (bf16[2,128,256]{2,1,0:T(8,128)(2,1)S(1)}, bf16[2,128,256]{2,1,0:T(8,128)(2,1)S(1)}, u32[]{:S(2)}, u32[]{:S(2)}) collective-permute-start(bf16[2,128,256]{2,1,0:T(8,128)(2,1)S(1)} %get-tuple-element.50), channel_id=1, source_target_pairs={{0,2},{1,3},{2,0},{3,1},{4,6},{5,7},{6,4},{7,5},{8,10},{9,11},{10,... | collective-permute-start | bytes 393224 | tf_op jit(solution)/shard_map/ppermute | solution.py:492
  103.4 11.4 %collective-permute-start.24 = (bf16[2,128,256]{2,1,0:T(8,128)(2,1)S(1)}, bf16[2,128,256]{2,1,0:T(8,128)(2,1)S(1)}, u32[]{:S(2)}, u32[]{:S(2)}) collective-permute-start(bf16[2,128,256]{2,1,0:T(8,128)(2,1)S(1)} %get-tuple-element.51), channel_id=1, source_target_pairs={{0,4},{1,5},{2,6},{3,7},{4,0},{5,1},{6,2},{7,3},{8,12},{9,13},{10,... | collective-permute-start | bytes 393224 | tf_op jit(solution)/shard_map/ppermute | solution.py:492
  104.7 10.6 %collective-permute-start.26 = (bf16[2,128,256]{2,1,0:T(8,128)(2,1)S(1)}, bf16[2,128,256]{2,1,0:T(8,128)(2,1)S(1)}, u32[]{:S(2)}, u32[]{:S(2)}) collective-permute-start(bf16[2,128,256]{2,1,0:T(8,128)(2,1)S(1)} %get-tuple-element.52), channel_id=1, source_target_pairs={{0,6},{1,7},{2,4},{3,5},{4,2},{5,3},{6,0},{7,1},{8,14},{9,15},{10,... | collective-permute-start | bytes 393224 | tf_op jit(solution)/shard_map/ppermute | solution.py:492
  105.1 11.9 %collective-permute-start.21 = (bf16[2,128,256]{2,1,0:T(8,128)(2,1)S(1)}, bf16[2,128,256]{2,1,0:T(8,128)(2,1)S(1)}, u32[]{:S(2)}, u32[]{:S(2)}) collective-permute-start(bf16[2,128,256]{2,1,0:T(8,128)(2,1)S(1)} %get-tuple-element.49.refs_8_), channel_id=1, source_target_pairs={{0,1},{1,0},{2,3},{3,2},{4,5},{5,4},{6,7},{7,6},{8,9},{9,8},{10,11... | collective-permute-start | bytes 393224 | tf_op jit(solution)/shard_map/ppermute | solution.py:332
  112.5 4.5 %collective-permute-start.14 = (bf16[2,128,256]{2,1,0:T(8,128)(2,1)S(1)}, bf16[2,128,256]{2,1,0:T(8,128)(2,1)S(1)}, u32[]{:S(2)}, u32[]{:S(2)}) collective-permute-start(bf16[2,128,256]{2,1,0:T(8,128)(2,1)S(1)} %get-tuple-element.45), channel_id=1, source_target_pairs={{0,2},{1,3},{2,0},{3,1},{4,6},{5,7},{6,4},{7,5},{8,10},{9,11},{10,... | collective-permute-start | bytes 393224 | tf_op jit(solution)/shard_map/ppermute | solution.py:492
  113.7 4.9 %collective-permute-start.16 = (bf16[2,128,256]{2,1,0:T(8,128)(2,1)S(1)}, bf16[2,128,256]{2,1,0:T(8,128)(2,1)S(1)}, u32[]{:S(2)}, u32[]{:S(2)}) collective-permute-start(bf16[2,128,256]{2,1,0:T(8,128)(2,1)S(1)} %get-tuple-element.46), channel_id=1, source_target_pairs={{0,4},{1,5},{2,6},{3,7},{4,0},{5,1},{6,2},{7,3},{8,12},{9,13},{10,... | collective-permute-start | bytes 393224 | tf_op jit(solution)/shard_map/ppermute | solution.py:492
  114.9 6.2 %collective-permute-start.18 = (bf16[2,128,256]{2,1,0:T(8,128)(2,1)S(1)}, bf16[2,128,256]{2,1,0:T(8,128)(2,1)S(1)}, u32[]{:S(2)}, u32[]{:S(2)}) collective-permute-start(bf16[2,128,256]{2,1,0:T(8,128)(2,1)S(1)} %get-tuple-element.47), channel_id=1, source_target_pairs={{0,6},{1,7},{2,4},{3,5},{4,2},{5,3},{6,0},{7,1},{8,14},{9,15},{10,... | collective-permute-start | bytes 393224 | tf_op jit(solution)/shard_map/ppermute | solution.py:492
  115.3 7.5 %collective-permute-start.13 = (bf16[2,128,256]{2,1,0:T(8,128)(2,1)S(1)}, bf16[2,128,256]{2,1,0:T(8,128)(2,1)S(1)}, u32[]{:S(2)}, u32[]{:S(2)}) collective-permute-start(bf16[2,128,256]{2,1,0:T(8,128)(2,1)S(1)} %get-tuple-element.44.refs_0_), channel_id=1, source_target_pairs={{0,1},{1,0},{2,3},{3,2},{4,5},{5,4},{6,7},{7,6},{8,9},{9,8},{10,11... | collective-permute-start | bytes 393224 | tf_op jit(solution)/shard_map/ppermute | solution.py:332
  117.0 5.8 %collective-permute-start.23 = (bf16[2,128,256]{2,1,0:T(8,128)(2,1)S(1)}, bf16[2,128,256]{2,1,0:T(8,128)(2,1)S(1)}, u32[]{:S(2)}, u32[]{:S(2)}) collective-permute-start(bf16[2,128,256]{2,1,0:T(8,128)(2,1)S(1)} %collective-permute-done.22.refs_10_), channel_id=1, source_target_pairs={{0,1},{1,0},{2,3},{3,2},{4,5},{5,4},{6,7},{7,6},{8,9},{9,8},{10,11... | collective-permute-start | bytes 393224 | tf_op jit(solution)/shard_map/ppermute | solution.py:332
  117.1 6.2 %collective-permute-start.25 = (bf16[2,128,256]{2,1,0:T(8,128)(2,1)S(1)}, bf16[2,128,256]{2,1,0:T(8,128)(2,1)S(1)}, u32[]{:S(2)}, u32[]{:S(2)}) collective-permute-start(bf16[2,128,256]{2,1,0:T(8,128)(2,1)S(1)} %collective-permute-done.24.refs_12_), channel_id=1, source_target_pairs={{0,1},{1,0},{2,3},{3,2},{4,5},{5,4},{6,7},{7,6},{8,9},{9,8},{10,11... | collective-permute-start | bytes 393224 | tf_op jit(solution)/shard_map/ppermute | solution.py:332
  118.5 4.7 %collective-permute-start.27 = (bf16[2,128,256]{2,1,0:T(8,128)(2,1)S(1)}, bf16[2,128,256]{2,1,0:T(8,128)(2,1)S(1)}, u32[]{:S(2)}, u32[]{:S(2)}) collective-permute-start(bf16[2,128,256]{2,1,0:T(8,128)(2,1)S(1)} %collective-permute-done.26.refs_14_), channel_id=1, source_target_pairs={{0,1},{1,0},{2,3},{3,2},{4,5},{5,4},{6,7},{7,6},{8,9},{9,8},{10,11... | collective-permute-start | bytes 393224 | tf_op jit(solution)/shard_map/ppermute | solution.py:332
  121.1 2.6 %collective-permute-start.15 = (bf16[2,128,256]{2,1,0:T(8,128)(2,1)S(1)}, bf16[2,128,256]{2,1,0:T(8,128)(2,1)S(1)}, u32[]{:S(2)}, u32[]{:S(2)}) collective-permute-start(bf16[2,128,256]{2,1,0:T(8,128)(2,1)S(1)} %collective-permute-done.14.refs_2_), channel_id=1, source_target_pairs={{0,1},{1,0},{2,3},{3,2},{4,5},{5,4},{6,7},{7,6},{8,9},{9,8},{10,11... | collective-permute-start | bytes 393224 | tf_op jit(solution)/shard_map/ppermute | solution.py:332
  122.7 1.3 %collective-permute-start.17 = (bf16[2,128,256]{2,1,0:T(8,128)(2,1)S(1)}, bf16[2,128,256]{2,1,0:T(8,128)(2,1)S(1)}, u32[]{:S(2)}, u32[]{:S(2)}) collective-permute-start(bf16[2,128,256]{2,1,0:T(8,128)(2,1)S(1)} %collective-permute-done.16.refs_4_), channel_id=1, source_target_pairs={{0,1},{1,0},{2,3},{3,2},{4,5},{5,4},{6,7},{7,6},{8,9},{9,8},{10,11... | collective-permute-start | bytes 393224 | tf_op jit(solution)/shard_map/ppermute | solution.py:332
  122.7 1.5 %collective-permute-start.19 = (bf16[2,128,256]{2,1,0:T(8,128)(2,1)S(1)}, bf16[2,128,256]{2,1,0:T(8,128)(2,1)S(1)}, u32[]{:S(2)}, u32[]{:S(2)}) collective-permute-start(bf16[2,128,256]{2,1,0:T(8,128)(2,1)S(1)} %collective-permute-done.18.refs_6_), channel_id=1, source_target_pairs={{0,1},{1,0},{2,3},{3,2},{4,5},{5,4},{6,7},{7,6},{8,9},{9,8},{10,11... | collective-permute-start | bytes 393224 | tf_op jit(solution)/shard_map/ppermute | solution.py:332

commit v4 on v3

--- a/solution.py
+++ b/solution.py
@@ -69,8 +69,8 @@
     ])
 
 
-def outward_kernel(columns_ref, *refs):
-    ins, out_ref, sem = refs[:-2], refs[-2], refs[-1]
+def outward_kernel(count, columns_ref, *refs):
+    ins, out_ref, sem = refs[:count], refs[-2], refs[-1]
     length, here = ins[0].shape[0], out_ref.shape[2]
     run_all([
         pltpu.make_async_copy(
@@ -331,19 +331,19 @@
     def swap(x):
         return lax.ppermute(x, ("side", "inner"), [(i, i ^ 1) for i in range(ways)])
 
-    def spread(*arrays, table=None, after=()):
+    def spread(*arrays, table=None, after=(), first=()):
         rows = len(arrays) * length
         extra = 0 if table is None else -(-3 * table.shape[0] // 16) * 16
         after = after if table is None else (table, *after)
         out = pl.pallas_call(
-            outward_kernel,
+            lambda *refs: outward_kernel(len(arrays), *refs),
             out_shape=pltpu.HBM((chips, rows, here), BF16),
-            in_specs=[SMEM] + [VMEM] * len(arrays),
+            in_specs=[SMEM] + [VMEM] * len(arrays) + [ANY] * len(first),
             out_specs=HBM,
             scratch_shapes=[pltpu.SemaphoreType.DMA((chips, len(arrays)))],
             compiler_params=PARAMS,
             name="outward",
-        )(columns, *arrays)
+        )(columns, *arrays, *first)
         parcels = pl.pallas_call(
             lambda *refs: parcel_kernel(len(arrays), extra, *refs),
             out_shape=[
@@ -372,7 +372,7 @@
             compiler_params=PARAMS,
             name="pieces",
         )(x, *after)
-        return lax.all_to_all(pieces, ("side", "inner"), split_axis=0, concat_axis=0, tiled=True)
+        return pieces, lax.all_to_all(pieces, ("side", "inner"), split_axis=0, concat_axis=0, tiled=True)
 
     def onward(x, steps=1):
         return lax.ppermute(x, "group", [(i, i + steps) for i in range(groups - steps)])
@@ -387,8 +387,8 @@
     mine = table(side * heads)
     gain = lax.dynamic_slice_in_dim(norm_gain, side * heads, heads, 0)
 
-    sparse_keys = exchange(sparse_key)
-    parcels, kv_parts = spread(lin_key, lin_value, table=table((1 - side) * heads))
+    pieces, sparse_keys = exchange(sparse_key)
+    parcels, kv_parts = spread(lin_key, lin_value, table=table((1 - side) * heads), first=(pieces,))
     _, q_parts = spread(lin_query, after=kv_parts[1:3])
     earlier_keys = onward(sparse_keys)
 
@@ -423,7 +423,7 @@
         cost_estimate=pl.CostEstimate(flops=2**31, bytes_accessed=6 * 2**20, transcendentals=2**19),
         name="inside",
     )(place, decays, starts, *q_parts, *kv_parts)
-    sparse_queries = exchange(sparse_query, after=(raw, *states))
+    _, sparse_queries = exchange(sparse_query, after=(raw, *states))
     firsts = pl.pallas_call(
         first_kernel,
         out_shape=[jax.ShapeDtypeStruct((ways, length, here // 2), BF16)] * 2,

time: 127 us -> 126 us (level)
    unnamed x47 -> x43, local copies, waits for them, and re-layouts: 9.55 us -> 8.47 us
where the time goes in v4:
time: 126 us; the launch traced here: 125 us
  starting transfers between devices  43.9 us (35%)
  Pallas kernels  40.1 us (32%)
  waiting for transfers between devices  31.2 us (25%)
  local copies, waits for them, and re-layouts  8.96 us (7%)
    ppermute x6, waiting for transfers between devices, spread(): lax.ppermute(x, ('side', 'inner'), [(i, i ^ 2 * k) for i in range(ways)])  17.1 us
    ppermute x6, starting transfers between devices, onward(): lax.ppermute(x, 'group', [(i, i + steps) for i in range(groups - steps)])  13.4 us
    ppermute x10, starting transfers between devices, swap(): return lax.ppermute(x, ('side', 'inner'), [(i, i ^ 1) for i in range(ways)])  11.5 us
    unnamed x43, local copies, waits for them, and re-layouts  8.47 us
    all_to_all x2, starting transfers between devices, exchange(): lax.all_to_all(pieces, ('side', 'inner'), split_axis=0, concat_axis=0, ti...  8.3 us
    pallas_call x2, Pallas kernels, local(): pl.pallas_call(sum_kernel, out_shape=[jax.ShapeDtypeStruct((2, length, so...  7.68 us
    pallas_call x1, Pallas kernels, local(): pl.pallas_call(weights_kernel, out_shape=jax.ShapeDtypeStruct((heads, tok...  7.67 us
    all_to_all x2, waiting for transfers between devices, exchange(): lax.all_to_all(pieces, ('side', 'inner'), split_axis=0, concat_axis=0, ti...  7.55 us
  transfers between devices with their start and end apart: 30, of which 14 were waited for; matrix products, arithmetic and copies ran while one was open for 0% of the time, Pallas kernels for 29%

profile of v4, /device:TPU:17, one launch (start us, length us, event | category | flops | bytes accessed | tf_op | source)
XLA Modules:
  0.0 124.9 jit_solution(16697881354649701531)
XLA Ops:
  0.1 1.4 %copy-done.8 = bf16[128,4096]{1,0:T(8,128)(2,1)S(1)} copy-done((bf16[128,4096]{1,0:T(8,128)(2,1)S(1)}, bf16[128,4096]{1,0:T(8,128)(2,1)}, u32[]{:S(2)}) %copy-start.8) | copy-done | bytes 1048600
  1.4 1.0 pieces.2.refs_3_
  2.6 1.6 %outward.2 = bf16[4,256,512]{2,1,0:T(8,128)(2,1)} custom-call(s32[4,2]{1,0:T(4,128)S(1)} %get-tuple-element.58.refs_0_.columns_ref, bf16[128,4096]{1,0:T(8,128)(2,1)S(1)} %copy-done.1, bf16[128,4096]{1,0:T(8,128)(2,1)S(1)} %copy-done.2, bf16[8,128,512]{2,1,0:T(8,128)(2,1)} %pieces.2.refs_3_), custom_call_target="tpu_custom_call" | custom-call | tf_op jit(solution)/shard_map/outward/pallas_call | solution.py:338
  4.3 0.7 collective-permute-start
  5.0 4.2 %all-to-all-start = ((bf16[8,128,512]{2,1,0:T(8,128)(2,1)}), bf16[8,128,512]{2,1,0:T(8,128)(2,1)}, u32[]{:S(2)}, u32[]{:S(2)}) async-start(bf16[8,128,512]{2,1,0:T(8,128)(2,1)} %pieces.2.refs_3_), calls=%async_computation | async-start | bytes 2097152 | tf_op jit(solution)/shard_map/all_to_all | solution.py:375
  9.5 2.8 %parcels.2 = (bf16[2,256,512]{2,1,0:T(8,128)(2,1)}, bf16[2,256,512]{2,1,0:T(8,128)(2,1)}, bf16[2,272,512]{2,1,0:T(8,128)(2,1)}, bf16[2,256,512]{2,1,0:T(8,128)(2,1)}) custom-call(s32[4,2]{1,0:T(4,128)S(1)} %get-tuple-element.58.refs_0_.columns_ref, s32[3]{0:T(128)S(1)} %pad_add_fusion.1.refs_1_.place_ref.refs_0_, bf16[128,4096]{1,0:T(8,128)(2,1)S(1)} %copy-done.1, ...), custom_call_target="tpu_custom_call" | custom-call | tf_op jit(solution)/shard_map/parcels/pallas_call | solution.py:347
  12.3 1.4 %collective-permute-start.2 = (bf16[2,272,512]{2,1,0:T(8,128)(2,1)}, bf16[2,272,512]{2,1,0:T(8,128)(2,1)S(1)}, u32[]{:S(2)}, u32[]{:S(2)}) collective-permute-start(bf16[2,272,512]{2,1,0:T(8,128)(2,1)} %get-tuple-element.31), channel_id=1, source_target_pairs={{0,4},{1,5},{2,6},{3,7},{4,0},{5,1},{6,2},{7,3},{8,12},{9,13},{10,... | collective-permute-start | bytes 1671176 | tf_op jit(solution)/shard_map/ppermute | solution.py:360
  13.7 1.4 %outward.3 = bf16[4,128,512]{2,1,0:T(8,128)(2,1)} custom-call(s32[4,2]{1,0:T(4,128)S(1)} %get-tuple-element.58.refs_0_.columns_ref, bf16[128,4096]{1,0:T(8,128)(2,1)S(1)} %copy-done.3), custom_call_target="tpu_custom_call" | custom-call | tf_op jit(solution)/shard_map/outward/pallas_call | solution.py:338
  15.1 0.7 collective-permute-start.5
  15.8 1.2 collective-permute-start.1
  17.0 5.8 %all-to-all-done = bf16[8,128,512]{2,1,0:T(8,128)(2,1)} async-done(((bf16[8,128,512]{2,1,0:T(8,128)(2,1)}), bf16[8,128,512]{2,1,0:T(8,128)(2,1)}, u32[]{:S(2)}, u32[]{:S(2)}) %all-to-all-start) | async-done | bytes 1048608 | tf_op jit(solution)/shard_map/all_to_all | solution.py:375
  22.9 3.2 %collective-permute-start.4 = (bf16[8,128,512]{2,1,0:T(8,128)(2,1)}, bf16[8,128,512]{2,1,0:T(8,128)(2,1)}, u32[]{:S(2)}, u32[]{:S(2)}) collective-permute-start(bf16[8,128,512]{2,1,0:T(8,128)(2,1)} %all-to-all-done), channel_id=1, source_target_pairs={{0,8},{8,16},{16,24},{1,9},{9,17},{17,25},{2,10},{10,18},{18,26},{... | collective-permute-start | bytes 3145736 | tf_op jit(solution)/shard_map/ppermute | solution.py:378
  26.1 8.0 %collective-permute-done.1.refs_1_.refs_4_.refs_8_ = bf16[2,256,512]{2,1,0:T(8,128)(2,1)S(1)} collective-permute-done((bf16[2,256,512]{2,1,0:T(8,128)(2,1)}, bf16[2,256,512]{2,1,0:T(8,128)(2,1)S(1)}, u32[]{:S(2)}, u32[]{:S(2)}) %collective-permute-start.1) | collective-permute-done | bytes 524320 | tf_op jit(solution)/shard_map/ppermute | solution.py:360
  34.1 0.7 collective-permute-done.2.refs_2_.refs_5_.refs_9_
  34.8 2.4 %parcels.3 = (bf16[2,128,512]{2,1,0:T(8,128)(2,1)}, bf16[2,128,512]{2,1,0:T(8,128)(2,1)}, bf16[2,128,512]{2,1,0:T(8,128)(2,1)}, bf16[2,128,512]{2,1,0:T(8,128)(2,1)}) custom-call(s32[4,2]{1,0:T(4,128)S(1)} %get-tuple-element.58.refs_0_.columns_ref, s32[3]{0:T(128)S(1)} %pad_add_fusion.1.refs_1_.place_ref.refs_0_, bf16[128,4096]{1,0:T(8,128)(2,1)S(1)} %copy-done.3, ...), custom_call_target="tpu_custom_call" | custom-call | tf_op jit(solution)/shard_map/parcels/pallas_call | solution.py:347
  37.2 1.3 %collective-permute-start.6 = (bf16[2,128,512]{2,1,0:T(8,128)(2,1)}, bf16[2,128,512]{2,1,0:T(8,128)(2,1)S(1)}, u32[]{:S(2)}, u32[]{:S(2)}) collective-permute-start(bf16[2,128,512]{2,1,0:T(8,128)(2,1)} %get-tuple-element.37), channel_id=1, source_target_pairs={{0,2},{1,3},{2,0},{3,1},{4,6},{5,7},{6,4},{7,5},{8,10},{9,11},{10,... | collective-permute-start | bytes 786440 | tf_op jit(solution)/shard_map/ppermute | solution.py:360
  38.5 0.3 collective-permute-start.7
  38.7 1.2 collective-permute-start.8
  39.9 7.1 %collective-permute-done.3.refs_3_.refs_10_ = bf16[2,256,512]{2,1,0:T(8,128)(2,1)} collective-permute-done((bf16[2,256,512]{2,1,0:T(8,128)(2,1)}, bf16[2,256,512]{2,1,0:T(8,128)(2,1)}, u32[]{:S(2)}, u32[]{:S(2)}) %collective-permute-start.3) | collective-permute-done | bytes 524320 | tf_op jit(solution)/shard_map/ppermute | solution.py:360
  47.0 4.0 %state.1 = (bf16[4,144,128]{2,1,0:T(8,128)(2,1)S(1)}, bf16[4,8,256,128]{3,2,1,0:T(8,128)(2,1)S(1)}, f32[32,128]{1,0:T(8,128)S(1)}, f32[2,1,512]{2,1,0:T(1,128)S(1)}) custom-call(s32[3]{0:T(128)S(1)} %pad_add_fusion.1.refs_1_.place_ref.refs_0_, f32[5,512]{1,0:T(8,128)S(1)} %get-tuple-element.56.table_ref, bf16[2,256,512]{2,1,0:T(8,128)(2,1)S(1)} %copy-done.14, ...), custom_call_target="tpu_custom_call" | custom-call | tf_op jit(solution)/shard_map/state/pallas_call | solution.py:395
  51.0 1.3 %collective-permute-start.10 = (bf16[4,144,128]{2,1,0:T(8,128)(2,1)S(1)}, bf16[4,144,128]{2,1,0:T(8,128)(2,1)S(1)}, u32[]{:S(2)}, u32[]{:S(2)}) collective-permute-start(bf16[4,144,128]{2,1,0:T(8,128)(2,1)S(1)} %get-tuple-element.41), channel_id=1, source_target_pairs={{0,16},{8,24},{1,17},{9,25},{2,18},{10,26},{3,19},{11,27},{4,20},{... | collective-permute-start | bytes 442376 | tf_op jit(solution)/shard_map/ppermute | solution.py:378
  52.3 0.8 collective-permute-done.6.refs_4_
  53.2 0.7 collective-permute-start.11
  53.9 3.8 %collective-permute-start.9 = (bf16[4,144,128]{2,1,0:T(8,128)(2,1)S(1)}, bf16[4,144,128]{2,1,0:T(8,128)(2,1)S(1)}, u32[]{:S(2)}, u32[]{:S(2)}) collective-permute-start(bf16[4,144,128]{2,1,0:T(8,128)(2,1)S(1)} %get-tuple-element.41), channel_id=1, source_target_pairs={{0,8},{8,16},{16,24},{1,9},{9,17},{17,25},{2,10},{10,18},{18,26},{... | collective-permute-start | bytes 442376 | tf_op jit(solution)/shard_map/ppermute | solution.py:378
  57.7 0.4 collective-permute-done.8.refs_6_
  58.1 1.1 copy-done.5
  59.2 1.0 copy-done.7
  60.2 1.0 copy-done.15
  61.3 4.7 %inside.1 = (f32[8,128,512]{2,1,0:T(8,128)S(1)}, bf16[8,128,512]{2,1,0:T(8,128)(2,1)S(1)}) custom-call(s32[3]{0:T(128)S(1)} %pad_add_fusion.1.refs_1_.place_ref.refs_0_, f32[32,128]{1,0:T(8,128)S(1)} %get-tuple-element.34.refs_1_.decay_ref, bf16[4,8,256,128]{3,2,1,0:T(8,128)(2,1)S(1)} %get-tuple-element.35.refs_2_, bf16[2,128,512]{2,1,0:T(8,128)(2,1)S(1)} %copy-done.18, ...), custom_call_target="tpu_custom_call" | custom-call | flops 2147483648 | bytes 6291456 | tf_op jit(solution)/shard_map/inside/pallas_call | solution.py:413
  66.0 1.0 copy-done.10
  67.0 2.0 %collective-permute-done.9.refs_1_.refs_0_ = bf16[4,144,128]{2,1,0:T(8,128)(2,1)S(1)} collective-permute-done((bf16[4,144,128]{2,1,0:T(8,128)(2,1)S(1)}, bf16[4,144,128]{2,1,0:T(8,128)(2,1)S(1)}, u32[]{:S(2)}, u32[]{:S(2)}) %collective-permute-start.9) | collective-permute-done | bytes 147488 | tf_op jit(solution)/shard_map/ppermute | solution.py:378
  69.0 1.1 pieces.3
  70.1 4.1 %all-to-all-start.1 = ((bf16[8,128,512]{2,1,0:T(8,128)(2,1)}), bf16[8,128,512]{2,1,0:T(8,128)(2,1)S(1)}, u32[]{:S(2)}, u32[]{:S(2)}) async-start(bf16[8,128,512]{2,1,0:T(8,128)(2,1)} %pieces.3), calls=%async_computation.1 | async-start | bytes 2097152 | tf_op jit(solution)/shard_map/all_to_all | solution.py:375
  74.2 0.1 add.79.order_ref
  74.3 1.2 copy-done.11
  75.5 0.9 copy-done.13
  76.4 4.0 %first.1 = (bf16[8,128,256]{2,1,0:T(8,128)(2,1)S(1)}, bf16[8,128,256]{2,1,0:T(8,128)(2,1)}) custom-call(f32[8,128,512]{2,1,0:T(8,128)S(1)} %get-tuple-element.40.refs_0_.raw_ref, bf16[8,128,512]{2,1,0:T(8,128)(2,1)S(1)} %copy-done.11, f32[32,128]{1,0:T(8,128)S(1)} %get-tuple-element.34.refs_1_.decay_ref, f32[4,128]{1,0:T(4,128)S(1)} %constant_dynamic-slice_fusion.gain_ref, ...), custom_call_target="tpu_custom_call" | custom-call | tf_op jit(solution)/shard_map/first/pallas_call | solution.py:427
  80.5 0.8 copy-done.16
  81.3 2.3 %collective-permute-start.20 = (bf16[8,128,256]{2,1,0:T(8,128)(2,1)}, bf16[8,128,256]{2,1,0:T(8,128)(2,1)S(1)}, u32[]{:S(2)}, u32[]{:S(2)}) collective-permute-start(bf16[8,128,256]{2,1,0:T(8,128)(2,1)} %get-tuple-element.48), channel_id=1, source_target_pairs={{0,8},{8,16},{16,24},{1,9},{9,17},{17,25},{2,10},{10,18},{18,26},{... | collective-permute-start | bytes 1572872 | tf_op jit(solution)/shard_map/ppermute | solution.py:378
  83.8 0.1 reshape.98.bias_ref
  83.9 2.1 %collective-permute-start.12 = (bf16[8,128,256]{2,1,0:T(8,128)(2,1)}, bf16[8,128,256]{2,1,0:T(8,128)(2,1)S(1)}, u32[]{:S(2)}, u32[]{:S(2)}) collective-permute-start(bf16[8,128,256]{2,1,0:T(8,128)(2,1)} %copy-done.16), channel_id=1, source_target_pairs={{0,8},{8,16},{16,24},{1,9},{9,17},{17,25},{2,10},{10,18},{18,26},{... | collective-permute-start | bytes 1572872 | tf_op jit(solution)/shard_map/ppermute | solution.py:378
  86.1 1.7 %all-to-all-done.1 = bf16[8,128,512]{2,1,0:T(8,128)(2,1)S(1)} async-done(((bf16[8,128,512]{2,1,0:T(8,128)(2,1)}), bf16[8,128,512]{2,1,0:T(8,128)(2,1)S(1)}, u32[]{:S(2)}, u32[]{:S(2)}) %all-to-all-start.1) | async-done | bytes 1048608 | tf_op jit(solution)/shard_map/all_to_all | solution.py:375
  87.8 7.7 %weights.1.weights_ref = bf16[4,1024,512]{2,1,0:T(8,128)(2,1)S(1)} custom-call(s32[16,8]{1,0:T(8,128)S(1)} %select_n.57.window_ref, bf16[1024,512]{1,0:T(8,128)(2,1)} %bitcast.4.own_ref, bf16[1024,512]{1,0:T(8,128)(2,1)} %bitcast.5.earlier_ref, f32[16,512]{1,0:T(8,128)S(1)} %reshape.98.bias_ref, bf16[1024,512]{1,0:T(8,128)(2,1)S(1)} %bitcast.14), custom_call_target="tpu_custom_call" | custom-call | flops 2147483648 | bytes 8388608 | tf_op jit(solution)/shard_map/weights/pallas_call | solution.py:442
  95.5 1.4 %collective-permute-done.20 = bf16[8,128,256]{2,1,0:T(8,128)(2,1)S(1)} collective-permute-done((bf16[8,128,256]{2,1,0:T(8,128)(2,1)}, bf16[8,128,256]{2,1,0:T(8,128)(2,1)S(1)}, u32[]{:S(2)}, u32[]{:S(2)}) %collective-permute-start.20) | collective-permute-done | bytes 524320 | tf_op jit(solution)/shard_map/ppermute | solution.py:378
  96.9 4.4 %sum.3 = (bf16[2,128,256]{2,1,0:T(8,128)(2,1)S(1)}, bf16[2,128,256]{2,1,0:T(8,128)(2,1)S(1)}, bf16[2,128,256]{2,1,0:T(8,128)(2,1)S(1)}, bf16[2,128,256]{2,1,0:T(8,128)(2,1)S(1)}) custom-call(s32[8]{0:T(128)S(1)} %add.79.order_ref, s32[16,8]{1,0:T(8,128)S(1)} %select_n.57.window_ref, bf16[4,1024,512]{2,1,0:T(8,128)(2,1)S(1)} %weights.1.weights_ref, ...), custom_call_target="tpu_custom_call" | custom-call | tf_op jit(solution)/shard_map/sum/pallas_call | solution.py:467
  101.3 1.1 collective-permute-start.22
  102.4 1.2 collective-permute-start.24
  103.6 0.4 collective-permute-start.26
  104.0 2.2 %collective-permute-start.21 = (bf16[2,128,256]{2,1,0:T(8,128)(2,1)S(1)}, bf16[2,128,256]{2,1,0:T(8,128)(2,1)S(1)}, u32[]{:S(2)}, u32[]{:S(2)}) collective-permute-start(bf16[2,128,256]{2,1,0:T(8,128)(2,1)S(1)} %get-tuple-element.49.refs_8_), channel_id=1, source_target_pairs={{0,1},{1,0},{2,3},{3,2},{4,5},{5,4},{6,7},{7,6},{8,9},{9,8},{10,11... | collective-permute-start | bytes 393224 | tf_op jit(solution)/shard_map/ppermute | solution.py:332
  106.2 2.0 %collective-permute-done.12 = bf16[8,128,256]{2,1,0:T(8,128)(2,1)S(1)} collective-permute-done((bf16[8,128,256]{2,1,0:T(8,128)(2,1)}, bf16[8,128,256]{2,1,0:T(8,128)(2,1)S(1)}, u32[]{:S(2)}, u32[]{:S(2)}) %collective-permute-start.12) | collective-permute-done | bytes 524320 | tf_op jit(solution)/shard_map/ppermute | solution.py:378
  108.1 3.3 %sum.2 = (bf16[2,128,256]{2,1,0:T(8,128)(2,1)S(1)}, bf16[2,128,256]{2,1,0:T(8,128)(2,1)S(1)}, bf16[2,128,256]{2,1,0:T(8,128)(2,1)S(1)}, bf16[2,128,256]{2,1,0:T(8,128)(2,1)S(1)}) custom-call(s32[8]{0:T(128)S(1)} %add.79.order_ref, s32[16,8]{1,0:T(8,128)S(1)} %select_n.57.window_ref, bf16[4,1024,512]{2,1,0:T(8,128)(2,1)S(1)} %weights.1.weights_ref, ...), custom_call_target="tpu_custom_call" | custom-call | tf_op jit(solution)/shard_map/sum/pallas_call | solution.py:467
  111.5 1.1 collective-permute-start.14
  112.6 1.2 collective-permute-start.16
  113.8 0.4 collective-permute-start.18
  114.2 1.7 %collective-permute-start.13 = (bf16[2,128,256]{2,1,0:T(8,128)(2,1)S(1)}, bf16[2,128,256]{2,1,0:T(8,128)(2,1)S(1)}, u32[]{:S(2)}, u32[]{:S(2)}) collective-permute-start(bf16[2,128,256]{2,1,0:T(8,128)(2,1)S(1)} %get-tuple-element.44.refs_0_), channel_id=1, source_target_pairs={{0,1},{1,0},{2,3},{3,2},{4,5},{5,4},{6,7},{7,6},{8,9},{9,8},{10,11... | collective-permute-start | bytes 393224 | tf_op jit(solution)/shard_map/ppermute | solution.py:332
  116.0 1.5 %collective-permute-start.25 = (bf16[2,128,256]{2,1,0:T(8,128)(2,1)S(1)}, bf16[2,128,256]{2,1,0:T(8,128)(2,1)S(1)}, u32[]{:S(2)}, u32[]{:S(2)}) collective-permute-start(bf16[2,128,256]{2,1,0:T(8,128)(2,1)S(1)} %collective-permute-done.24.refs_12_), channel_id=1, source_target_pairs={{0,1},{1,0},{2,3},{3,2},{4,5},{5,4},{6,7},{7,6},{8,9},{9,8},{10,11... | collective-permute-start | bytes 393224 | tf_op jit(solution)/shard_map/ppermute | solution.py:332
  117.4 2.5 %collective-permute-start.27 = (bf16[2,128,256]{2,1,0:T(8,128)(2,1)S(1)}, bf16[2,128,256]{2,1,0:T(8,128)(2,1)S(1)}, u32[]{:S(2)}, u32[]{:S(2)}) collective-permute-start(bf16[2,128,256]{2,1,0:T(8,128)(2,1)S(1)} %collective-permute-done.26.refs_14_), channel_id=1, source_target_pairs={{0,1},{1,0},{2,3},{3,2},{4,5},{5,4},{6,7},{7,6},{8,9},{9,8},{10,11... | collective-permute-start | bytes 393224 | tf_op jit(solution)/shard_map/ppermute | solution.py:332
  119.9 0.1 collective-permute-done.18.refs_6_
  120.0 1.6 %collective-permute-start.15 = (bf16[2,128,256]{2,1,0:T(8,128)(2,1)S(1)}, bf16[2,128,256]{2,1,0:T(8,128)(2,1)S(1)}, u32[]{:S(2)}, u32[]{:S(2)}) collective-permute-start(bf16[2,128,256]{2,1,0:T(8,128)(2,1)S(1)} %collective-permute-done.14.refs_2_), channel_id=1, source_target_pairs={{0,1},{1,0},{2,3},{3,2},{4,5},{5,4},{6,7},{7,6},{8,9},{9,8},{10,11... | collective-permute-start | bytes 393224 | tf_op jit(solution)/shard_map/ppermute | solution.py:332
  121.7 0.5 collective-permute-start.19
  122.2 0.5 collective-permute-done.15.refs_3_
  122.6 0.4 collective-permute-done.17.refs_5_
  123.0 0.2 collective-permute-done.19.refs_7_
  123.2 1.7 %join.1 = bf16[128,4096]{1,0:T(8,128)(2,1)} custom-call(s32[4,2]{1,0:T(4,128)S(1)} %get-tuple-element.58.refs_0_.columns_ref, bf16[2,128,256]{2,1,0:T(8,128)(2,1)S(1)} %get-tuple-element.44.refs_0_, bf16[2,128,256]{2,1,0:T(8,128)(2,1)S(1)} %collective-permute-done.13.refs_1_, bf16[2,128,256]{2,1,0:T(8,128)(2,1)S(1)} %collective-permute-done.14.refs_2_, ...), custom_call_target="tpu_custom_call" | custom-call | tf_op jit(solution)/shard_map/join/pallas_call | solution.py:494
  (69 shorter events, 0.8 us)
Async XLA Ops:
  0.0 74.3 %copy-start = (f32[8,128]{1,0:T(8,128)S(1)}, f32[8,128]{1,0:T(8,128)}, u32[]{:S(2)}) copy-start(f32[8,128]{1,0:T(8,128)} %param.14) | copy-start | bytes 12292
  0.0 2.6 %copy-start.2 = (bf16[128,4096]{1,0:T(8,128)(2,1)S(1)}, bf16[128,4096]{1,0:T(8,128)(2,1)}, u32[]{:S(2)}) copy-start(bf16[128,4096]{1,0:T(8,128)(2,1)} %refs_3_.1) | copy-start | bytes 3145732
  0.0 2.6 %copy-start.1 = (bf16[128,4096]{1,0:T(8,128)(2,1)S(1)}, bf16[128,4096]{1,0:T(8,128)(2,1)}, u32[]{:S(2)}) copy-start(bf16[128,4096]{1,0:T(8,128)(2,1)} %refs_2_.4) | copy-start | bytes 3145732
  0.1 1.4 %copy-start.8 = (bf16[128,4096]{1,0:T(8,128)(2,1)S(1)}, bf16[128,4096]{1,0:T(8,128)(2,1)}, u32[]{:S(2)}) copy-start(bf16[128,4096]{1,0:T(8,128)(2,1)} %in_ref.2) | copy-start | bytes 3145732
  4.3 5.0 %copy-start.20 = (s32[8,8]{1,0:T(8,128)S(1)}, s32[8,8]{1,0:T(8,128)}, u32[]{:S(2)}) copy-start(s32[8,8]{1,0:T(8,128)} %param.15) | copy-start | bytes 772
  4.3 5.2 %copy-start.19 = (f32[8,512]{1,0:T(8,128)S(1)}, f32[8,512]{1,0:T(8,128)}, u32[]{:S(2)}) copy-start(f32[8,512]{1,0:T(8,128)} %param.13) | copy-start | bytes 49156
  4.3 5.2 %collective-permute-start = (bf16[4,256,512]{2,1,0:T(8,128)(2,1)}, bf16[4,256,512]{2,1,0:T(8,128)(2,1)}, u32[]{:S(2)}, u32[]{:S(2)}) collective-permute-start(bf16[4,256,512]{2,1,0:T(8,128)(2,1)} %outward.2), channel_id=1, source_target_pairs={{0,1},{1,0},{2,3},{3,2},{4,5},{5,4},{6,7},{7,6},{8,9},{9,8},{10,11... | collective-permute-start | bytes 3145736 | tf_op jit(solution)/shard_map/ppermute | solution.py:332
  5.0 17.9 %all-to-all-start = ((bf16[8,128,512]{2,1,0:T(8,128)(2,1)}), bf16[8,128,512]{2,1,0:T(8,128)(2,1)}, u32[]{:S(2)}, u32[]{:S(2)}) async-start(bf16[8,128,512]{2,1,0:T(8,128)(2,1)} %pieces.2.refs_3_), calls=%async_computation | async-start | bytes 2097152 | tf_op jit(solution)/shard_map/all_to_all | solution.py:375
  9.2 4.5 %copy-start.3 = (bf16[128,4096]{1,0:T(8,128)(2,1)S(1)}, bf16[128,4096]{1,0:T(8,128)(2,1)}, u32[]{:S(2)}) copy-start(bf16[128,4096]{1,0:T(8,128)(2,1)} %refs_2_.5) | copy-start | bytes 3145732
  12.3 34.7 %copy-start.14 = (bf16[2,256,512]{2,1,0:T(8,128)(2,1)S(1)}, bf16[2,256,512]{2,1,0:T(8,128)(2,1)}, u32[]{:S(2)}) copy-start(bf16[2,256,512]{2,1,0:T(8,128)(2,1)} %get-tuple-element.29.refs_0_.refs_7_) | copy-start | bytes 1572868
  12.3 22.5 %collective-permute-start.2 = (bf16[2,272,512]{2,1,0:T(8,128)(2,1)}, bf16[2,272,512]{2,1,0:T(8,128)(2,1)S(1)}, u32[]{:S(2)}, u32[]{:S(2)}) collective-permute-start(bf16[2,272,512]{2,1,0:T(8,128)(2,1)} %get-tuple-element.31), channel_id=1, source_target_pairs={{0,4},{1,5},{2,6},{3,7},{4,0},{5,1},{6,2},{7,3},{8,12},{9,13},{10,... | collective-permute-start | bytes 1671176 | tf_op jit(solution)/shard_map/ppermute | solution.py:360
  15.1 11.0 %collective-permute-start.5 = (bf16[4,128,512]{2,1,0:T(8,128)(2,1)}, bf16[4,128,512]{2,1,0:T(8,128)(2,1)}, u32[]{:S(2)}, u32[]{:S(2)}) collective-permute-start(bf16[4,128,512]{2,1,0:T(8,128)(2,1)} %outward.3), channel_id=1, source_target_pairs={{0,1},{1,0},{2,3},{3,2},{4,5},{5,4},{6,7},{7,6},{8,9},{9,8},{10,11... | collective-permute-start | bytes 1572872 | tf_op jit(solution)/shard_map/ppermute | solution.py:332
  15.8 18.3 %collective-permute-start.1 = (bf16[2,256,512]{2,1,0:T(8,128)(2,1)}, bf16[2,256,512]{2,1,0:T(8,128)(2,1)S(1)}, u32[]{:S(2)}, u32[]{:S(2)}) collective-permute-start(bf16[2,256,512]{2,1,0:T(8,128)(2,1)} %get-tuple-element.30), channel_id=1, source_target_pairs={{0,2},{1,3},{2,0},{3,1},{4,6},{5,7},{6,4},{7,5},{8,10},{9,11},{10,... | collective-permute-start | bytes 1572872 | tf_op jit(solution)/shard_map/ppermute | solution.py:360
  17.0 30.0 %collective-permute-start.3 = (bf16[2,256,512]{2,1,0:T(8,128)(2,1)}, bf16[2,256,512]{2,1,0:T(8,128)(2,1)}, u32[]{:S(2)}, u32[]{:S(2)}) collective-permute-start(bf16[2,256,512]{2,1,0:T(8,128)(2,1)} %get-tuple-element.32), channel_id=1, source_target_pairs={{0,6},{1,7},{2,4},{3,5},{4,2},{5,3},{6,0},{7,1},{8,14},{9,15},{10,... | collective-permute-start | bytes 1572872 | tf_op jit(solution)/shard_map/ppermute | solution.py:360
  22.9 51.4 %collective-permute-start.4 = (bf16[8,128,512]{2,1,0:T(8,128)(2,1)}, bf16[8,128,512]{2,1,0:T(8,128)(2,1)}, u32[]{:S(2)}, u32[]{:S(2)}) collective-permute-start(bf16[8,128,512]{2,1,0:T(8,128)(2,1)} %all-to-all-done), channel_id=1, source_target_pairs={{0,8},{8,16},{16,24},{1,9},{9,17},{17,25},{2,10},{10,18},{18,26},{... | collective-permute-start | bytes 3145736 | tf_op jit(solution)/shard_map/ppermute | solution.py:378
  34.1 16.9 %copy-start.6 = (bf16[2,256,512]{2,1,0:T(8,128)(2,1)}, bf16[2,256,512]{2,1,0:T(8,128)(2,1)S(1)}, u32[]{:S(2)}) copy-start(bf16[2,256,512]{2,1,0:T(8,128)(2,1)S(1)} %collective-permute-done.1.refs_1_.refs_4_.refs_8_) | copy-start | bytes 1572868
  34.8 16.2 %copy-start.4 = (bf16[2,272,512]{2,1,0:T(8,128)(2,1)}, bf16[2,272,512]{2,1,0:T(8,128)(2,1)S(1)}, u32[]{:S(2)}) copy-start(bf16[2,272,512]{2,1,0:T(8,128)(2,1)S(1)} %collective-permute-done.2.refs_2_.refs_5_.refs_9_) | copy-start | bytes 1671172
  37.2 21.0 %copy-start.18 = (bf16[2,128,512]{2,1,0:T(8,128)(2,1)S(1)}, bf16[2,128,512]{2,1,0:T(8,128)(2,1)}, u32[]{:S(2)}) copy-start(bf16[2,128,512]{2,1,0:T(8,128)(2,1)} %get-tuple-element.36.refs_3_) | copy-start | bytes 786436
  37.2 16.0 %collective-permute-start.6 = (bf16[2,128,512]{2,1,0:T(8,128)(2,1)}, bf16[2,128,512]{2,1,0:T(8,128)(2,1)S(1)}, u32[]{:S(2)}, u32[]{:S(2)}) collective-permute-start(bf16[2,128,512]{2,1,0:T(8,128)(2,1)} %get-tuple-element.37), channel_id=1, source_target_pairs={{0,2},{1,3},{2,0},{3,1},{4,6},{5,7},{6,4},{7,5},{8,10},{9,11},{10,... | collective-permute-start | bytes 786440 | tf_op jit(solution)/shard_map/ppermute | solution.py:360
  38.5 15.4 %collective-permute-start.7 = (bf16[2,128,512]{2,1,0:T(8,128)(2,1)}, bf16[2,128,512]{2,1,0:T(8,128)(2,1)S(1)}, u32[]{:S(2)}, u32[]{:S(2)}) collective-permute-start(bf16[2,128,512]{2,1,0:T(8,128)(2,1)} %get-tuple-element.38), channel_id=1, source_target_pairs={{0,4},{1,5},{2,6},{3,7},{4,0},{5,1},{6,2},{7,3},{8,12},{9,13},{10,... | collective-permute-start | bytes 786440 | tf_op jit(solution)/shard_map/ppermute | solution.py:360
  38.7 19.4 %collective-permute-start.8 = (bf16[2,128,512]{2,1,0:T(8,128)(2,1)}, bf16[2,128,512]{2,1,0:T(8,128)(2,1)S(1)}, u32[]{:S(2)}, u32[]{:S(2)}) collective-permute-start(bf16[2,128,512]{2,1,0:T(8,128)(2,1)} %get-tuple-element.39), channel_id=1, source_target_pairs={{0,6},{1,7},{2,4},{3,5},{4,2},{5,3},{6,0},{7,1},{8,14},{9,15},{10,... | collective-permute-start | bytes 786440 | tf_op jit(solution)/shard_map/ppermute | solution.py:360
  51.0 15.9 %collective-permute-start.10 = (bf16[4,144,128]{2,1,0:T(8,128)(2,1)S(1)}, bf16[4,144,128]{2,1,0:T(8,128)(2,1)S(1)}, u32[]{:S(2)}, u32[]{:S(2)}) collective-permute-start(bf16[4,144,128]{2,1,0:T(8,128)(2,1)S(1)} %get-tuple-element.41), channel_id=1, source_target_pairs={{0,16},{8,24},{1,17},{9,25},{2,18},{10,26},{3,19},{11,27},{4,20},{... | collective-permute-start | bytes 442376 | tf_op jit(solution)/shard_map/ppermute | solution.py:378
  53.2 13.8 %collective-permute-start.11 = (bf16[4,144,128]{2,1,0:T(8,128)(2,1)S(1)}, bf16[4,144,128]{2,1,0:T(8,128)(2,1)S(1)}, u32[]{:S(2)}, u32[]{:S(2)}) collective-permute-start(bf16[4,144,128]{2,1,0:T(8,128)(2,1)S(1)} %get-tuple-element.41), channel_id=1, source_target_pairs={{0,24},{1,25},{2,26},{3,27},{4,28},{5,29},{6,30},{7,31}} | collective-permute-start | bytes 442376 | tf_op jit(solution)/shard_map/ppermute | solution.py:378
  53.9 15.1 %collective-permute-start.9 = (bf16[4,144,128]{2,1,0:T(8,128)(2,1)S(1)}, bf16[4,144,128]{2,1,0:T(8,128)(2,1)S(1)}, u32[]{:S(2)}, u32[]{:S(2)}) collective-permute-start(bf16[4,144,128]{2,1,0:T(8,128)(2,1)S(1)} %get-tuple-element.41), channel_id=1, source_target_pairs={{0,8},{8,16},{16,24},{1,9},{9,17},{17,25},{2,10},{10,18},{18,26},{... | collective-permute-start | bytes 442376 | tf_op jit(solution)/shard_map/ppermute | solution.py:378
  58.1 1.1 copy-start.5
  59.2 1.0 copy-start.7
  60.2 1.0 copy-start.15
  61.3 7.7 %copy-start.9 = (bf16[128,4096]{1,0:T(8,128)(2,1)S(1)}, bf16[128,4096]{1,0:T(8,128)(2,1)}, u32[]{:S(2)}) copy-start(bf16[128,4096]{1,0:T(8,128)(2,1)} %in_ref.3) | copy-start | bytes 3145732
  66.0 1.0 copy-start.10
  69.0 1.1 copy-start.12
  70.1 17.7 %all-to-all-start.1 = ((bf16[8,128,512]{2,1,0:T(8,128)(2,1)}), bf16[8,128,512]{2,1,0:T(8,128)(2,1)S(1)}, u32[]{:S(2)}, u32[]{:S(2)}) async-start(bf16[8,128,512]{2,1,0:T(8,128)(2,1)} %pieces.3), calls=%async_computation.1 | async-start | bytes 2097152 | tf_op jit(solution)/shard_map/all_to_all | solution.py:375
  74.3 1.2 copy-start.11
  75.5 0.9 copy-start.13
  80.5 0.8 copy-start.16
  81.3 15.6 %collective-permute-start.20 = (bf16[8,128,256]{2,1,0:T(8,128)(2,1)}, bf16[8,128,256]{2,1,0:T(8,128)(2,1)S(1)}, u32[]{:S(2)}, u32[]{:S(2)}) collective-permute-start(bf16[8,128,256]{2,1,0:T(8,128)(2,1)} %get-tuple-element.48), channel_id=1, source_target_pairs={{0,8},{8,16},{16,24},{1,9},{9,17},{17,25},{2,10},{10,18},{18,26},{... | collective-permute-start | bytes 1572872 | tf_op jit(solution)/shard_map/ppermute | solution.py:378
  83.9 24.2 %collective-permute-start.12 = (bf16[8,128,256]{2,1,0:T(8,128)(2,1)}, bf16[8,128,256]{2,1,0:T(8,128)(2,1)S(1)}, u32[]{:S(2)}, u32[]{:S(2)}) collective-permute-start(bf16[8,128,256]{2,1,0:T(8,128)(2,1)} %copy-done.16), channel_id=1, source_target_pairs={{0,8},{8,16},{16,24},{1,9},{9,17},{17,25},{2,10},{10,18},{18,26},{... | collective-permute-start | bytes 1572872 | tf_op jit(solution)/shard_map/ppermute | solution.py:378
  96.9 11.2 %copy-start.17 = (bf16[8,128,256]{2,1,0:T(8,128)(2,1)S(1)}, bf16[8,128,256]{2,1,0:T(8,128)(2,1)}, u32[]{:S(2)}) copy-start(bf16[8,128,256]{2,1,0:T(8,128)(2,1)} %copy-done.16) | copy-start | bytes 1572868
  101.3 11.3 %collective-permute-start.22 = (bf16[2,128,256]{2,1,0:T(8,128)(2,1)S(1)}, bf16[2,128,256]{2,1,0:T(8,128)(2,1)S(1)}, u32[]{:S(2)}, u32[]{:S(2)}) collective-permute-start(bf16[2,128,256]{2,1,0:T(8,128)(2,1)S(1)} %get-tuple-element.50), channel_id=1, source_target_pairs={{0,2},{1,3},{2,0},{3,1},{4,6},{5,7},{6,4},{7,5},{8,10},{9,11},{10,... | collective-permute-start | bytes 393224 | tf_op jit(solution)/shard_map/ppermute | solution.py:492
  102.4 11.4 %collective-permute-start.24 = (bf16[2,128,256]{2,1,0:T(8,128)(2,1)S(1)}, bf16[2,128,256]{2,1,0:T(8,128)(2,1)S(1)}, u32[]{:S(2)}, u32[]{:S(2)}) collective-permute-start(bf16[2,128,256]{2,1,0:T(8,128)(2,1)S(1)} %get-tuple-element.51), channel_id=1, source_target_pairs={{0,4},{1,5},{2,6},{3,7},{4,0},{5,1},{6,2},{7,3},{8,12},{9,13},{10,... | collective-permute-start | bytes 393224 | tf_op jit(solution)/shard_map/ppermute | solution.py:492
  103.6 10.6 %collective-permute-start.26 = (bf16[2,128,256]{2,1,0:T(8,128)(2,1)S(1)}, bf16[2,128,256]{2,1,0:T(8,128)(2,1)S(1)}, u32[]{:S(2)}, u32[]{:S(2)}) collective-permute-start(bf16[2,128,256]{2,1,0:T(8,128)(2,1)S(1)} %get-tuple-element.52), channel_id=1, source_target_pairs={{0,6},{1,7},{2,4},{3,5},{4,2},{5,3},{6,0},{7,1},{8,14},{9,15},{10,... | collective-permute-start | bytes 393224 | tf_op jit(solution)/shard_map/ppermute | solution.py:492
  104.0 11.9 %collective-permute-start.21 = (bf16[2,128,256]{2,1,0:T(8,128)(2,1)S(1)}, bf16[2,128,256]{2,1,0:T(8,128)(2,1)S(1)}, u32[]{:S(2)}, u32[]{:S(2)}) collective-permute-start(bf16[2,128,256]{2,1,0:T(8,128)(2,1)S(1)} %get-tuple-element.49.refs_8_), channel_id=1, source_target_pairs={{0,1},{1,0},{2,3},{3,2},{4,5},{5,4},{6,7},{7,6},{8,9},{9,8},{10,11... | collective-permute-start | bytes 393224 | tf_op jit(solution)/shard_map/ppermute | solution.py:332
  111.5 4.5 %collective-permute-start.14 = (bf16[2,128,256]{2,1,0:T(8,128)(2,1)S(1)}, bf16[2,128,256]{2,1,0:T(8,128)(2,1)S(1)}, u32[]{:S(2)}, u32[]{:S(2)}) collective-permute-start(bf16[2,128,256]{2,1,0:T(8,128)(2,1)S(1)} %get-tuple-element.45), channel_id=1, source_target_pairs={{0,2},{1,3},{2,0},{3,1},{4,6},{5,7},{6,4},{7,5},{8,10},{9,11},{10,... | collective-permute-start | bytes 393224 | tf_op jit(solution)/shard_map/ppermute | solution.py:492
  112.6 4.9 %collective-permute-start.16 = (bf16[2,128,256]{2,1,0:T(8,128)(2,1)S(1)}, bf16[2,128,256]{2,1,0:T(8,128)(2,1)S(1)}, u32[]{:S(2)}, u32[]{:S(2)}) collective-permute-start(bf16[2,128,256]{2,1,0:T(8,128)(2,1)S(1)} %get-tuple-element.46), channel_id=1, source_target_pairs={{0,4},{1,5},{2,6},{3,7},{4,0},{5,1},{6,2},{7,3},{8,12},{9,13},{10,... | collective-permute-start | bytes 393224 | tf_op jit(solution)/shard_map/ppermute | solution.py:492
  113.8 6.2 %collective-permute-start.18 = (bf16[2,128,256]{2,1,0:T(8,128)(2,1)S(1)}, bf16[2,128,256]{2,1,0:T(8,128)(2,1)S(1)}, u32[]{:S(2)}, u32[]{:S(2)}) collective-permute-start(bf16[2,128,256]{2,1,0:T(8,128)(2,1)S(1)} %get-tuple-element.47), channel_id=1, source_target_pairs={{0,6},{1,7},{2,4},{3,5},{4,2},{5,3},{6,0},{7,1},{8,14},{9,15},{10,... | collective-permute-start | bytes 393224 | tf_op jit(solution)/shard_map/ppermute | solution.py:492
  114.2 7.5 %collective-permute-start.13 = (bf16[2,128,256]{2,1,0:T(8,128)(2,1)S(1)}, bf16[2,128,256]{2,1,0:T(8,128)(2,1)S(1)}, u32[]{:S(2)}, u32[]{:S(2)}) collective-permute-start(bf16[2,128,256]{2,1,0:T(8,128)(2,1)S(1)} %get-tuple-element.44.refs_0_), channel_id=1, source_target_pairs={{0,1},{1,0},{2,3},{3,2},{4,5},{5,4},{6,7},{7,6},{8,9},{9,8},{10,11... | collective-permute-start | bytes 393224 | tf_op jit(solution)/shard_map/ppermute | solution.py:332
  115.9 5.8 %collective-permute-start.23 = (bf16[2,128,256]{2,1,0:T(8,128)(2,1)S(1)}, bf16[2,128,256]{2,1,0:T(8,128)(2,1)S(1)}, u32[]{:S(2)}, u32[]{:S(2)}) collective-permute-start(bf16[2,128,256]{2,1,0:T(8,128)(2,1)S(1)} %collective-permute-done.22.refs_10_), channel_id=1, source_target_pairs={{0,1},{1,0},{2,3},{3,2},{4,5},{5,4},{6,7},{7,6},{8,9},{9,8},{10,11... | collective-permute-start | bytes 393224 | tf_op jit(solution)/shard_map/ppermute | solution.py:332
  116.0 6.2 %collective-permute-start.25 = (bf16[2,128,256]{2,1,0:T(8,128)(2,1)S(1)}, bf16[2,128,256]{2,1,0:T(8,128)(2,1)S(1)}, u32[]{:S(2)}, u32[]{:S(2)}) collective-permute-start(bf16[2,128,256]{2,1,0:T(8,128)(2,1)S(1)} %collective-permute-done.24.refs_12_), channel_id=1, source_target_pairs={{0,1},{1,0},{2,3},{3,2},{4,5},{5,4},{6,7},{7,6},{8,9},{9,8},{10,11... | collective-permute-start | bytes 393224 | tf_op jit(solution)/shard_map/ppermute | solution.py:332
  117.4 4.7 %collective-permute-start.27 = (bf16[2,128,256]{2,1,0:T(8,128)(2,1)S(1)}, bf16[2,128,256]{2,1,0:T(8,128)(2,1)S(1)}, u32[]{:S(2)}, u32[]{:S(2)}) collective-permute-start(bf16[2,128,256]{2,1,0:T(8,128)(2,1)S(1)} %collective-permute-done.26.refs_14_), channel_id=1, source_target_pairs={{0,1},{1,0},{2,3},{3,2},{4,5},{5,4},{6,7},{7,6},{8,9},{9,8},{10,11... | collective-permute-start | bytes 393224 | tf_op jit(solution)/shard_map/ppermute | solution.py:332
  120.0 2.6 %collective-permute-start.15 = (bf16[2,128,256]{2,1,0:T(8,128)(2,1)S(1)}, bf16[2,128,256]{2,1,0:T(8,128)(2,1)S(1)}, u32[]{:S(2)}, u32[]{:S(2)}) collective-permute-start(bf16[2,128,256]{2,1,0:T(8,128)(2,1)S(1)} %collective-permute-done.14.refs_2_), channel_id=1, source_target_pairs={{0,1},{1,0},{2,3},{3,2},{4,5},{5,4},{6,7},{7,6},{8,9},{9,8},{10,11... | collective-permute-start | bytes 393224 | tf_op jit(solution)/shard_map/ppermute | solution.py:332
  121.7 1.3 %collective-permute-start.17 = (bf16[2,128,256]{2,1,0:T(8,128)(2,1)S(1)}, bf16[2,128,256]{2,1,0:T(8,128)(2,1)S(1)}, u32[]{:S(2)}, u32[]{:S(2)}) collective-permute-start(bf16[2,128,256]{2,1,0:T(8,128)(2,1)S(1)} %collective-permute-done.16.refs_4_), channel_id=1, source_target_pairs={{0,1},{1,0},{2,3},{3,2},{4,5},{5,4},{6,7},{7,6},{8,9},{9,8},{10,11... | collective-permute-start | bytes 393224 | tf_op jit(solution)/shard_map/ppermute | solution.py:332
  121.7 1.5 %collective-permute-start.19 = (bf16[2,128,256]{2,1,0:T(8,128)(2,1)S(1)}, bf16[2,128,256]{2,1,0:T(8,128)(2,1)S(1)}, u32[]{:S(2)}, u32[]{:S(2)}) collective-permute-start(bf16[2,128,256]{2,1,0:T(8,128)(2,1)S(1)} %collective-permute-done.18.refs_6_), channel_id=1, source_target_pairs={{0,1},{1,0},{2,3},{3,2},{4,5},{5,4},{6,7},{7,6},{8,9},{9,8},{10,11... | collective-permute-start | bytes 393224 | tf_op jit(solution)/shard_map/ppermute | solution.py:332

commit v5 on v4

--- a/solution.py
+++ b/solution.py
@@ -210,11 +210,12 @@
 
 
 def first_kernel(raw_ref, q_ref, decay_ref, gain_ref, *refs):
-    earlier, outs = refs[:-3], refs[-2:]
+    earlier, outs, (made_ref, sem) = refs[:-5], refs[-4:-2], refs[-2:]
     chunks, length, here = q_ref.shape
     heads, width = gain_ref.shape
     down = summed_down(jnp.log(decay_ref[...]))
     lifts = jnp.exp(down + other_chunks(down[length - 1 : length, :], chunks, False))
+    copies = []
     for h in range(heads):
         columns = slice(h * width, (h + 1) * width)
         carried = jnp.zeros((width, width), F32)
@@ -225,14 +226,19 @@
             factor = factor * (parts[0:1, 0:1] + parts[1:2, 0:1] + parts[2:3, 0:1])
         both = jnp.concatenate(halves(carried), 0)
         gain = gain_ref[h : h + 1, :]
-        place = h % (heads // 2)
+        half, place = divmod(h, heads // 2)
         for c in range(chunks):
             at = h * chunks + c
             queries = q_ref[c, :, columns]
             outside = dot(jnp.concatenate([queries, queries], 1), both, ((1,), (0,)))
             raw = raw_ref[c, :, columns] + lifts[:, at : at + 1] * outside
             scale = lax.rsqrt(jnp.mean(raw * raw, axis=-1, keepdims=True) + 1e-06)
-            outs[h // (heads // 2)][c, :, place * width : (place + 1) * width] = (raw * scale * gain).astype(BF16)
+            made_ref[half, c, :, place * width : (place + 1) * width] = (raw * scale * gain).astype(BF16)
+        if place == heads // 2 - 1:
+            copies.append(pltpu.make_async_copy(made_ref.at[half], outs[half], sem.at[half]))
+            copies[-1].start()
+    for copy in copies:
+        copy.wait()
 
 
 def pick(window_ref, b, source_ref, picked_ref):
@@ -426,9 +432,10 @@
     _, sparse_queries = exchange(sparse_query, after=(raw, *states))
     firsts = pl.pallas_call(
         first_kernel,
-        out_shape=[jax.ShapeDtypeStruct((ways, length, here // 2), BF16)] * 2,
+        out_shape=[pltpu.HBM((ways, length, here // 2), BF16)] * 2,
         in_specs=[VMEM] * (4 + len(states)) + [ANY],
-        out_specs=[VMEM] * 2,
+        out_specs=[HBM] * 2,
+        scratch_shapes=[pltpu.VMEM((2, ways, length, here // 2), BF16), pltpu.SemaphoreType.DMA((2,))],
         compiler_params=PARAMS,
         name="first",
     )(raw, queries, decays, gain, *states, earlier_keys)

time: 126 us -> 125 us (level)
  transfers between devices with their start and end apart: 30 -> 30, of which waited for: 14 -> 14; matrix products, arithmetic and copies ran while one was open for 0% -> 0% of each run, Pallas kernels for 29% -> 28%
where the time goes in v5:
time: 125 us; the launch traced here: 124 us
  starting transfers between devices  43.9 us (35%)
  Pallas kernels  39.3 us (31%)
  waiting for transfers between devices  32 us (26%)
  local copies, waits for them, and re-layouts  8.15 us (7%)
    ppermute x6, waiting for transfers between devices, spread(): lax.ppermute(x, ('side', 'inner'), [(i, i ^ 2 * k) for i in range(ways)])  17.1 us
    ppermute x6, starting transfers between devices, onward(): lax.ppermute(x, 'group', [(i, i + steps) for i in range(groups - steps)])  13.4 us
    ppermute x10, starting transfers between devices, swap(): return lax.ppermute(x, ('side', 'inner'), [(i, i ^ 1) for i in range(ways)])  11.5 us
    all_to_all x2, starting transfers between devices, exchange(): lax.all_to_all(pieces, ('side', 'inner'), split_axis=0, concat_axis=0, ti...  8.3 us
    all_to_all x2, waiting for transfers between devices, exchange(): lax.all_to_all(pieces, ('side', 'inner'), split_axis=0, concat_axis=0, ti...  8.29 us
    pallas_call x1, Pallas kernels, local(): pl.pallas_call(weights_kernel, out_shape=jax.ShapeDtypeStruct((heads, tok...  7.82 us
    unnamed x43, local copies, waits for them, and re-layouts  7.66 us
    pallas_call x2, Pallas kernels, local(): pl.pallas_call(sum_kernel, out_shape=[jax.ShapeDtypeStruct((2, length, so...  6.66 us
  transfers between devices with their start and end apart: 30, of which 14 were waited for; matrix products, arithmetic and copies ran while one was open for 0% of the time, Pallas kernels for 28%

profile of v5, /device:TPU:17, one launch (start us, length us, event | category | flops | bytes accessed | tf_op | source)
XLA Modules:
  0.0 124.1 jit_solution(14244010453850525183)
XLA Ops:
  0.1 1.4 %copy-done.8 = bf16[128,4096]{1,0:T(8,128)(2,1)S(1)} copy-done((bf16[128,4096]{1,0:T(8,128)(2,1)S(1)}, bf16[128,4096]{1,0:T(8,128)(2,1)}, u32[]{:S(2)}) %copy-start.8) | copy-done | bytes 1048600
  1.4 1.0 pieces.2.refs_3_
  2.6 1.6 %outward.2 = bf16[4,256,512]{2,1,0:T(8,128)(2,1)} custom-call(s32[4,2]{1,0:T(4,128)S(1)} %get-tuple-element.58.refs_0_.columns_ref, bf16[128,4096]{1,0:T(8,128)(2,1)S(1)} %copy-done.1, bf16[128,4096]{1,0:T(8,128)(2,1)S(1)} %copy-done.2, bf16[8,128,512]{2,1,0:T(8,128)(2,1)} %pieces.2.refs_3_), custom_call_target="tpu_custom_call" | custom-call | tf_op jit(solution)/shard_map/outward/pallas_call | solution.py:344
  4.3 0.7 collective-permute-start
  5.0 4.2 %all-to-all-start = ((bf16[8,128,512]{2,1,0:T(8,128)(2,1)}), bf16[8,128,512]{2,1,0:T(8,128)(2,1)}, u32[]{:S(2)}, u32[]{:S(2)}) async-start(bf16[8,128,512]{2,1,0:T(8,128)(2,1)} %pieces.2.refs_3_), calls=%async_computation | async-start | bytes 2097152 | tf_op jit(solution)/shard_map/all_to_all | solution.py:381
  9.3 0.1 convert_element_type.21
  9.5 2.8 %parcels.2 = (bf16[2,256,512]{2,1,0:T(8,128)(2,1)}, bf16[2,256,512]{2,1,0:T(8,128)(2,1)}, bf16[2,272,512]{2,1,0:T(8,128)(2,1)}, bf16[2,256,512]{2,1,0:T(8,128)(2,1)}) custom-call(s32[4,2]{1,0:T(4,128)S(1)} %get-tuple-element.58.refs_0_.columns_ref, s32[3]{0:T(128)S(1)} %pad_add_fusion.1.refs_1_.place_ref.refs_0_, bf16[128,4096]{1,0:T(8,128)(2,1)S(1)} %copy-done.1, ...), custom_call_target="tpu_custom_call" | custom-call | tf_op jit(solution)/shard_map/parcels/pallas_call | solution.py:353
  12.3 1.4 %collective-permute-start.2 = (bf16[2,272,512]{2,1,0:T(8,128)(2,1)}, bf16[2,272,512]{2,1,0:T(8,128)(2,1)S(1)}, u32[]{:S(2)}, u32[]{:S(2)}) collective-permute-start(bf16[2,272,512]{2,1,0:T(8,128)(2,1)} %get-tuple-element.31), channel_id=1, source_target_pairs={{0,4},{1,5},{2,6},{3,7},{4,0},{5,1},{6,2},{7,3},{8,12},{9,13},{10,... | collective-permute-start | bytes 1671176 | tf_op jit(solution)/shard_map/ppermute | solution.py:366
  13.7 1.4 %outward.3 = bf16[4,128,512]{2,1,0:T(8,128)(2,1)} custom-call(s32[4,2]{1,0:T(4,128)S(1)} %get-tuple-element.58.refs_0_.columns_ref, bf16[128,4096]{1,0:T(8,128)(2,1)S(1)} %copy-done.3), custom_call_target="tpu_custom_call" | custom-call | tf_op jit(solution)/shard_map/outward/pallas_call | solution.py:344
  15.1 0.7 collective-permute-start.5
  15.8 1.2 collective-permute-start.1
  17.0 5.8 %all-to-all-done = bf16[8,128,512]{2,1,0:T(8,128)(2,1)} async-done(((bf16[8,128,512]{2,1,0:T(8,128)(2,1)}), bf16[8,128,512]{2,1,0:T(8,128)(2,1)}, u32[]{:S(2)}, u32[]{:S(2)}) %all-to-all-start) | async-done | bytes 1048608 | tf_op jit(solution)/shard_map/all_to_all | solution.py:381
  22.9 3.2 %collective-permute-start.4 = (bf16[8,128,512]{2,1,0:T(8,128)(2,1)}, bf16[8,128,512]{2,1,0:T(8,128)(2,1)}, u32[]{:S(2)}, u32[]{:S(2)}) collective-permute-start(bf16[8,128,512]{2,1,0:T(8,128)(2,1)} %all-to-all-done), channel_id=1, source_target_pairs={{0,8},{8,16},{16,24},{1,9},{9,17},{17,25},{2,10},{10,18},{18,26},{... | collective-permute-start | bytes 3145736 | tf_op jit(solution)/shard_map/ppermute | solution.py:384
  26.1 8.0 %collective-permute-done.1.refs_1_.refs_4_.refs_8_ = bf16[2,256,512]{2,1,0:T(8,128)(2,1)S(1)} collective-permute-done((bf16[2,256,512]{2,1,0:T(8,128)(2,1)}, bf16[2,256,512]{2,1,0:T(8,128)(2,1)S(1)}, u32[]{:S(2)}, u32[]{:S(2)}) %collective-permute-start.1) | collective-permute-done | bytes 524320 | tf_op jit(solution)/shard_map/ppermute | solution.py:366
  34.1 0.7 collective-permute-done.2.refs_2_.refs_5_.refs_9_
  34.8 2.4 %parcels.3 = (bf16[2,128,512]{2,1,0:T(8,128)(2,1)}, bf16[2,128,512]{2,1,0:T(8,128)(2,1)}, bf16[2,128,512]{2,1,0:T(8,128)(2,1)}, bf16[2,128,512]{2,1,0:T(8,128)(2,1)}) custom-call(s32[4,2]{1,0:T(4,128)S(1)} %get-tuple-element.58.refs_0_.columns_ref, s32[3]{0:T(128)S(1)} %pad_add_fusion.1.refs_1_.place_ref.refs_0_, bf16[128,4096]{1,0:T(8,128)(2,1)S(1)} %copy-done.3, ...), custom_call_target="tpu_custom_call" | custom-call | tf_op jit(solution)/shard_map/parcels/pallas_call | solution.py:353
  37.2 1.3 %collective-permute-start.6 = (bf16[2,128,512]{2,1,0:T(8,128)(2,1)}, bf16[2,128,512]{2,1,0:T(8,128)(2,1)S(1)}, u32[]{:S(2)}, u32[]{:S(2)}) collective-permute-start(bf16[2,128,512]{2,1,0:T(8,128)(2,1)} %get-tuple-element.37), channel_id=1, source_target_pairs={{0,2},{1,3},{2,0},{3,1},{4,6},{5,7},{6,4},{7,5},{8,10},{9,11},{10,... | collective-permute-start | bytes 786440 | tf_op jit(solution)/shard_map/ppermute | solution.py:366
  38.5 0.3 collective-permute-start.7
  38.7 1.2 collective-permute-start.8
  39.9 7.1 %collective-permute-done.3.refs_3_.refs_10_ = bf16[2,256,512]{2,1,0:T(8,128)(2,1)} collective-permute-done((bf16[2,256,512]{2,1,0:T(8,128)(2,1)}, bf16[2,256,512]{2,1,0:T(8,128)(2,1)}, u32[]{:S(2)}, u32[]{:S(2)}) %collective-permute-start.3) | collective-permute-done | bytes 524320 | tf_op jit(solution)/shard_map/ppermute | solution.py:366
  47.0 4.0 %state.1 = (bf16[4,144,128]{2,1,0:T(8,128)(2,1)S(1)}, bf16[4,8,256,128]{3,2,1,0:T(8,128)(2,1)S(1)}, f32[32,128]{1,0:T(8,128)S(1)}, f32[2,1,512]{2,1,0:T(1,128)S(1)}) custom-call(s32[3]{0:T(128)S(1)} %pad_add_fusion.1.refs_1_.place_ref.refs_0_, f32[5,512]{1,0:T(8,128)S(1)} %get-tuple-element.56.table_ref, bf16[2,256,512]{2,1,0:T(8,128)(2,1)S(1)} %copy-done.14, ...), custom_call_target="tpu_custom_call" | custom-call | tf_op jit(solution)/shard_map/state/pallas_call | solution.py:401
  51.0 1.3 %collective-permute-start.10 = (bf16[4,144,128]{2,1,0:T(8,128)(2,1)S(1)}, bf16[4,144,128]{2,1,0:T(8,128)(2,1)S(1)}, u32[]{:S(2)}, u32[]{:S(2)}) collective-permute-start(bf16[4,144,128]{2,1,0:T(8,128)(2,1)S(1)} %get-tuple-element.41), channel_id=1, source_target_pairs={{0,16},{8,24},{1,17},{9,25},{2,18},{10,26},{3,19},{11,27},{4,20},{... | collective-permute-start | bytes 442376 | tf_op jit(solution)/shard_map/ppermute | solution.py:384
  52.3 0.8 collective-permute-done.6.refs_4_
  53.2 0.7 collective-permute-start.11
  53.9 3.8 %collective-permute-start.9 = (bf16[4,144,128]{2,1,0:T(8,128)(2,1)S(1)}, bf16[4,144,128]{2,1,0:T(8,128)(2,1)S(1)}, u32[]{:S(2)}, u32[]{:S(2)}) collective-permute-start(bf16[4,144,128]{2,1,0:T(8,128)(2,1)S(1)} %get-tuple-element.41), channel_id=1, source_target_pairs={{0,8},{8,16},{16,24},{1,9},{9,17},{17,25},{2,10},{10,18},{18,26},{... | collective-permute-start | bytes 442376 | tf_op jit(solution)/shard_map/ppermute | solution.py:384
  57.7 0.4 collective-permute-done.8.refs_6_
  58.1 1.1 copy-done.5
  59.2 1.0 copy-done.7
  60.2 1.0 copy-done.15
  61.3 4.7 %inside.1 = (f32[8,128,512]{2,1,0:T(8,128)S(1)}, bf16[8,128,512]{2,1,0:T(8,128)(2,1)S(1)}) custom-call(s32[3]{0:T(128)S(1)} %pad_add_fusion.1.refs_1_.place_ref.refs_0_, f32[32,128]{1,0:T(8,128)S(1)} %get-tuple-element.34.refs_1_.decay_ref, bf16[4,8,256,128]{3,2,1,0:T(8,128)(2,1)S(1)} %get-tuple-element.35.refs_2_, bf16[2,128,512]{2,1,0:T(8,128)(2,1)S(1)} %copy-done.18, ...), custom_call_target="tpu_custom_call" | custom-call | flops 2147483648 | bytes 6291456 | tf_op jit(solution)/shard_map/inside/pallas_call | solution.py:419
  66.1 1.0 copy-done.10
  67.0 2.0 %collective-permute-done.9.refs_1_.refs_0_ = bf16[4,144,128]{2,1,0:T(8,128)(2,1)S(1)} collective-permute-done((bf16[4,144,128]{2,1,0:T(8,128)(2,1)S(1)}, bf16[4,144,128]{2,1,0:T(8,128)(2,1)S(1)}, u32[]{:S(2)}, u32[]{:S(2)}) %collective-permute-start.9) | collective-permute-done | bytes 147488 | tf_op jit(solution)/shard_map/ppermute | solution.py:384
  69.0 1.1 pieces.3
  70.1 4.1 %all-to-all-start.1 = ((bf16[8,128,512]{2,1,0:T(8,128)(2,1)}), bf16[8,128,512]{2,1,0:T(8,128)(2,1)S(1)}, u32[]{:S(2)}, u32[]{:S(2)}) async-start(bf16[8,128,512]{2,1,0:T(8,128)(2,1)} %pieces.3), calls=%async_computation.1 | async-start | bytes 2097152 | tf_op jit(solution)/shard_map/all_to_all | solution.py:381
  74.2 0.1 add.79.order_ref
  74.3 1.2 copy-done.11
  75.5 0.9 copy-done.13
  76.4 4.1 %first.1 = (bf16[8,128,256]{2,1,0:T(8,128)(2,1)}, bf16[8,128,256]{2,1,0:T(8,128)(2,1)}) custom-call(f32[8,128,512]{2,1,0:T(8,128)S(1)} %get-tuple-element.40.refs_0_.raw_ref, bf16[8,128,512]{2,1,0:T(8,128)(2,1)S(1)} %copy-done.11, f32[32,128]{1,0:T(8,128)S(1)} %get-tuple-element.34.refs_1_.decay_ref, f32[4,128]{1,0:T(4,128)S(1)} %constant_dynamic-slice_fusion.gain_ref, ...), custom_call_target="tpu_custom_call" | custom-call | tf_op jit(solution)/shard_map/first/pallas_call | solution.py:433
  80.5 2.3 %collective-permute-start.20 = (bf16[8,128,256]{2,1,0:T(8,128)(2,1)}, bf16[8,128,256]{2,1,0:T(8,128)(2,1)S(1)}, u32[]{:S(2)}, u32[]{:S(2)}) collective-permute-start(bf16[8,128,256]{2,1,0:T(8,128)(2,1)} %get-tuple-element.48), channel_id=1, source_target_pairs={{0,8},{8,16},{16,24},{1,9},{9,17},{17,25},{2,10},{10,18},{18,26},{... | collective-permute-start | bytes 1572872 | tf_op jit(solution)/shard_map/ppermute | solution.py:384
  83.1 0.1 reshape.98.bias_ref
  83.2 2.1 %collective-permute-start.12 = (bf16[8,128,256]{2,1,0:T(8,128)(2,1)}, bf16[8,128,256]{2,1,0:T(8,128)(2,1)S(1)}, u32[]{:S(2)}, u32[]{:S(2)}) collective-permute-start(bf16[8,128,256]{2,1,0:T(8,128)(2,1)} %get-tuple-element.43), channel_id=1, source_target_pairs={{0,8},{8,16},{16,24},{1,9},{9,17},{17,25},{2,10},{10,18},{18,26},{... | collective-permute-start | bytes 1572872 | tf_op jit(solution)/shard_map/ppermute | solution.py:384
  85.4 2.5 %all-to-all-done.1 = bf16[8,128,512]{2,1,0:T(8,128)(2,1)S(1)} async-done(((bf16[8,128,512]{2,1,0:T(8,128)(2,1)}), bf16[8,128,512]{2,1,0:T(8,128)(2,1)S(1)}, u32[]{:S(2)}, u32[]{:S(2)}) %all-to-all-start.1) | async-done | bytes 1048608 | tf_op jit(solution)/shard_map/all_to_all | solution.py:381
  87.8 7.8 %weights.1.weights_ref = bf16[4,1024,512]{2,1,0:T(8,128)(2,1)S(1)} custom-call(s32[16,8]{1,0:T(8,128)S(1)} %select_n.57.window_ref, bf16[1024,512]{1,0:T(8,128)(2,1)} %bitcast.4.own_ref, bf16[1024,512]{1,0:T(8,128)(2,1)} %bitcast.5.earlier_ref, f32[16,512]{1,0:T(8,128)S(1)} %reshape.98.bias_ref, bf16[1024,512]{1,0:T(8,128)(2,1)S(1)} %bitcast.14), custom_call_target="tpu_custom_call" | custom-call | flops 2147483648 | bytes 8388608 | tf_op jit(solution)/shard_map/weights/pallas_call | solution.py:449
  95.6 0.5 collective-permute-done.20
  96.2 3.3 %sum.3 = (bf16[2,128,256]{2,1,0:T(8,128)(2,1)S(1)}, bf16[2,128,256]{2,1,0:T(8,128)(2,1)S(1)}, bf16[2,128,256]{2,1,0:T(8,128)(2,1)S(1)}, bf16[2,128,256]{2,1,0:T(8,128)(2,1)S(1)}) custom-call(s32[8]{0:T(128)S(1)} %add.79.order_ref, s32[16,8]{1,0:T(8,128)S(1)} %select_n.57.window_ref, bf16[4,1024,512]{2,1,0:T(8,128)(2,1)S(1)} %weights.1.weights_ref, ...), custom_call_target="tpu_custom_call" | custom-call | tf_op jit(solution)/shard_map/sum/pallas_call | solution.py:474
  99.5 1.1 collective-permute-start.22
  100.6 1.2 collective-permute-start.24
  101.8 0.4 collective-permute-start.26
  102.2 2.2 %collective-permute-start.21 = (bf16[2,128,256]{2,1,0:T(8,128)(2,1)S(1)}, bf16[2,128,256]{2,1,0:T(8,128)(2,1)S(1)}, u32[]{:S(2)}, u32[]{:S(2)}) collective-permute-start(bf16[2,128,256]{2,1,0:T(8,128)(2,1)S(1)} %get-tuple-element.49.refs_8_), channel_id=1, source_target_pairs={{0,1},{1,0},{2,3},{3,2},{4,5},{5,4},{6,7},{7,6},{8,9},{9,8},{10,11... | collective-permute-start | bytes 393224 | tf_op jit(solution)/shard_map/ppermute | solution.py:338
  104.4 3.0 %collective-permute-done.12 = bf16[8,128,256]{2,1,0:T(8,128)(2,1)S(1)} collective-permute-done((bf16[8,128,256]{2,1,0:T(8,128)(2,1)}, bf16[8,128,256]{2,1,0:T(8,128)(2,1)S(1)}, u32[]{:S(2)}, u32[]{:S(2)}) %collective-permute-start.12) | collective-permute-done | bytes 524320 | tf_op jit(solution)/shard_map/ppermute | solution.py:384
  107.4 3.3 %sum.2 = (bf16[2,128,256]{2,1,0:T(8,128)(2,1)S(1)}, bf16[2,128,256]{2,1,0:T(8,128)(2,1)S(1)}, bf16[2,128,256]{2,1,0:T(8,128)(2,1)S(1)}, bf16[2,128,256]{2,1,0:T(8,128)(2,1)S(1)}) custom-call(s32[8]{0:T(128)S(1)} %add.79.order_ref, s32[16,8]{1,0:T(8,128)S(1)} %select_n.57.window_ref, bf16[4,1024,512]{2,1,0:T(8,128)(2,1)S(1)} %weights.1.weights_ref, ...), custom_call_target="tpu_custom_call" | custom-call | tf_op jit(solution)/shard_map/sum/pallas_call | solution.py:474
  110.7 1.1 collective-permute-start.14
  111.8 1.2 collective-permute-start.16
  113.0 0.4 collective-permute-start.18
  113.4 1.7 %collective-permute-start.13 = (bf16[2,128,256]{2,1,0:T(8,128)(2,1)S(1)}, bf16[2,128,256]{2,1,0:T(8,128)(2,1)S(1)}, u32[]{:S(2)}, u32[]{:S(2)}) collective-permute-start(bf16[2,128,256]{2,1,0:T(8,128)(2,1)S(1)} %get-tuple-element.44.refs_0_), channel_id=1, source_target_pairs={{0,1},{1,0},{2,3},{3,2},{4,5},{5,4},{6,7},{7,6},{8,9},{9,8},{10,11... | collective-permute-start | bytes 393224 | tf_op jit(solution)/shard_map/ppermute | solution.py:338
  115.2 1.5 %collective-permute-start.25 = (bf16[2,128,256]{2,1,0:T(8,128)(2,1)S(1)}, bf16[2,128,256]{2,1,0:T(8,128)(2,1)S(1)}, u32[]{:S(2)}, u32[]{:S(2)}) collective-permute-start(bf16[2,128,256]{2,1,0:T(8,128)(2,1)S(1)} %collective-permute-done.24.refs_12_), channel_id=1, source_target_pairs={{0,1},{1,0},{2,3},{3,2},{4,5},{5,4},{6,7},{7,6},{8,9},{9,8},{10,11... | collective-permute-start | bytes 393224 | tf_op jit(solution)/shard_map/ppermute | solution.py:338
  116.7 2.4 %collective-permute-start.27 = (bf16[2,128,256]{2,1,0:T(8,128)(2,1)S(1)}, bf16[2,128,256]{2,1,0:T(8,128)(2,1)S(1)}, u32[]{:S(2)}, u32[]{:S(2)}) collective-permute-start(bf16[2,128,256]{2,1,0:T(8,128)(2,1)S(1)} %collective-permute-done.26.refs_14_), channel_id=1, source_target_pairs={{0,1},{1,0},{2,3},{3,2},{4,5},{5,4},{6,7},{7,6},{8,9},{9,8},{10,11... | collective-permute-start | bytes 393224 | tf_op jit(solution)/shard_map/ppermute | solution.py:338
  119.2 0.1 collective-permute-done.18.refs_6_
  119.3 1.6 %collective-permute-start.15 = (bf16[2,128,256]{2,1,0:T(8,128)(2,1)S(1)}, bf16[2,128,256]{2,1,0:T(8,128)(2,1)S(1)}, u32[]{:S(2)}, u32[]{:S(2)}) collective-permute-start(bf16[2,128,256]{2,1,0:T(8,128)(2,1)S(1)} %collective-permute-done.14.refs_2_), channel_id=1, source_target_pairs={{0,1},{1,0},{2,3},{3,2},{4,5},{5,4},{6,7},{7,6},{8,9},{9,8},{10,11... | collective-permute-start | bytes 393224 | tf_op jit(solution)/shard_map/ppermute | solution.py:338
  120.9 0.5 collective-permute-start.19
  121.4 0.5 collective-permute-done.15.refs_3_
  121.9 0.4 collective-permute-done.17.refs_5_
  122.3 0.2 collective-permute-done.19.refs_7_
  122.4 1.7 %join.1 = bf16[128,4096]{1,0:T(8,128)(2,1)} custom-call(s32[4,2]{1,0:T(4,128)S(1)} %get-tuple-element.58.refs_0_.columns_ref, bf16[2,128,256]{2,1,0:T(8,128)(2,1)S(1)} %get-tuple-element.44.refs_0_, bf16[2,128,256]{2,1,0:T(8,128)(2,1)S(1)} %collective-permute-done.13.refs_1_, bf16[2,128,256]{2,1,0:T(8,128)(2,1)S(1)} %collective-permute-done.14.refs_2_, ...), custom_call_target="tpu_custom_call" | custom-call | tf_op jit(solution)/shard_map/join/pallas_call | solution.py:501
  (69 shorter events, 0.7 us)
Async XLA Ops:
  0.0 74.3 %copy-start = (f32[8,128]{1,0:T(8,128)S(1)}, f32[8,128]{1,0:T(8,128)}, u32[]{:S(2)}) copy-start(f32[8,128]{1,0:T(8,128)} %param.14) | copy-start | bytes 12292
  0.0 2.6 %copy-start.2 = (bf16[128,4096]{1,0:T(8,128)(2,1)S(1)}, bf16[128,4096]{1,0:T(8,128)(2,1)}, u32[]{:S(2)}) copy-start(bf16[128,4096]{1,0:T(8,128)(2,1)} %refs_3_.1) | copy-start | bytes 3145732
  0.0 2.6 %copy-start.1 = (bf16[128,4096]{1,0:T(8,128)(2,1)S(1)}, bf16[128,4096]{1,0:T(8,128)(2,1)}, u32[]{:S(2)}) copy-start(bf16[128,4096]{1,0:T(8,128)(2,1)} %refs_2_.4) | copy-start | bytes 3145732
  0.1 1.4 %copy-start.8 = (bf16[128,4096]{1,0:T(8,128)(2,1)S(1)}, bf16[128,4096]{1,0:T(8,128)(2,1)}, u32[]{:S(2)}) copy-start(bf16[128,4096]{1,0:T(8,128)(2,1)} %in_ref.2) | copy-start | bytes 3145732
  4.3 5.0 %copy-start.20 = (s32[8,8]{1,0:T(8,128)S(1)}, s32[8,8]{1,0:T(8,128)}, u32[]{:S(2)}) copy-start(s32[8,8]{1,0:T(8,128)} %param.15) | copy-start | bytes 772
  4.3 5.2 %copy-start.19 = (f32[8,512]{1,0:T(8,128)S(1)}, f32[8,512]{1,0:T(8,128)}, u32[]{:S(2)}) copy-start(f32[8,512]{1,0:T(8,128)} %param.13) | copy-start | bytes 49156
  4.3 5.2 %collective-permute-start = (bf16[4,256,512]{2,1,0:T(8,128)(2,1)}, bf16[4,256,512]{2,1,0:T(8,128)(2,1)}, u32[]{:S(2)}, u32[]{:S(2)}) collective-permute-start(bf16[4,256,512]{2,1,0:T(8,128)(2,1)} %outward.2), channel_id=1, source_target_pairs={{0,1},{1,0},{2,3},{3,2},{4,5},{5,4},{6,7},{7,6},{8,9},{9,8},{10,11... | collective-permute-start | bytes 3145736 | tf_op jit(solution)/shard_map/ppermute | solution.py:338
  5.0 17.9 %all-to-all-start = ((bf16[8,128,512]{2,1,0:T(8,128)(2,1)}), bf16[8,128,512]{2,1,0:T(8,128)(2,1)}, u32[]{:S(2)}, u32[]{:S(2)}) async-start(bf16[8,128,512]{2,1,0:T(8,128)(2,1)} %pieces.2.refs_3_), calls=%async_computation | async-start | bytes 2097152 | tf_op jit(solution)/shard_map/all_to_all | solution.py:381
  9.2 4.5 %copy-start.3 = (bf16[128,4096]{1,0:T(8,128)(2,1)S(1)}, bf16[128,4096]{1,0:T(8,128)(2,1)}, u32[]{:S(2)}) copy-start(bf16[128,4096]{1,0:T(8,128)(2,1)} %refs_2_.5) | copy-start | bytes 3145732
  12.3 34.7 %copy-start.14 = (bf16[2,256,512]{2,1,0:T(8,128)(2,1)S(1)}, bf16[2,256,512]{2,1,0:T(8,128)(2,1)}, u32[]{:S(2)}) copy-start(bf16[2,256,512]{2,1,0:T(8,128)(2,1)} %get-tuple-element.29.refs_0_.refs_7_) | copy-start | bytes 1572868
  12.3 22.5 %collective-permute-start.2 = (bf16[2,272,512]{2,1,0:T(8,128)(2,1)}, bf16[2,272,512]{2,1,0:T(8,128)(2,1)S(1)}, u32[]{:S(2)}, u32[]{:S(2)}) collective-permute-start(bf16[2,272,512]{2,1,0:T(8,128)(2,1)} %get-tuple-element.31), channel_id=1, source_target_pairs={{0,4},{1,5},{2,6},{3,7},{4,0},{5,1},{6,2},{7,3},{8,12},{9,13},{10,... | collective-permute-start | bytes 1671176 | tf_op jit(solution)/shard_map/ppermute | solution.py:366
  15.1 11.0 %collective-permute-start.5 = (bf16[4,128,512]{2,1,0:T(8,128)(2,1)}, bf16[4,128,512]{2,1,0:T(8,128)(2,1)}, u32[]{:S(2)}, u32[]{:S(2)}) collective-permute-start(bf16[4,128,512]{2,1,0:T(8,128)(2,1)} %outward.3), channel_id=1, source_target_pairs={{0,1},{1,0},{2,3},{3,2},{4,5},{5,4},{6,7},{7,6},{8,9},{9,8},{10,11... | collective-permute-start | bytes 1572872 | tf_op jit(solution)/shard_map/ppermute | solution.py:338
  15.8 18.3 %collective-permute-start.1 = (bf16[2,256,512]{2,1,0:T(8,128)(2,1)}, bf16[2,256,512]{2,1,0:T(8,128)(2,1)S(1)}, u32[]{:S(2)}, u32[]{:S(2)}) collective-permute-start(bf16[2,256,512]{2,1,0:T(8,128)(2,1)} %get-tuple-element.30), channel_id=1, source_target_pairs={{0,2},{1,3},{2,0},{3,1},{4,6},{5,7},{6,4},{7,5},{8,10},{9,11},{10,... | collective-permute-start | bytes 1572872 | tf_op jit(solution)/shard_map/ppermute | solution.py:366
  17.0 30.0 %collective-permute-start.3 = (bf16[2,256,512]{2,1,0:T(8,128)(2,1)}, bf16[2,256,512]{2,1,0:T(8,128)(2,1)}, u32[]{:S(2)}, u32[]{:S(2)}) collective-permute-start(bf16[2,256,512]{2,1,0:T(8,128)(2,1)} %get-tuple-element.32), channel_id=1, source_target_pairs={{0,6},{1,7},{2,4},{3,5},{4,2},{5,3},{6,0},{7,1},{8,14},{9,15},{10,... | collective-permute-start | bytes 1572872 | tf_op jit(solution)/shard_map/ppermute | solution.py:366
  22.9 51.4 %collective-permute-start.4 = (bf16[8,128,512]{2,1,0:T(8,128)(2,1)}, bf16[8,128,512]{2,1,0:T(8,128)(2,1)}, u32[]{:S(2)}, u32[]{:S(2)}) collective-permute-start(bf16[8,128,512]{2,1,0:T(8,128)(2,1)} %all-to-all-done), channel_id=1, source_target_pairs={{0,8},{8,16},{16,24},{1,9},{9,17},{17,25},{2,10},{10,18},{18,26},{... | collective-permute-start | bytes 3145736 | tf_op jit(solution)/shard_map/ppermute | solution.py:384
  34.1 16.9 %copy-start.6 = (bf16[2,256,512]{2,1,0:T(8,128)(2,1)}, bf16[2,256,512]{2,1,0:T(8,128)(2,1)S(1)}, u32[]{:S(2)}) copy-start(bf16[2,256,512]{2,1,0:T(8,128)(2,1)S(1)} %collective-permute-done.1.refs_1_.refs_4_.refs_8_) | copy-start | bytes 1572868
  34.8 16.2 %copy-start.4 = (bf16[2,272,512]{2,1,0:T(8,128)(2,1)}, bf16[2,272,512]{2,1,0:T(8,128)(2,1)S(1)}, u32[]{:S(2)}) copy-start(bf16[2,272,512]{2,1,0:T(8,128)(2,1)S(1)} %collective-permute-done.2.refs_2_.refs_5_.refs_9_) | copy-start | bytes 1671172
  37.2 21.0 %copy-start.18 = (bf16[2,128,512]{2,1,0:T(8,128)(2,1)S(1)}, bf16[2,128,512]{2,1,0:T(8,128)(2,1)}, u32[]{:S(2)}) copy-start(bf16[2,128,512]{2,1,0:T(8,128)(2,1)} %get-tuple-element.36.refs_3_) | copy-start | bytes 786436
  37.2 16.0 %collective-permute-start.6 = (bf16[2,128,512]{2,1,0:T(8,128)(2,1)}, bf16[2,128,512]{2,1,0:T(8,128)(2,1)S(1)}, u32[]{:S(2)}, u32[]{:S(2)}) collective-permute-start(bf16[2,128,512]{2,1,0:T(8,128)(2,1)} %get-tuple-element.37), channel_id=1, source_target_pairs={{0,2},{1,3},{2,0},{3,1},{4,6},{5,7},{6,4},{7,5},{8,10},{9,11},{10,... | collective-permute-start | bytes 786440 | tf_op jit(solution)/shard_map/ppermute | solution.py:366
  38.5 15.4 %collective-permute-start.7 = (bf16[2,128,512]{2,1,0:T(8,128)(2,1)}, bf16[2,128,512]{2,1,0:T(8,128)(2,1)S(1)}, u32[]{:S(2)}, u32[]{:S(2)}) collective-permute-start(bf16[2,128,512]{2,1,0:T(8,128)(2,1)} %get-tuple-element.38), channel_id=1, source_target_pairs={{0,4},{1,5},{2,6},{3,7},{4,0},{5,1},{6,2},{7,3},{8,12},{9,13},{10,... | collective-permute-start | bytes 786440 | tf_op jit(solution)/shard_map/ppermute | solution.py:366
  38.7 19.4 %collective-permute-start.8 = (bf16[2,128,512]{2,1,0:T(8,128)(2,1)}, bf16[2,128,512]{2,1,0:T(8,128)(2,1)S(1)}, u32[]{:S(2)}, u32[]{:S(2)}) collective-permute-start(bf16[2,128,512]{2,1,0:T(8,128)(2,1)} %get-tuple-element.39), channel_id=1, source_target_pairs={{0,6},{1,7},{2,4},{3,5},{4,2},{5,3},{6,0},{7,1},{8,14},{9,15},{10,... | collective-permute-start | bytes 786440 | tf_op jit(solution)/shard_map/ppermute | solution.py:366
  51.0 16.0 %collective-permute-start.10 = (bf16[4,144,128]{2,1,0:T(8,128)(2,1)S(1)}, bf16[4,144,128]{2,1,0:T(8,128)(2,1)S(1)}, u32[]{:S(2)}, u32[]{:S(2)}) collective-permute-start(bf16[4,144,128]{2,1,0:T(8,128)(2,1)S(1)} %get-tuple-element.41), channel_id=1, source_target_pairs={{0,16},{8,24},{1,17},{9,25},{2,18},{10,26},{3,19},{11,27},{4,20},{... | collective-permute-start | bytes 442376 | tf_op jit(solution)/shard_map/ppermute | solution.py:384
  53.2 13.8 %collective-permute-start.11 = (bf16[4,144,128]{2,1,0:T(8,128)(2,1)S(1)}, bf16[4,144,128]{2,1,0:T(8,128)(2,1)S(1)}, u32[]{:S(2)}, u32[]{:S(2)}) collective-permute-start(bf16[4,144,128]{2,1,0:T(8,128)(2,1)S(1)} %get-tuple-element.41), channel_id=1, source_target_pairs={{0,24},{1,25},{2,26},{3,27},{4,28},{5,29},{6,30},{7,31}} | collective-permute-start | bytes 442376 | tf_op jit(solution)/shard_map/ppermute | solution.py:384
  53.9 15.1 %collective-permute-start.9 = (bf16[4,144,128]{2,1,0:T(8,128)(2,1)S(1)}, bf16[4,144,128]{2,1,0:T(8,128)(2,1)S(1)}, u32[]{:S(2)}, u32[]{:S(2)}) collective-permute-start(bf16[4,144,128]{2,1,0:T(8,128)(2,1)S(1)} %get-tuple-element.41), channel_id=1, source_target_pairs={{0,8},{8,16},{16,24},{1,9},{9,17},{17,25},{2,10},{10,18},{18,26},{... | collective-permute-start | bytes 442376 | tf_op jit(solution)/shard_map/ppermute | solution.py:384
  58.1 1.1 copy-start.5
  59.2 1.0 copy-start.7
  60.2 1.0 copy-start.15
  61.3 7.7 %copy-start.9 = (bf16[128,4096]{1,0:T(8,128)(2,1)S(1)}, bf16[128,4096]{1,0:T(8,128)(2,1)}, u32[]{:S(2)}) copy-start(bf16[128,4096]{1,0:T(8,128)(2,1)} %in_ref.3) | copy-start | bytes 3145732
  66.0 1.0 copy-start.10
  69.0 1.1 copy-start.12
  70.1 17.7 %all-to-all-start.1 = ((bf16[8,128,512]{2,1,0:T(8,128)(2,1)}), bf16[8,128,512]{2,1,0:T(8,128)(2,1)S(1)}, u32[]{:S(2)}, u32[]{:S(2)}) async-start(bf16[8,128,512]{2,1,0:T(8,128)(2,1)} %pieces.3), calls=%async_computation.1 | async-start | bytes 2097152 | tf_op jit(solution)/shard_map/all_to_all | solution.py:381
  74.3 1.2 copy-start.11
  75.5 0.9 copy-start.13
  80.5 15.6 %collective-permute-start.20 = (bf16[8,128,256]{2,1,0:T(8,128)(2,1)}, bf16[8,128,256]{2,1,0:T(8,128)(2,1)S(1)}, u32[]{:S(2)}, u32[]{:S(2)}) collective-permute-start(bf16[8,128,256]{2,1,0:T(8,128)(2,1)} %get-tuple-element.48), channel_id=1, source_target_pairs={{0,8},{8,16},{16,24},{1,9},{9,17},{17,25},{2,10},{10,18},{18,26},{... | collective-permute-start | bytes 1572872 | tf_op jit(solution)/shard_map/ppermute | solution.py:384
  83.2 24.2 %collective-permute-start.12 = (bf16[8,128,256]{2,1,0:T(8,128)(2,1)}, bf16[8,128,256]{2,1,0:T(8,128)(2,1)S(1)}, u32[]{:S(2)}, u32[]{:S(2)}) collective-permute-start(bf16[8,128,256]{2,1,0:T(8,128)(2,1)} %get-tuple-element.43), channel_id=1, source_target_pairs={{0,8},{8,16},{16,24},{1,9},{9,17},{17,25},{2,10},{10,18},{18,26},{... | collective-permute-start | bytes 1572872 | tf_op jit(solution)/shard_map/ppermute | solution.py:384
  87.8 8.3 %copy-start.17 = (bf16[8,128,256]{2,1,0:T(8,128)(2,1)S(1)}, bf16[8,128,256]{2,1,0:T(8,128)(2,1)}, u32[]{:S(2)}) copy-start(bf16[8,128,256]{2,1,0:T(8,128)(2,1)} %get-tuple-element.48) | copy-start | bytes 1572868
  96.1 11.2 %copy-start.16 = (bf16[8,128,256]{2,1,0:T(8,128)(2,1)S(1)}, bf16[8,128,256]{2,1,0:T(8,128)(2,1)}, u32[]{:S(2)}) copy-start(bf16[8,128,256]{2,1,0:T(8,128)(2,1)} %get-tuple-element.43) | copy-start | bytes 1572868
  99.5 12.3 %collective-permute-start.22 = (bf16[2,128,256]{2,1,0:T(8,128)(2,1)S(1)}, bf16[2,128,256]{2,1,0:T(8,128)(2,1)S(1)}, u32[]{:S(2)}, u32[]{:S(2)}) collective-permute-start(bf16[2,128,256]{2,1,0:T(8,128)(2,1)S(1)} %get-tuple-element.50), channel_id=1, source_target_pairs={{0,2},{1,3},{2,0},{3,1},{4,6},{5,7},{6,4},{7,5},{8,10},{9,11},{10,... | collective-permute-start | bytes 393224 | tf_op jit(solution)/shard_map/ppermute | solution.py:499
  100.6 12.4 %collective-permute-start.24 = (bf16[2,128,256]{2,1,0:T(8,128)(2,1)S(1)}, bf16[2,128,256]{2,1,0:T(8,128)(2,1)S(1)}, u32[]{:S(2)}, u32[]{:S(2)}) collective-permute-start(bf16[2,128,256]{2,1,0:T(8,128)(2,1)S(1)} %get-tuple-element.51), channel_id=1, source_target_pairs={{0,4},{1,5},{2,6},{3,7},{4,0},{5,1},{6,2},{7,3},{8,12},{9,13},{10,... | collective-permute-start | bytes 393224 | tf_op jit(solution)/shard_map/ppermute | solution.py:499
  101.8 11.6 %collective-permute-start.26 = (bf16[2,128,256]{2,1,0:T(8,128)(2,1)S(1)}, bf16[2,128,256]{2,1,0:T(8,128)(2,1)S(1)}, u32[]{:S(2)}, u32[]{:S(2)}) collective-permute-start(bf16[2,128,256]{2,1,0:T(8,128)(2,1)S(1)} %get-tuple-element.52), channel_id=1, source_target_pairs={{0,6},{1,7},{2,4},{3,5},{4,2},{5,3},{6,0},{7,1},{8,14},{9,15},{10,... | collective-permute-start | bytes 393224 | tf_op jit(solution)/shard_map/ppermute | solution.py:499
  102.2 13.0 %collective-permute-start.21 = (bf16[2,128,256]{2,1,0:T(8,128)(2,1)S(1)}, bf16[2,128,256]{2,1,0:T(8,128)(2,1)S(1)}, u32[]{:S(2)}, u32[]{:S(2)}) collective-permute-start(bf16[2,128,256]{2,1,0:T(8,128)(2,1)S(1)} %get-tuple-element.49.refs_8_), channel_id=1, source_target_pairs={{0,1},{1,0},{2,3},{3,2},{4,5},{5,4},{6,7},{7,6},{8,9},{9,8},{10,11... | collective-permute-start | bytes 393224 | tf_op jit(solution)/shard_map/ppermute | solution.py:338
  110.7 4.5 %collective-permute-start.14 = (bf16[2,128,256]{2,1,0:T(8,128)(2,1)S(1)}, bf16[2,128,256]{2,1,0:T(8,128)(2,1)S(1)}, u32[]{:S(2)}, u32[]{:S(2)}) collective-permute-start(bf16[2,128,256]{2,1,0:T(8,128)(2,1)S(1)} %get-tuple-element.45), channel_id=1, source_target_pairs={{0,2},{1,3},{2,0},{3,1},{4,6},{5,7},{6,4},{7,5},{8,10},{9,11},{10,... | collective-permute-start | bytes 393224 | tf_op jit(solution)/shard_map/ppermute | solution.py:499
  111.8 4.9 %collective-permute-start.16 = (bf16[2,128,256]{2,1,0:T(8,128)(2,1)S(1)}, bf16[2,128,256]{2,1,0:T(8,128)(2,1)S(1)}, u32[]{:S(2)}, u32[]{:S(2)}) collective-permute-start(bf16[2,128,256]{2,1,0:T(8,128)(2,1)S(1)} %get-tuple-element.46), channel_id=1, source_target_pairs={{0,4},{1,5},{2,6},{3,7},{4,0},{5,1},{6,2},{7,3},{8,12},{9,13},{10,... | collective-permute-start | bytes 393224 | tf_op jit(solution)/shard_map/ppermute | solution.py:499
  113.0 6.2 %collective-permute-start.18 = (bf16[2,128,256]{2,1,0:T(8,128)(2,1)S(1)}, bf16[2,128,256]{2,1,0:T(8,128)(2,1)S(1)}, u32[]{:S(2)}, u32[]{:S(2)}) collective-permute-start(bf16[2,128,256]{2,1,0:T(8,128)(2,1)S(1)} %get-tuple-element.47), channel_id=1, source_target_pairs={{0,6},{1,7},{2,4},{3,5},{4,2},{5,3},{6,0},{7,1},{8,14},{9,15},{10,... | collective-permute-start | bytes 393224 | tf_op jit(solution)/shard_map/ppermute | solution.py:499
  113.4 7.5 %collective-permute-start.13 = (bf16[2,128,256]{2,1,0:T(8,128)(2,1)S(1)}, bf16[2,128,256]{2,1,0:T(8,128)(2,1)S(1)}, u32[]{:S(2)}, u32[]{:S(2)}) collective-permute-start(bf16[2,128,256]{2,1,0:T(8,128)(2,1)S(1)} %get-tuple-element.44.refs_0_), channel_id=1, source_target_pairs={{0,1},{1,0},{2,3},{3,2},{4,5},{5,4},{6,7},{7,6},{8,9},{9,8},{10,11... | collective-permute-start | bytes 393224 | tf_op jit(solution)/shard_map/ppermute | solution.py:338
  115.2 5.8 %collective-permute-start.23 = (bf16[2,128,256]{2,1,0:T(8,128)(2,1)S(1)}, bf16[2,128,256]{2,1,0:T(8,128)(2,1)S(1)}, u32[]{:S(2)}, u32[]{:S(2)}) collective-permute-start(bf16[2,128,256]{2,1,0:T(8,128)(2,1)S(1)} %collective-permute-done.22.refs_10_), channel_id=1, source_target_pairs={{0,1},{1,0},{2,3},{3,2},{4,5},{5,4},{6,7},{7,6},{8,9},{9,8},{10,11... | collective-permute-start | bytes 393224 | tf_op jit(solution)/shard_map/ppermute | solution.py:338
  115.2 6.2 %collective-permute-start.25 = (bf16[2,128,256]{2,1,0:T(8,128)(2,1)S(1)}, bf16[2,128,256]{2,1,0:T(8,128)(2,1)S(1)}, u32[]{:S(2)}, u32[]{:S(2)}) collective-permute-start(bf16[2,128,256]{2,1,0:T(8,128)(2,1)S(1)} %collective-permute-done.24.refs_12_), channel_id=1, source_target_pairs={{0,1},{1,0},{2,3},{3,2},{4,5},{5,4},{6,7},{7,6},{8,9},{9,8},{10,11... | collective-permute-start | bytes 393224 | tf_op jit(solution)/shard_map/ppermute | solution.py:338
  116.7 4.7 %collective-permute-start.27 = (bf16[2,128,256]{2,1,0:T(8,128)(2,1)S(1)}, bf16[2,128,256]{2,1,0:T(8,128)(2,1)S(1)}, u32[]{:S(2)}, u32[]{:S(2)}) collective-permute-start(bf16[2,128,256]{2,1,0:T(8,128)(2,1)S(1)} %collective-permute-done.26.refs_14_), channel_id=1, source_target_pairs={{0,1},{1,0},{2,3},{3,2},{4,5},{5,4},{6,7},{7,6},{8,9},{9,8},{10,11... | collective-permute-start | bytes 393224 | tf_op jit(solution)/shard_map/ppermute | solution.py:338
  119.3 2.6 %collective-permute-start.15 = (bf16[2,128,256]{2,1,0:T(8,128)(2,1)S(1)}, bf16[2,128,256]{2,1,0:T(8,128)(2,1)S(1)}, u32[]{:S(2)}, u32[]{:S(2)}) collective-permute-start(bf16[2,128,256]{2,1,0:T(8,128)(2,1)S(1)} %collective-permute-done.14.refs_2_), channel_id=1, source_target_pairs={{0,1},{1,0},{2,3},{3,2},{4,5},{5,4},{6,7},{7,6},{8,9},{9,8},{10,11... | collective-permute-start | bytes 393224 | tf_op jit(solution)/shard_map/ppermute | solution.py:338
  120.9 1.3 %collective-permute-start.17 = (bf16[2,128,256]{2,1,0:T(8,128)(2,1)S(1)}, bf16[2,128,256]{2,1,0:T(8,128)(2,1)S(1)}, u32[]{:S(2)}, u32[]{:S(2)}) collective-permute-start(bf16[2,128,256]{2,1,0:T(8,128)(2,1)S(1)} %collective-permute-done.16.refs_4_), channel_id=1, source_target_pairs={{0,1},{1,0},{2,3},{3,2},{4,5},{5,4},{6,7},{7,6},{8,9},{9,8},{10,11... | collective-permute-start | bytes 393224 | tf_op jit(solution)/shard_map/ppermute | solution.py:338
  120.9 1.5 %collective-permute-start.19 = (bf16[2,128,256]{2,1,0:T(8,128)(2,1)S(1)}, bf16[2,128,256]{2,1,0:T(8,128)(2,1)S(1)}, u32[]{:S(2)}, u32[]{:S(2)}) collective-permute-start(bf16[2,128,256]{2,1,0:T(8,128)(2,1)S(1)} %collective-permute-done.18.refs_6_), channel_id=1, source_target_pairs={{0,1},{1,0},{2,3},{3,2},{4,5},{5,4},{6,7},{7,6},{8,9},{9,8},{10,11... | collective-permute-start | bytes 393224 | tf_op jit(solution)/shard_map/ppermute | solution.py:338

commit v6 on v5

--- a/solution.py
+++ b/solution.py
@@ -9,7 +9,7 @@
 from jax.sharding import PartitionSpec as P
 
 BLK = 64
-STEP = 2
+STEP = 4
 F32 = jnp.float32
 BF16 = jnp.bfloat16
 HIGHEST = lax.Precision.HIGHEST
@@ -180,11 +180,14 @@
 
 
 def inside_kernel(count, place_ref, decay_ref, start_ref, *refs):
-    q_parts, kv_parts, (raw_ref, q_ref, kv_ref) = refs[:count], refs[count : 2 * count], refs[2 * count :]
+    q_parts, kv_parts = refs[:count], refs[count : 2 * count]
+    raw_ref, out_ref, q_ref, kv_ref, sem = refs[2 * count :]
     chunks, length, here = q_ref.shape
     heads = decay_ref.shape[0] // chunks
     width = here // heads
     gather_chunks(place_ref, q_parts, q_ref)
+    copy = pltpu.make_async_copy(q_ref, out_ref, sem)
+    copy.start()
     gather_chunks(place_ref, kv_parts, kv_ref)
     logs = jnp.log(decay_ref[...])
     row, col = grid_of((length, length))
@@ -207,6 +210,7 @@
                     jnp.concatenate([queries, queries], 1), start_ref[h, c], ((1,), (0,))
                 )
             raw_ref[c, :, columns] = raw
+    copy.wait()
 
 
 def first_kernel(raw_ref, q_ref, decay_ref, gain_ref, *refs):
@@ -420,11 +424,15 @@
         lambda *refs: inside_kernel(chips, *refs),
         out_shape=(
             jax.ShapeDtypeStruct((ways, length, here), F32),
-            jax.ShapeDtypeStruct((ways, length, here), BF16),
+            pltpu.HBM((ways, length, here), BF16),
         ),
         in_specs=[SMEM, VMEM, VMEM] + [VMEM] * (2 * chips),
-        out_specs=(VMEM, VMEM),
-        scratch_shapes=[pltpu.VMEM((ways, 2 * length, here), BF16)],
+        out_specs=(VMEM, HBM),
+        scratch_shapes=[
+            pltpu.VMEM((ways, length, here), BF16),
+            pltpu.VMEM((ways, 2 * length, here), BF16),
+            pltpu.SemaphoreType.DMA,
+        ],
         compiler_params=PARAMS,
         cost_estimate=pl.CostEstimate(flops=2**31, bytes_accessed=6 * 2**20, transcendentals=2**19),
         name="inside",

time: 125 us -> 125 us (level)
  waiting for transfers between devices: 32 us -> 34.2 us
    ppermute x6, waiting for transfers between devices: 5.46 us -> 7.62 us  [onward(): lax.ppermute(x, 'group', [(i, i + steps) for i in range(groups - steps)])]
    unnamed x43 -> x41, local copies, waits for them, and re-layouts: 7.66 us -> 6.69 us
  transfers between devices with their start and end apart: 30 -> 30, of which waited for: 14 -> 14; matrix products, arithmetic and copies ran while one was open for 0% -> 0% of each run, Pallas kernels for 28% -> 27%
where the time goes in v6:
time: 125 us; the launch traced here: 124 us
  starting transfers between devices  43.9 us (35%)
  Pallas kernels  38.1 us (30%)
  waiting for transfers between devices  34.2 us (27%)
  local copies, waits for them, and re-layouts  7.18 us (6%)
    ppermute x6, waiting for transfers between devices, spread(): lax.ppermute(x, ('side', 'inner'), [(i, i ^ 2 * k) for i in range(ways)])  17.1 us
    ppermute x6, starting transfers between devices, onward(): lax.ppermute(x, 'group', [(i, i + steps) for i in range(groups - steps)])  13.4 us
    ppermute x10, starting transfers between devices, swap(): return lax.ppermute(x, ('side', 'inner'), [(i, i ^ 1) for i in range(ways)])  11.5 us
    all_to_all x2, waiting for transfers between devices, exchange(): lax.all_to_all(pieces, ('side', 'inner'), split_axis=0, concat_axis=0, ti...  8.3 us
    all_to_all x2, starting transfers between devices, exchange(): lax.all_to_all(pieces, ('side', 'inner'), split_axis=0, concat_axis=0, ti...  8.29 us
    ppermute x6, waiting for transfers between devices, onward(): lax.ppermute(x, 'group', [(i, i + steps) for i in range(groups - steps)])  7.62 us
    unnamed x41, local copies, waits for them, and re-layouts  6.69 us
    pallas_call x2, Pallas kernels, local(): pl.pallas_call(sum_kernel, out_shape=[jax.ShapeDtypeStruct((2, length, so...  6.67 us
  transfers between devices with their start and end apart: 30, of which 14 were waited for; matrix products, arithmetic and copies ran while one was open for 0% of the time, Pallas kernels for 27%

profile of v6, /device:TPU:17, one launch (start us, length us, event | category | flops | bytes accessed | tf_op | source)
XLA Modules:
  0.0 124.1 jit_solution(992430910734402436)
XLA Ops:
  0.1 1.4 %copy-done.8 = bf16[128,4096]{1,0:T(8,128)(2,1)S(1)} copy-done((bf16[128,4096]{1,0:T(8,128)(2,1)S(1)}, bf16[128,4096]{1,0:T(8,128)(2,1)}, u32[]{:S(2)}) %copy-start.8) | copy-done | bytes 1048600
  1.4 1.0 pieces.2.refs_3_
  2.5 0.1 pad_add_fusion
  2.6 1.6 %outward.2 = bf16[4,256,512]{2,1,0:T(8,128)(2,1)} custom-call(s32[4,2]{1,0:T(4,128)S(1)} %get-tuple-element.58.refs_0_.columns_ref, bf16[128,4096]{1,0:T(8,128)(2,1)S(1)} %copy-done.1, bf16[128,4096]{1,0:T(8,128)(2,1)S(1)} %copy-done.2, bf16[8,128,512]{2,1,0:T(8,128)(2,1)} %pieces.2.refs_3_), custom_call_target="tpu_custom_call" | custom-call | tf_op jit(solution)/shard_map/outward/pallas_call | solution.py:348
  4.3 0.7 collective-permute-start
  5.0 4.2 %all-to-all-start = ((bf16[8,128,512]{2,1,0:T(8,128)(2,1)}), bf16[8,128,512]{2,1,0:T(8,128)(2,1)}, u32[]{:S(2)}, u32[]{:S(2)}) async-start(bf16[8,128,512]{2,1,0:T(8,128)(2,1)} %pieces.2.refs_3_), calls=%async_computation | async-start | bytes 2097152 | tf_op jit(solution)/shard_map/all_to_all | solution.py:385
  9.3 0.1 convert_element_type.21
  9.5 2.8 %parcels.2 = (bf16[2,256,512]{2,1,0:T(8,128)(2,1)}, bf16[2,256,512]{2,1,0:T(8,128)(2,1)}, bf16[2,272,512]{2,1,0:T(8,128)(2,1)}, bf16[2,256,512]{2,1,0:T(8,128)(2,1)}) custom-call(s32[4,2]{1,0:T(4,128)S(1)} %get-tuple-element.58.refs_0_.columns_ref, s32[3]{0:T(128)S(1)} %pad_add_fusion.1.refs_1_.place_ref.refs_0_, bf16[128,4096]{1,0:T(8,128)(2,1)S(1)} %copy-done.1, ...), custom_call_target="tpu_custom_call" | custom-call | tf_op jit(solution)/shard_map/parcels/pallas_call | solution.py:357
  12.3 1.4 %collective-permute-start.2 = (bf16[2,272,512]{2,1,0:T(8,128)(2,1)}, bf16[2,272,512]{2,1,0:T(8,128)(2,1)S(1)}, u32[]{:S(2)}, u32[]{:S(2)}) collective-permute-start(bf16[2,272,512]{2,1,0:T(8,128)(2,1)} %get-tuple-element.31), channel_id=1, source_target_pairs={{0,4},{1,5},{2,6},{3,7},{4,0},{5,1},{6,2},{7,3},{8,12},{9,13},{10,... | collective-permute-start | bytes 1671176 | tf_op jit(solution)/shard_map/ppermute | solution.py:370
  13.7 1.4 %outward.3 = bf16[4,128,512]{2,1,0:T(8,128)(2,1)} custom-call(s32[4,2]{1,0:T(4,128)S(1)} %get-tuple-element.58.refs_0_.columns_ref, bf16[128,4096]{1,0:T(8,128)(2,1)S(1)} %copy-done.3), custom_call_target="tpu_custom_call" | custom-call | tf_op jit(solution)/shard_map/outward/pallas_call | solution.py:348
  15.1 0.7 collective-permute-start.5
  15.8 1.2 collective-permute-start.1
  17.0 5.8 %all-to-all-done = bf16[8,128,512]{2,1,0:T(8,128)(2,1)} async-done(((bf16[8,128,512]{2,1,0:T(8,128)(2,1)}), bf16[8,128,512]{2,1,0:T(8,128)(2,1)}, u32[]{:S(2)}, u32[]{:S(2)}) %all-to-all-start) | async-done | bytes 1048608 | tf_op jit(solution)/shard_map/all_to_all | solution.py:385
  22.9 3.2 %collective-permute-start.4 = (bf16[8,128,512]{2,1,0:T(8,128)(2,1)}, bf16[8,128,512]{2,1,0:T(8,128)(2,1)}, u32[]{:S(2)}, u32[]{:S(2)}) collective-permute-start(bf16[8,128,512]{2,1,0:T(8,128)(2,1)} %all-to-all-done), channel_id=1, source_target_pairs={{0,8},{8,16},{16,24},{1,9},{9,17},{17,25},{2,10},{10,18},{18,26},{... | collective-permute-start | bytes 3145736 | tf_op jit(solution)/shard_map/ppermute | solution.py:388
  26.1 8.0 %collective-permute-done.1.refs_1_.refs_4_.refs_8_ = bf16[2,256,512]{2,1,0:T(8,128)(2,1)S(1)} collective-permute-done((bf16[2,256,512]{2,1,0:T(8,128)(2,1)}, bf16[2,256,512]{2,1,0:T(8,128)(2,1)S(1)}, u32[]{:S(2)}, u32[]{:S(2)}) %collective-permute-start.1) | collective-permute-done | bytes 524320 | tf_op jit(solution)/shard_map/ppermute | solution.py:370
  34.1 0.7 collective-permute-done.2.refs_2_.refs_5_.refs_9_
  34.8 2.3 %parcels.3 = (bf16[2,128,512]{2,1,0:T(8,128)(2,1)}, bf16[2,128,512]{2,1,0:T(8,128)(2,1)}, bf16[2,128,512]{2,1,0:T(8,128)(2,1)}, bf16[2,128,512]{2,1,0:T(8,128)(2,1)}) custom-call(s32[4,2]{1,0:T(4,128)S(1)} %get-tuple-element.58.refs_0_.columns_ref, s32[3]{0:T(128)S(1)} %pad_add_fusion.1.refs_1_.place_ref.refs_0_, bf16[128,4096]{1,0:T(8,128)(2,1)S(1)} %copy-done.3, ...), custom_call_target="tpu_custom_call" | custom-call | tf_op jit(solution)/shard_map/parcels/pallas_call | solution.py:357
  37.2 1.3 %collective-permute-start.6 = (bf16[2,128,512]{2,1,0:T(8,128)(2,1)}, bf16[2,128,512]{2,1,0:T(8,128)(2,1)S(1)}, u32[]{:S(2)}, u32[]{:S(2)}) collective-permute-start(bf16[2,128,512]{2,1,0:T(8,128)(2,1)} %get-tuple-element.37), channel_id=1, source_target_pairs={{0,2},{1,3},{2,0},{3,1},{4,6},{5,7},{6,4},{7,5},{8,10},{9,11},{10,... | collective-permute-start | bytes 786440 | tf_op jit(solution)/shard_map/ppermute | solution.py:370
  38.4 0.3 collective-permute-start.7
  38.7 1.2 collective-permute-start.8
  39.9 7.1 %collective-permute-done.3.refs_3_.refs_10_ = bf16[2,256,512]{2,1,0:T(8,128)(2,1)} collective-permute-done((bf16[2,256,512]{2,1,0:T(8,128)(2,1)}, bf16[2,256,512]{2,1,0:T(8,128)(2,1)}, u32[]{:S(2)}, u32[]{:S(2)}) %collective-permute-start.3) | collective-permute-done | bytes 524320 | tf_op jit(solution)/shard_map/ppermute | solution.py:370
  47.0 4.0 %state.1 = (bf16[4,144,128]{2,1,0:T(8,128)(2,1)S(1)}, bf16[4,8,256,128]{3,2,1,0:T(8,128)(2,1)S(1)}, f32[32,128]{1,0:T(8,128)S(1)}, f32[2,1,512]{2,1,0:T(1,128)S(1)}) custom-call(s32[3]{0:T(128)S(1)} %pad_add_fusion.1.refs_1_.place_ref.refs_0_, f32[5,512]{1,0:T(8,128)S(1)} %get-tuple-element.56.table_ref, bf16[2,256,512]{2,1,0:T(8,128)(2,1)S(1)} %copy-done.13, ...), custom_call_target="tpu_custom_call" | custom-call | tf_op jit(solution)/shard_map/state/pallas_call | solution.py:405
  51.0 1.3 %collective-permute-start.10 = (bf16[4,144,128]{2,1,0:T(8,128)(2,1)S(1)}, bf16[4,144,128]{2,1,0:T(8,128)(2,1)S(1)}, u32[]{:S(2)}, u32[]{:S(2)}) collective-permute-start(bf16[4,144,128]{2,1,0:T(8,128)(2,1)S(1)} %get-tuple-element.41), channel_id=1, source_target_pairs={{0,16},{8,24},{1,17},{9,25},{2,18},{10,26},{3,19},{11,27},{4,20},{... | collective-permute-start | bytes 442376 | tf_op jit(solution)/shard_map/ppermute | solution.py:388
  52.3 0.8 collective-permute-done.6.refs_4_
  53.2 0.7 collective-permute-start.11
  53.9 3.8 %collective-permute-start.9 = (bf16[4,144,128]{2,1,0:T(8,128)(2,1)S(1)}, bf16[4,144,128]{2,1,0:T(8,128)(2,1)S(1)}, u32[]{:S(2)}, u32[]{:S(2)}) collective-permute-start(bf16[4,144,128]{2,1,0:T(8,128)(2,1)S(1)} %get-tuple-element.41), channel_id=1, source_target_pairs={{0,8},{8,16},{16,24},{1,9},{9,17},{17,25},{2,10},{10,18},{18,26},{... | collective-permute-start | bytes 442376 | tf_op jit(solution)/shard_map/ppermute | solution.py:388
  57.7 0.4 collective-permute-done.8.refs_6_
  58.1 1.1 copy-done.5
  59.2 1.0 copy-done.7
  60.2 1.0 copy-done.14
  61.3 4.7 %inside.1 = (f32[8,128,512]{2,1,0:T(8,128)S(1)}, bf16[8,128,512]{2,1,0:T(8,128)(2,1)}) custom-call(s32[3]{0:T(128)S(1)} %pad_add_fusion.1.refs_1_.place_ref.refs_0_, f32[32,128]{1,0:T(8,128)S(1)} %get-tuple-element.34.refs_1_.decay_ref, bf16[4,8,256,128]{3,2,1,0:T(8,128)(2,1)S(1)} %get-tuple-element.35.refs_2_, bf16[2,128,512]{2,1,0:T(8,128)(2,1)S(1)} %copy-done.17, ...), custom_call_target="tpu_custom_call" | custom-call | flops 2147483648 | bytes 6291456 | tf_op jit(solution)/shard_map/inside/pallas_call | solution.py:423
  66.0 3.0 %collective-permute-done.9.refs_1_.refs_0_ = bf16[4,144,128]{2,1,0:T(8,128)(2,1)S(1)} collective-permute-done((bf16[4,144,128]{2,1,0:T(8,128)(2,1)S(1)}, bf16[4,144,128]{2,1,0:T(8,128)(2,1)S(1)}, u32[]{:S(2)}, u32[]{:S(2)}) %collective-permute-start.9) | collective-permute-done | bytes 147488 | tf_op jit(solution)/shard_map/ppermute | solution.py:388
  69.0 1.1 pieces.3
  70.1 4.1 %all-to-all-start.1 = ((bf16[8,128,512]{2,1,0:T(8,128)(2,1)}), bf16[8,128,512]{2,1,0:T(8,128)(2,1)S(1)}, u32[]{:S(2)}, u32[]{:S(2)}) async-start(bf16[8,128,512]{2,1,0:T(8,128)(2,1)} %pieces.3), calls=%async_computation.1 | async-start | bytes 2097152 | tf_op jit(solution)/shard_map/all_to_all | solution.py:385
  74.2 0.1 add.79.order_ref
  74.3 1.2 copy-done.10
  75.5 0.9 copy-done.12
  76.5 4.1 %first.1 = (bf16[8,128,256]{2,1,0:T(8,128)(2,1)}, bf16[8,128,256]{2,1,0:T(8,128)(2,1)}) custom-call(f32[8,128,512]{2,1,0:T(8,128)S(1)} %get-tuple-element.40.refs_0_.raw_ref, bf16[8,128,512]{2,1,0:T(8,128)(2,1)S(1)} %copy-done.10, f32[32,128]{1,0:T(8,128)S(1)} %get-tuple-element.34.refs_1_.decay_ref, f32[4,128]{1,0:T(4,128)S(1)} %constant_dynamic-slice_fusion.gain_ref, ...), custom_call_target="tpu_custom_call" | custom-call | tf_op jit(solution)/shard_map/first/pallas_call | solution.py:441
  80.5 2.3 %collective-permute-start.20 = (bf16[8,128,256]{2,1,0:T(8,128)(2,1)}, bf16[8,128,256]{2,1,0:T(8,128)(2,1)S(1)}, u32[]{:S(2)}, u32[]{:S(2)}) collective-permute-start(bf16[8,128,256]{2,1,0:T(8,128)(2,1)} %get-tuple-element.48), channel_id=1, source_target_pairs={{0,8},{8,16},{16,24},{1,9},{9,17},{17,25},{2,10},{10,18},{18,26},{... | collective-permute-start | bytes 1572872 | tf_op jit(solution)/shard_map/ppermute | solution.py:388
  83.1 0.1 reshape.98.bias_ref
  83.2 2.1 %collective-permute-start.12 = (bf16[8,128,256]{2,1,0:T(8,128)(2,1)}, bf16[8,128,256]{2,1,0:T(8,128)(2,1)S(1)}, u32[]{:S(2)}, u32[]{:S(2)}) collective-permute-start(bf16[8,128,256]{2,1,0:T(8,128)(2,1)} %get-tuple-element.43), channel_id=1, source_target_pairs={{0,8},{8,16},{16,24},{1,9},{9,17},{17,25},{2,10},{10,18},{18,26},{... | collective-permute-start | bytes 1572872 | tf_op jit(solution)/shard_map/ppermute | solution.py:388
  85.3 2.5 %all-to-all-done.1 = bf16[8,128,512]{2,1,0:T(8,128)(2,1)S(1)} async-done(((bf16[8,128,512]{2,1,0:T(8,128)(2,1)}), bf16[8,128,512]{2,1,0:T(8,128)(2,1)S(1)}, u32[]{:S(2)}, u32[]{:S(2)}) %all-to-all-start.1) | async-done | bytes 1048608 | tf_op jit(solution)/shard_map/all_to_all | solution.py:385
  87.8 6.7 %weights.1.weights_ref = bf16[4,1024,512]{2,1,0:T(8,128)(2,1)S(1)} custom-call(s32[16,8]{1,0:T(8,128)S(1)} %select_n.57.window_ref, bf16[1024,512]{1,0:T(8,128)(2,1)} %bitcast.4.own_ref, bf16[1024,512]{1,0:T(8,128)(2,1)} %bitcast.5.earlier_ref, f32[16,512]{1,0:T(8,128)S(1)} %reshape.98.bias_ref, bf16[1024,512]{1,0:T(8,128)(2,1)S(1)} %bitcast.14), custom_call_target="tpu_custom_call" | custom-call | flops 2147483648 | bytes 8388608 | tf_op jit(solution)/shard_map/weights/pallas_call | solution.py:457
  94.5 1.7 %collective-permute-done.20 = bf16[8,128,256]{2,1,0:T(8,128)(2,1)S(1)} collective-permute-done((bf16[8,128,256]{2,1,0:T(8,128)(2,1)}, bf16[8,128,256]{2,1,0:T(8,128)(2,1)S(1)}, u32[]{:S(2)}, u32[]{:S(2)}) %collective-permute-start.20) | collective-permute-done | bytes 524320 | tf_op jit(solution)/shard_map/ppermute | solution.py:388
  96.2 3.3 %sum.3 = (bf16[2,128,256]{2,1,0:T(8,128)(2,1)S(1)}, bf16[2,128,256]{2,1,0:T(8,128)(2,1)S(1)}, bf16[2,128,256]{2,1,0:T(8,128)(2,1)S(1)}, bf16[2,128,256]{2,1,0:T(8,128)(2,1)S(1)}) custom-call(s32[8]{0:T(128)S(1)} %add.79.order_ref, s32[16,8]{1,0:T(8,128)S(1)} %select_n.57.window_ref, bf16[4,1024,512]{2,1,0:T(8,128)(2,1)S(1)} %weights.1.weights_ref, ...), custom_call_target="tpu_custom_call" | custom-call | tf_op jit(solution)/shard_map/sum/pallas_call | solution.py:482
  99.5 1.1 collective-permute-start.22
  100.6 1.2 collective-permute-start.24
  101.8 0.4 collective-permute-start.26
  102.2 2.2 %collective-permute-start.21 = (bf16[2,128,256]{2,1,0:T(8,128)(2,1)S(1)}, bf16[2,128,256]{2,1,0:T(8,128)(2,1)S(1)}, u32[]{:S(2)}, u32[]{:S(2)}) collective-permute-start(bf16[2,128,256]{2,1,0:T(8,128)(2,1)S(1)} %get-tuple-element.49.refs_8_), channel_id=1, source_target_pairs={{0,1},{1,0},{2,3},{3,2},{4,5},{5,4},{6,7},{7,6},{8,9},{9,8},{10,11... | collective-permute-start | bytes 393224 | tf_op jit(solution)/shard_map/ppermute | solution.py:342
  104.4 3.0 %collective-permute-done.12 = bf16[8,128,256]{2,1,0:T(8,128)(2,1)S(1)} collective-permute-done((bf16[8,128,256]{2,1,0:T(8,128)(2,1)}, bf16[8,128,256]{2,1,0:T(8,128)(2,1)S(1)}, u32[]{:S(2)}, u32[]{:S(2)}) %collective-permute-start.12) | collective-permute-done | bytes 524320 | tf_op jit(solution)/shard_map/ppermute | solution.py:388
  107.4 3.3 %sum.2 = (bf16[2,128,256]{2,1,0:T(8,128)(2,1)S(1)}, bf16[2,128,256]{2,1,0:T(8,128)(2,1)S(1)}, bf16[2,128,256]{2,1,0:T(8,128)(2,1)S(1)}, bf16[2,128,256]{2,1,0:T(8,128)(2,1)S(1)}) custom-call(s32[8]{0:T(128)S(1)} %add.79.order_ref, s32[16,8]{1,0:T(8,128)S(1)} %select_n.57.window_ref, bf16[4,1024,512]{2,1,0:T(8,128)(2,1)S(1)} %weights.1.weights_ref, ...), custom_call_target="tpu_custom_call" | custom-call | tf_op jit(solution)/shard_map/sum/pallas_call | solution.py:482
  110.7 1.1 collective-permute-start.14
  111.8 1.2 collective-permute-start.16
  113.0 0.4 collective-permute-start.18
  113.4 1.7 %collective-permute-start.13 = (bf16[2,128,256]{2,1,0:T(8,128)(2,1)S(1)}, bf16[2,128,256]{2,1,0:T(8,128)(2,1)S(1)}, u32[]{:S(2)}, u32[]{:S(2)}) collective-permute-start(bf16[2,128,256]{2,1,0:T(8,128)(2,1)S(1)} %get-tuple-element.44.refs_0_), channel_id=1, source_target_pairs={{0,1},{1,0},{2,3},{3,2},{4,5},{5,4},{6,7},{7,6},{8,9},{9,8},{10,11... | collective-permute-start | bytes 393224 | tf_op jit(solution)/shard_map/ppermute | solution.py:342
  115.2 1.5 %collective-permute-start.25 = (bf16[2,128,256]{2,1,0:T(8,128)(2,1)S(1)}, bf16[2,128,256]{2,1,0:T(8,128)(2,1)S(1)}, u32[]{:S(2)}, u32[]{:S(2)}) collective-permute-start(bf16[2,128,256]{2,1,0:T(8,128)(2,1)S(1)} %collective-permute-done.24.refs_12_), channel_id=1, source_target_pairs={{0,1},{1,0},{2,3},{3,2},{4,5},{5,4},{6,7},{7,6},{8,9},{9,8},{10,11... | collective-permute-start | bytes 393224 | tf_op jit(solution)/shard_map/ppermute | solution.py:342
  116.7 2.4 %collective-permute-start.27 = (bf16[2,128,256]{2,1,0:T(8,128)(2,1)S(1)}, bf16[2,128,256]{2,1,0:T(8,128)(2,1)S(1)}, u32[]{:S(2)}, u32[]{:S(2)}) collective-permute-start(bf16[2,128,256]{2,1,0:T(8,128)(2,1)S(1)} %collective-permute-done.26.refs_14_), channel_id=1, source_target_pairs={{0,1},{1,0},{2,3},{3,2},{4,5},{5,4},{6,7},{7,6},{8,9},{9,8},{10,11... | collective-permute-start | bytes 393224 | tf_op jit(solution)/shard_map/ppermute | solution.py:342
  119.2 0.1 collective-permute-done.18.refs_6_
  119.3 1.6 %collective-permute-start.15 = (bf16[2,128,256]{2,1,0:T(8,128)(2,1)S(1)}, bf16[2,128,256]{2,1,0:T(8,128)(2,1)S(1)}, u32[]{:S(2)}, u32[]{:S(2)}) collective-permute-start(bf16[2,128,256]{2,1,0:T(8,128)(2,1)S(1)} %collective-permute-done.14.refs_2_), channel_id=1, source_target_pairs={{0,1},{1,0},{2,3},{3,2},{4,5},{5,4},{6,7},{7,6},{8,9},{9,8},{10,11... | collective-permute-start | bytes 393224 | tf_op jit(solution)/shard_map/ppermute | solution.py:342
  120.9 0.5 collective-permute-start.19
  121.4 0.5 collective-permute-done.15.refs_3_
  121.9 0.4 collective-permute-done.17.refs_5_
  122.3 0.2 collective-permute-done.19.refs_7_
  122.4 1.7 %join.1 = bf16[128,4096]{1,0:T(8,128)(2,1)} custom-call(s32[4,2]{1,0:T(4,128)S(1)} %get-tuple-element.58.refs_0_.columns_ref, bf16[2,128,256]{2,1,0:T(8,128)(2,1)S(1)} %get-tuple-element.44.refs_0_, bf16[2,128,256]{2,1,0:T(8,128)(2,1)S(1)} %collective-permute-done.13.refs_1_, bf16[2,128,256]{2,1,0:T(8,128)(2,1)S(1)} %collective-permute-done.14.refs_2_, ...), custom_call_target="tpu_custom_call" | custom-call | tf_op jit(solution)/shard_map/join/pallas_call | solution.py:509
  (67 shorter events, 0.6 us)
Async XLA Ops:
  0.0 74.3 %copy-start = (f32[8,128]{1,0:T(8,128)S(1)}, f32[8,128]{1,0:T(8,128)}, u32[]{:S(2)}) copy-start(f32[8,128]{1,0:T(8,128)} %param.14) | copy-start | bytes 12292
  0.0 2.6 %copy-start.2 = (bf16[128,4096]{1,0:T(8,128)(2,1)S(1)}, bf16[128,4096]{1,0:T(8,128)(2,1)}, u32[]{:S(2)}) copy-start(bf16[128,4096]{1,0:T(8,128)(2,1)} %refs_3_.1) | copy-start | bytes 3145732
  0.0 2.6 %copy-start.1 = (bf16[128,4096]{1,0:T(8,128)(2,1)S(1)}, bf16[128,4096]{1,0:T(8,128)(2,1)}, u32[]{:S(2)}) copy-start(bf16[128,4096]{1,0:T(8,128)(2,1)} %refs_2_.4) | copy-start | bytes 3145732
  0.1 1.4 %copy-start.8 = (bf16[128,4096]{1,0:T(8,128)(2,1)S(1)}, bf16[128,4096]{1,0:T(8,128)(2,1)}, u32[]{:S(2)}) copy-start(bf16[128,4096]{1,0:T(8,128)(2,1)} %in_ref.2) | copy-start | bytes 3145732
  4.3 5.0 %copy-start.19 = (s32[8,8]{1,0:T(8,128)S(1)}, s32[8,8]{1,0:T(8,128)}, u32[]{:S(2)}) copy-start(s32[8,8]{1,0:T(8,128)} %param.15) | copy-start | bytes 772
  4.3 5.2 %copy-start.18 = (f32[8,512]{1,0:T(8,128)S(1)}, f32[8,512]{1,0:T(8,128)}, u32[]{:S(2)}) copy-start(f32[8,512]{1,0:T(8,128)} %param.13) | copy-start | bytes 49156
  4.3 5.2 %collective-permute-start = (bf16[4,256,512]{2,1,0:T(8,128)(2,1)}, bf16[4,256,512]{2,1,0:T(8,128)(2,1)}, u32[]{:S(2)}, u32[]{:S(2)}) collective-permute-start(bf16[4,256,512]{2,1,0:T(8,128)(2,1)} %outward.2), channel_id=1, source_target_pairs={{0,1},{1,0},{2,3},{3,2},{4,5},{5,4},{6,7},{7,6},{8,9},{9,8},{10,11... | collective-permute-start | bytes 3145736 | tf_op jit(solution)/shard_map/ppermute | solution.py:342
  5.0 17.9 %all-to-all-start = ((bf16[8,128,512]{2,1,0:T(8,128)(2,1)}), bf16[8,128,512]{2,1,0:T(8,128)(2,1)}, u32[]{:S(2)}, u32[]{:S(2)}) async-start(bf16[8,128,512]{2,1,0:T(8,128)(2,1)} %pieces.2.refs_3_), calls=%async_computation | async-start | bytes 2097152 | tf_op jit(solution)/shard_map/all_to_all | solution.py:385
  9.2 4.5 %copy-start.3 = (bf16[128,4096]{1,0:T(8,128)(2,1)S(1)}, bf16[128,4096]{1,0:T(8,128)(2,1)}, u32[]{:S(2)}) copy-start(bf16[128,4096]{1,0:T(8,128)(2,1)} %refs_2_.5) | copy-start | bytes 3145732
  12.3 34.7 %copy-start.13 = (bf16[2,256,512]{2,1,0:T(8,128)(2,1)S(1)}, bf16[2,256,512]{2,1,0:T(8,128)(2,1)}, u32[]{:S(2)}) copy-start(bf16[2,256,512]{2,1,0:T(8,128)(2,1)} %get-tuple-element.29.refs_0_.refs_7_) | copy-start | bytes 1572868
  12.3 22.5 %collective-permute-start.2 = (bf16[2,272,512]{2,1,0:T(8,128)(2,1)}, bf16[2,272,512]{2,1,0:T(8,128)(2,1)S(1)}, u32[]{:S(2)}, u32[]{:S(2)}) collective-permute-start(bf16[2,272,512]{2,1,0:T(8,128)(2,1)} %get-tuple-element.31), channel_id=1, source_target_pairs={{0,4},{1,5},{2,6},{3,7},{4,0},{5,1},{6,2},{7,3},{8,12},{9,13},{10,... | collective-permute-start | bytes 1671176 | tf_op jit(solution)/shard_map/ppermute | solution.py:370
  15.1 11.0 %collective-permute-start.5 = (bf16[4,128,512]{2,1,0:T(8,128)(2,1)}, bf16[4,128,512]{2,1,0:T(8,128)(2,1)}, u32[]{:S(2)}, u32[]{:S(2)}) collective-permute-start(bf16[4,128,512]{2,1,0:T(8,128)(2,1)} %outward.3), channel_id=1, source_target_pairs={{0,1},{1,0},{2,3},{3,2},{4,5},{5,4},{6,7},{7,6},{8,9},{9,8},{10,11... | collective-permute-start | bytes 1572872 | tf_op jit(solution)/shard_map/ppermute | solution.py:342
  15.8 18.3 %collective-permute-start.1 = (bf16[2,256,512]{2,1,0:T(8,128)(2,1)}, bf16[2,256,512]{2,1,0:T(8,128)(2,1)S(1)}, u32[]{:S(2)}, u32[]{:S(2)}) collective-permute-start(bf16[2,256,512]{2,1,0:T(8,128)(2,1)} %get-tuple-element.30), channel_id=1, source_target_pairs={{0,2},{1,3},{2,0},{3,1},{4,6},{5,7},{6,4},{7,5},{8,10},{9,11},{10,... | collective-permute-start | bytes 1572872 | tf_op jit(solution)/shard_map/ppermute | solution.py:370
  17.0 30.0 %collective-permute-start.3 = (bf16[2,256,512]{2,1,0:T(8,128)(2,1)}, bf16[2,256,512]{2,1,0:T(8,128)(2,1)}, u32[]{:S(2)}, u32[]{:S(2)}) collective-permute-start(bf16[2,256,512]{2,1,0:T(8,128)(2,1)} %get-tuple-element.32), channel_id=1, source_target_pairs={{0,6},{1,7},{2,4},{3,5},{4,2},{5,3},{6,0},{7,1},{8,14},{9,15},{10,... | collective-permute-start | bytes 1572872 | tf_op jit(solution)/shard_map/ppermute | solution.py:370
  22.9 51.4 %collective-permute-start.4 = (bf16[8,128,512]{2,1,0:T(8,128)(2,1)}, bf16[8,128,512]{2,1,0:T(8,128)(2,1)}, u32[]{:S(2)}, u32[]{:S(2)}) collective-permute-start(bf16[8,128,512]{2,1,0:T(8,128)(2,1)} %all-to-all-done), channel_id=1, source_target_pairs={{0,8},{8,16},{16,24},{1,9},{9,17},{17,25},{2,10},{10,18},{18,26},{... | collective-permute-start | bytes 3145736 | tf_op jit(solution)/shard_map/ppermute | solution.py:388
  34.1 16.9 %copy-start.6 = (bf16[2,256,512]{2,1,0:T(8,128)(2,1)}, bf16[2,256,512]{2,1,0:T(8,128)(2,1)S(1)}, u32[]{:S(2)}) copy-start(bf16[2,256,512]{2,1,0:T(8,128)(2,1)S(1)} %collective-permute-done.1.refs_1_.refs_4_.refs_8_) | copy-start | bytes 1572868
  34.8 16.2 %copy-start.4 = (bf16[2,272,512]{2,1,0:T(8,128)(2,1)}, bf16[2,272,512]{2,1,0:T(8,128)(2,1)S(1)}, u32[]{:S(2)}) copy-start(bf16[2,272,512]{2,1,0:T(8,128)(2,1)S(1)} %collective-permute-done.2.refs_2_.refs_5_.refs_9_) | copy-start | bytes 1671172
  37.2 21.0 %copy-start.17 = (bf16[2,128,512]{2,1,0:T(8,128)(2,1)S(1)}, bf16[2,128,512]{2,1,0:T(8,128)(2,1)}, u32[]{:S(2)}) copy-start(bf16[2,128,512]{2,1,0:T(8,128)(2,1)} %get-tuple-element.36.refs_3_) | copy-start | bytes 786436
  37.2 16.0 %collective-permute-start.6 = (bf16[2,128,512]{2,1,0:T(8,128)(2,1)}, bf16[2,128,512]{2,1,0:T(8,128)(2,1)S(1)}, u32[]{:S(2)}, u32[]{:S(2)}) collective-permute-start(bf16[2,128,512]{2,1,0:T(8,128)(2,1)} %get-tuple-element.37), channel_id=1, source_target_pairs={{0,2},{1,3},{2,0},{3,1},{4,6},{5,7},{6,4},{7,5},{8,10},{9,11},{10,... | collective-permute-start | bytes 786440 | tf_op jit(solution)/shard_map/ppermute | solution.py:370
  38.4 15.4 %collective-permute-start.7 = (bf16[2,128,512]{2,1,0:T(8,128)(2,1)}, bf16[2,128,512]{2,1,0:T(8,128)(2,1)S(1)}, u32[]{:S(2)}, u32[]{:S(2)}) collective-permute-start(bf16[2,128,512]{2,1,0:T(8,128)(2,1)} %get-tuple-element.38), channel_id=1, source_target_pairs={{0,4},{1,5},{2,6},{3,7},{4,0},{5,1},{6,2},{7,3},{8,12},{9,13},{10,... | collective-permute-start | bytes 786440 | tf_op jit(solution)/shard_map/ppermute | solution.py:370
  38.7 19.4 %collective-permute-start.8 = (bf16[2,128,512]{2,1,0:T(8,128)(2,1)}, bf16[2,128,512]{2,1,0:T(8,128)(2,1)S(1)}, u32[]{:S(2)}, u32[]{:S(2)}) collective-permute-start(bf16[2,128,512]{2,1,0:T(8,128)(2,1)} %get-tuple-element.39), channel_id=1, source_target_pairs={{0,6},{1,7},{2,4},{3,5},{4,2},{5,3},{6,0},{7,1},{8,14},{9,15},{10,... | collective-permute-start | bytes 786440 | tf_op jit(solution)/shard_map/ppermute | solution.py:370
  51.0 15.0 %collective-permute-start.10 = (bf16[4,144,128]{2,1,0:T(8,128)(2,1)S(1)}, bf16[4,144,128]{2,1,0:T(8,128)(2,1)S(1)}, u32[]{:S(2)}, u32[]{:S(2)}) collective-permute-start(bf16[4,144,128]{2,1,0:T(8,128)(2,1)S(1)} %get-tuple-element.41), channel_id=1, source_target_pairs={{0,16},{8,24},{1,17},{9,25},{2,18},{10,26},{3,19},{11,27},{4,20},{... | collective-permute-start | bytes 442376 | tf_op jit(solution)/shard_map/ppermute | solution.py:388
  53.2 12.8 %collective-permute-start.11 = (bf16[4,144,128]{2,1,0:T(8,128)(2,1)S(1)}, bf16[4,144,128]{2,1,0:T(8,128)(2,1)S(1)}, u32[]{:S(2)}, u32[]{:S(2)}) collective-permute-start(bf16[4,144,128]{2,1,0:T(8,128)(2,1)S(1)} %get-tuple-element.41), channel_id=1, source_target_pairs={{0,24},{1,25},{2,26},{3,27},{4,28},{5,29},{6,30},{7,31}} | collective-permute-start | bytes 442376 | tf_op jit(solution)/shard_map/ppermute | solution.py:388
  53.9 15.1 %collective-permute-start.9 = (bf16[4,144,128]{2,1,0:T(8,128)(2,1)S(1)}, bf16[4,144,128]{2,1,0:T(8,128)(2,1)S(1)}, u32[]{:S(2)}, u32[]{:S(2)}) collective-permute-start(bf16[4,144,128]{2,1,0:T(8,128)(2,1)S(1)} %get-tuple-element.41), channel_id=1, source_target_pairs={{0,8},{8,16},{16,24},{1,9},{9,17},{17,25},{2,10},{10,18},{18,26},{... | collective-permute-start | bytes 442376 | tf_op jit(solution)/shard_map/ppermute | solution.py:388
  58.1 1.1 copy-start.5
  59.2 1.0 copy-start.7
  60.2 1.0 copy-start.14
  61.3 7.7 %copy-start.9 = (bf16[128,4096]{1,0:T(8,128)(2,1)S(1)}, bf16[128,4096]{1,0:T(8,128)(2,1)}, u32[]{:S(2)}) copy-start(bf16[128,4096]{1,0:T(8,128)(2,1)} %in_ref.3) | copy-start | bytes 3145732
  69.0 1.1 copy-start.11
  70.1 17.7 %all-to-all-start.1 = ((bf16[8,128,512]{2,1,0:T(8,128)(2,1)}), bf16[8,128,512]{2,1,0:T(8,128)(2,1)S(1)}, u32[]{:S(2)}, u32[]{:S(2)}) async-start(bf16[8,128,512]{2,1,0:T(8,128)(2,1)} %pieces.3), calls=%async_computation.1 | async-start | bytes 2097152 | tf_op jit(solution)/shard_map/all_to_all | solution.py:385
  74.3 1.2 copy-start.10
  75.5 0.9 copy-start.12
  80.5 15.6 %collective-permute-start.20 = (bf16[8,128,256]{2,1,0:T(8,128)(2,1)}, bf16[8,128,256]{2,1,0:T(8,128)(2,1)S(1)}, u32[]{:S(2)}, u32[]{:S(2)}) collective-permute-start(bf16[8,128,256]{2,1,0:T(8,128)(2,1)} %get-tuple-element.48), channel_id=1, source_target_pairs={{0,8},{8,16},{16,24},{1,9},{9,17},{17,25},{2,10},{10,18},{18,26},{... | collective-permute-start | bytes 1572872 | tf_op jit(solution)/shard_map/ppermute | solution.py:388
  83.2 24.2 %collective-permute-start.12 = (bf16[8,128,256]{2,1,0:T(8,128)(2,1)}, bf16[8,128,256]{2,1,0:T(8,128)(2,1)S(1)}, u32[]{:S(2)}, u32[]{:S(2)}) collective-permute-start(bf16[8,128,256]{2,1,0:T(8,128)(2,1)} %get-tuple-element.43), channel_id=1, source_target_pairs={{0,8},{8,16},{16,24},{1,9},{9,17},{17,25},{2,10},{10,18},{18,26},{... | collective-permute-start | bytes 1572872 | tf_op jit(solution)/shard_map/ppermute | solution.py:388
  87.8 8.3 %copy-start.16 = (bf16[8,128,256]{2,1,0:T(8,128)(2,1)S(1)}, bf16[8,128,256]{2,1,0:T(8,128)(2,1)}, u32[]{:S(2)}) copy-start(bf16[8,128,256]{2,1,0:T(8,128)(2,1)} %get-tuple-element.48) | copy-start | bytes 1572868
  96.2 11.2 %copy-start.15 = (bf16[8,128,256]{2,1,0:T(8,128)(2,1)S(1)}, bf16[8,128,256]{2,1,0:T(8,128)(2,1)}, u32[]{:S(2)}) copy-start(bf16[8,128,256]{2,1,0:T(8,128)(2,1)} %get-tuple-element.43) | copy-start | bytes 1572868
  99.5 12.3 %collective-permute-start.22 = (bf16[2,128,256]{2,1,0:T(8,128)(2,1)S(1)}, bf16[2,128,256]{2,1,0:T(8,128)(2,1)S(1)}, u32[]{:S(2)}, u32[]{:S(2)}) collective-permute-start(bf16[2,128,256]{2,1,0:T(8,128)(2,1)S(1)} %get-tuple-element.50), channel_id=1, source_target_pairs={{0,2},{1,3},{2,0},{3,1},{4,6},{5,7},{6,4},{7,5},{8,10},{9,11},{10,... | collective-permute-start | bytes 393224 | tf_op jit(solution)/shard_map/ppermute | solution.py:507
  100.6 12.4 %collective-permute-start.24 = (bf16[2,128,256]{2,1,0:T(8,128)(2,1)S(1)}, bf16[2,128,256]{2,1,0:T(8,128)(2,1)S(1)}, u32[]{:S(2)}, u32[]{:S(2)}) collective-permute-start(bf16[2,128,256]{2,1,0:T(8,128)(2,1)S(1)} %get-tuple-element.51), channel_id=1, source_target_pairs={{0,4},{1,5},{2,6},{3,7},{4,0},{5,1},{6,2},{7,3},{8,12},{9,13},{10,... | collective-permute-start | bytes 393224 | tf_op jit(solution)/shard_map/ppermute | solution.py:507
  101.8 11.6 %collective-permute-start.26 = (bf16[2,128,256]{2,1,0:T(8,128)(2,1)S(1)}, bf16[2,128,256]{2,1,0:T(8,128)(2,1)S(1)}, u32[]{:S(2)}, u32[]{:S(2)}) collective-permute-start(bf16[2,128,256]{2,1,0:T(8,128)(2,1)S(1)} %get-tuple-element.52), channel_id=1, source_target_pairs={{0,6},{1,7},{2,4},{3,5},{4,2},{5,3},{6,0},{7,1},{8,14},{9,15},{10,... | collective-permute-start | bytes 393224 | tf_op jit(solution)/shard_map/ppermute | solution.py:507
  102.2 13.0 %collective-permute-start.21 = (bf16[2,128,256]{2,1,0:T(8,128)(2,1)S(1)}, bf16[2,128,256]{2,1,0:T(8,128)(2,1)S(1)}, u32[]{:S(2)}, u32[]{:S(2)}) collective-permute-start(bf16[2,128,256]{2,1,0:T(8,128)(2,1)S(1)} %get-tuple-element.49.refs_8_), channel_id=1, source_target_pairs={{0,1},{1,0},{2,3},{3,2},{4,5},{5,4},{6,7},{7,6},{8,9},{9,8},{10,11... | collective-permute-start | bytes 393224 | tf_op jit(solution)/shard_map/ppermute | solution.py:342
  110.7 4.5 %collective-permute-start.14 = (bf16[2,128,256]{2,1,0:T(8,128)(2,1)S(1)}, bf16[2,128,256]{2,1,0:T(8,128)(2,1)S(1)}, u32[]{:S(2)}, u32[]{:S(2)}) collective-permute-start(bf16[2,128,256]{2,1,0:T(8,128)(2,1)S(1)} %get-tuple-element.45), channel_id=1, source_target_pairs={{0,2},{1,3},{2,0},{3,1},{4,6},{5,7},{6,4},{7,5},{8,10},{9,11},{10,... | collective-permute-start | bytes 393224 | tf_op jit(solution)/shard_map/ppermute | solution.py:507
  111.8 4.9 %collective-permute-start.16 = (bf16[2,128,256]{2,1,0:T(8,128)(2,1)S(1)}, bf16[2,128,256]{2,1,0:T(8,128)(2,1)S(1)}, u32[]{:S(2)}, u32[]{:S(2)}) collective-permute-start(bf16[2,128,256]{2,1,0:T(8,128)(2,1)S(1)} %get-tuple-element.46), channel_id=1, source_target_pairs={{0,4},{1,5},{2,6},{3,7},{4,0},{5,1},{6,2},{7,3},{8,12},{9,13},{10,... | collective-permute-start | bytes 393224 | tf_op jit(solution)/shard_map/ppermute | solution.py:507
  113.0 6.2 %collective-permute-start.18 = (bf16[2,128,256]{2,1,0:T(8,128)(2,1)S(1)}, bf16[2,128,256]{2,1,0:T(8,128)(2,1)S(1)}, u32[]{:S(2)}, u32[]{:S(2)}) collective-permute-start(bf16[2,128,256]{2,1,0:T(8,128)(2,1)S(1)} %get-tuple-element.47), channel_id=1, source_target_pairs={{0,6},{1,7},{2,4},{3,5},{4,2},{5,3},{6,0},{7,1},{8,14},{9,15},{10,... | collective-permute-start | bytes 393224 | tf_op jit(solution)/shard_map/ppermute | solution.py:507
  113.4 7.5 %collective-permute-start.13 = (bf16[2,128,256]{2,1,0:T(8,128)(2,1)S(1)}, bf16[2,128,256]{2,1,0:T(8,128)(2,1)S(1)}, u32[]{:S(2)}, u32[]{:S(2)}) collective-permute-start(bf16[2,128,256]{2,1,0:T(8,128)(2,1)S(1)} %get-tuple-element.44.refs_0_), channel_id=1, source_target_pairs={{0,1},{1,0},{2,3},{3,2},{4,5},{5,4},{6,7},{7,6},{8,9},{9,8},{10,11... | collective-permute-start | bytes 393224 | tf_op jit(solution)/shard_map/ppermute | solution.py:342
  115.2 5.8 %collective-permute-start.23 = (bf16[2,128,256]{2,1,0:T(8,128)(2,1)S(1)}, bf16[2,128,256]{2,1,0:T(8,128)(2,1)S(1)}, u32[]{:S(2)}, u32[]{:S(2)}) collective-permute-start(bf16[2,128,256]{2,1,0:T(8,128)(2,1)S(1)} %collective-permute-done.22.refs_10_), channel_id=1, source_target_pairs={{0,1},{1,0},{2,3},{3,2},{4,5},{5,4},{6,7},{7,6},{8,9},{9,8},{10,11... | collective-permute-start | bytes 393224 | tf_op jit(solution)/shard_map/ppermute | solution.py:342
  115.2 6.2 %collective-permute-start.25 = (bf16[2,128,256]{2,1,0:T(8,128)(2,1)S(1)}, bf16[2,128,256]{2,1,0:T(8,128)(2,1)S(1)}, u32[]{:S(2)}, u32[]{:S(2)}) collective-permute-start(bf16[2,128,256]{2,1,0:T(8,128)(2,1)S(1)} %collective-permute-done.24.refs_12_), channel_id=1, source_target_pairs={{0,1},{1,0},{2,3},{3,2},{4,5},{5,4},{6,7},{7,6},{8,9},{9,8},{10,11... | collective-permute-start | bytes 393224 | tf_op jit(solution)/shard_map/ppermute | solution.py:342
  116.7 4.7 %collective-permute-start.27 = (bf16[2,128,256]{2,1,0:T(8,128)(2,1)S(1)}, bf16[2,128,256]{2,1,0:T(8,128)(2,1)S(1)}, u32[]{:S(2)}, u32[]{:S(2)}) collective-permute-start(bf16[2,128,256]{2,1,0:T(8,128)(2,1)S(1)} %collective-permute-done.26.refs_14_), channel_id=1, source_target_pairs={{0,1},{1,0},{2,3},{3,2},{4,5},{5,4},{6,7},{7,6},{8,9},{9,8},{10,11... | collective-permute-start | bytes 393224 | tf_op jit(solution)/shard_map/ppermute | solution.py:342
  119.3 2.6 %collective-permute-start.15 = (bf16[2,128,256]{2,1,0:T(8,128)(2,1)S(1)}, bf16[2,128,256]{2,1,0:T(8,128)(2,1)S(1)}, u32[]{:S(2)}, u32[]{:S(2)}) collective-permute-start(bf16[2,128,256]{2,1,0:T(8,128)(2,1)S(1)} %collective-permute-done.14.refs_2_), channel_id=1, source_target_pairs={{0,1},{1,0},{2,3},{3,2},{4,5},{5,4},{6,7},{7,6},{8,9},{9,8},{10,11... | collective-permute-start | bytes 393224 | tf_op jit(solution)/shard_map/ppermute | solution.py:342
  120.9 1.3 %collective-permute-start.17 = (bf16[2,128,256]{2,1,0:T(8,128)(2,1)S(1)}, bf16[2,128,256]{2,1,0:T(8,128)(2,1)S(1)}, u32[]{:S(2)}, u32[]{:S(2)}) collective-permute-start(bf16[2,128,256]{2,1,0:T(8,128)(2,1)S(1)} %collective-permute-done.16.refs_4_), channel_id=1, source_target_pairs={{0,1},{1,0},{2,3},{3,2},{4,5},{5,4},{6,7},{7,6},{8,9},{9,8},{10,11... | collective-permute-start | bytes 393224 | tf_op jit(solution)/shard_map/ppermute | solution.py:342
  120.9 1.5 %collective-permute-start.19 = (bf16[2,128,256]{2,1,0:T(8,128)(2,1)S(1)}, bf16[2,128,256]{2,1,0:T(8,128)(2,1)S(1)}, u32[]{:S(2)}, u32[]{:S(2)}) collective-permute-start(bf16[2,128,256]{2,1,0:T(8,128)(2,1)S(1)} %collective-permute-done.18.refs_6_), channel_id=1, source_target_pairs={{0,1},{1,0},{2,3},{3,2},{4,5},{5,4},{6,7},{7,6},{8,9},{9,8},{10,11... | collective-permute-start | bytes 393224 | tf_op jit(solution)/shard_map/ppermute | solution.py:342
